TPU v7x, 32 devices: a whole 2x2x4 slice. The times are simulated.
32 devices in a mesh: groups: 2 (over x), ao: 16 (over z, y, core).
Axes of the slice: x: 2, y: 2, z: 4, core: 2. Of those that a mesh axis runs over, the one named last changes fastest.
Arguments:
- b_half: bfloat16 [6144, 8192], P('groups', 'ao'), parts along dimension 0
- significant: int32 [32, 3], P('groups'), parts along dimension 0, may hold values 0 or 1
- live_rows: int32 [32], P('groups'), parts along dimension 0, may hold values from 512 to 3072, as said below
Outputs:
- k_diagonal: float32 [32, 512, 512], P(('groups', 'ao')), parts along dimension 0
- k_upper: float32 [32, 3, 512, 512], P(('groups', 'ao')), parts along dimension 0
- k_lower: float32 [32, 3, 512, 512], P(('groups', 'ao')), parts along dimension 0
There are 2 independent parts, one for each index of `groups`. A program takes and returns all parts, laid end to end along the dimension named above; each array names one. Nothing has to cross between parts.
Inputs may be any that keep to these rules, and one draw needn't show every extreme that they name: `live_rows`: a multiple of 512; every draw has a block with all 3072 rows and one with 512.
All inputs are finite; a program needn't handle non-finite values.
Results may differ from a plain program's by a relative error of at most 0.0003.
Values may be sent and summed in bfloat16 or wider, within the bound.
No kernel may reach another device: no remote copies, remote signals or barrier semaphores. Data moves between devices by JAX's collectives and lax.ppermute only.
A program may use at most 128 MiB of HBM per device.

v0:
```python
import jax
import jax.numpy as jnp
from jax import lax
from jax.sharding import PartitionSpec as P

ROWBLK = 512
HOPS = 3


def passed_along(block, axis, distance):
    devices = range(lax.axis_size(axis))
    route = [(i - distance, i) for i in devices if i - distance in devices]
    return lax.ppermute(block, axis, route)


def pair_tile(first_block, second_block, row_limit):

    def add_block(turn, running):
        first_rows = lax.dynamic_slice_in_dim(first_block, turn * ROWBLK, ROWBLK, 0)
        second_rows = lax.dynamic_slice_in_dim(second_block, turn * ROWBLK, ROWBLK, 0)
        return running + lax.dot_general(
            first_rows, second_rows, (((0,), (0,)), ((), ())), preferred_element_type=jnp.float32
        )

    zero_tile = jnp.zeros((first_block.shape[1], second_block.shape[1]), jnp.float32)
    return lax.fori_loop(0, row_limit // ROWBLK, add_block, zero_tile)


def fetch_blocks(block, direction):
    return [passed_along(block, "ao", direction * (offset + 1)) for offset in range(HOPS)]


def per_device(b_half, significant, live_rows):
    position = lax.axis_index("ao")
    block_total = lax.axis_size("ao")
    own_count = live_rows[position]
    diagonal = pair_tile(b_half, b_half, own_count)
    uppers = fetch_blocks(b_half, -1)
    upper_tiles = []
    for offset in range(HOPS):
        partner_id = jnp.minimum(position + offset + 1, block_total - 1)
        row_limit = jnp.minimum(own_count, live_rows[partner_id]) * significant[position, offset]
        upper_tiles.append(pair_tile(b_half, uppers[offset], row_limit))
    lowers = fetch_blocks(b_half, 1)
    lower_tiles = []
    for offset in range(HOPS):
        partner_id = jnp.maximum(position - offset - 1, 0)
        row_limit = jnp.minimum(own_count, live_rows[partner_id]) * significant[partner_id, offset]
        lower_tiles.append(pair_tile(b_half, lowers[offset], row_limit))
    return (diagonal[None], jnp.stack(upper_tiles)[None], jnp.stack(lower_tiles)[None])


def solution(mesh):
    in_specs = (P("groups", "ao"), P("groups", None), P("groups"))
    out_specs = (
        P(("groups", "ao"), None, None),
        P(("groups", "ao"), None, None, None),
        P(("groups", "ao"), None, None, None),
    )
    return jax.shard_map(
        per_device, mesh=mesh, in_specs=in_specs, out_specs=out_specs, check_vma=False
    )
```

profile of v0, /device:TPU:5, one launch (start us, length us, event | category | flops | bytes accessed | tf_op | source)
XLA Modules:
  0.0 317.5 jit_solution(9141098468343796945)
XLA Ops:
  0.6 3.7 %collective-permute-start.3 = (bf16[3072,512]{1,0:T(8,128)(2,1)}, bf16[3072,512]{1,0:T(8,128)(2,1)}, u32[]{:S(2)}, u32[]{:S(2)}) collective-permute-start(bf16[3072,512]{1,0:T(8,128)(2,1)} %param.17), channel_id=1, source_target_pairs={{0,1},{1,2},{2,3},{3,4},{4,5},{5,6},{6,7},{7,8},{8,9},{9,10},{10,1... | collective-permute-start | bytes 9437192 | tf_op jit(solution)/shard_map/ppermute | solution.py:13
  4.3 3.2 collective-permute-start.4
  7.5 2.3 collective-permute-start.5
  9.8 4.8 %collective-permute-start = (bf16[3072,512]{1,0:T(8,128)(2,1)}, bf16[3072,512]{1,0:T(8,128)(2,1)}, u32[]{:S(2)}, u32[]{:S(2)}) collective-permute-start(bf16[3072,512]{1,0:T(8,128)(2,1)} %param.17), channel_id=1, source_target_pairs={{1,0},{2,1},{3,2},{4,3},{5,4},{6,5},{7,6},{8,7},{9,8},{10,9},{11,1... | collective-permute-start | bytes 9437192 | tf_op jit(solution)/shard_map/ppermute | solution.py:13
  14.6 2.1 collective-permute-start.1
  16.8 1.6 fusion.20
  19.7 1.6 constant_dynamic-slice_fusion.4
  34.7 0.1 broadcast.10.clone
  34.8 10.4 %while.70 = (s32[]{:T(128)}, f32[512,512]{1,0:T(8,128)S(1)}, s32[]{:T(128)}, bf16[3072,512]{1,0:T(8,128)(2,1)}, s32[]{:T(128)}, /*index=5*/s32[]{:T(128)}, s32[]{:T(128)}, s32[]{:T(128)}) while((s32[]{:T(128)}, f32[512,512]{1,0:T(8,128)S(1)}, s32[]{:T(128)}, bf16[3072,512]{1,0:T(8,128)(2,1)}, s32[]{:T(128)}, /*index=5*/s32[]{:T(128)}, ...), condition=%wide.region_1.2_spmd, body=%wide.region_0.1_spmd.sunk | while | flops 268697600 | bytes 2621575 | solution.py:26
  34.8 1.7 convolution_add_fusion.14
  36.5 1.7 convolution_add_fusion.14
  38.3 1.7 convolution_add_fusion.14
  40.0 1.7 convolution_add_fusion.14
  41.7 1.7 convolution_add_fusion.14
  43.5 1.7 convolution_add_fusion.14
  45.2 0.0 copy-start.2
  45.2 24.8 %collective-permute-done.3 = bf16[3072,512]{1,0:T(8,128)(2,1)} collective-permute-done((bf16[3072,512]{1,0:T(8,128)(2,1)}, bf16[3072,512]{1,0:T(8,128)(2,1)}, u32[]{:S(2)}, u32[]{:S(2)}) %collective-permute-start.3) | collective-permute-done | bytes 3145760 | tf_op jit(solution)/shard_map/ppermute | solution.py:13
  70.0 0.0 copy-done.2
  70.0 1.9 collective-permute-start.2
  72.0 0.1 broadcast.10.clone.6
  72.1 8.5 %while.74 = (s32[]{:T(128)}, f32[512,512]{1,0:T(8,128)S(1)}, s32[]{:T(128)}, bf16[3072,512]{1,0:T(8,128)(2,1)}, bf16[3072,512]{1,0:T(8,128)(2,1)}, /*index=5*/s32[]{:T(128)}, s32[]{:T(128)}, s32[]{:T(128)}, s32[]{:T(128)}) while((s32[]{:T(128)}, f32[512,512]{1,0:T(8,128)S(1)}, s32[]{:T(128)}, bf16[3072,512]{1,0:T(8,128)(2,1)}, ...), condition=%wide.region_9.10_spmd, body=%wide.region_8.9_spmd.sunk | while | flops 268697600 | bytes 3146891 | solution.py:26
  72.1 1.7 convolution_add_fusion.18
  73.8 1.7 convolution_add_fusion.18
  75.5 1.7 convolution_add_fusion.18
  77.2 1.7 convolution_add_fusion.18
  78.9 1.7 convolution_add_fusion.18
  80.6 192.3 %collective-permute-done.4 = bf16[3072,512]{1,0:T(8,128)(2,1)} collective-permute-done((bf16[3072,512]{1,0:T(8,128)(2,1)}, bf16[3072,512]{1,0:T(8,128)(2,1)}, u32[]{:S(2)}, u32[]{:S(2)}) %collective-permute-start.4) | collective-permute-done | bytes 3145760 | tf_op jit(solution)/shard_map/ppermute | solution.py:13
  272.9 0.1 broadcast.10.clone.5
  273.0 5.1 %while.75 = (s32[]{:T(128)}, f32[512,512]{1,0:T(8,128)S(1)}, s32[]{:T(128)}, bf16[3072,512]{1,0:T(8,128)(2,1)}, bf16[3072,512]{1,0:T(8,128)(2,1)}, /*index=5*/s32[]{:T(128)}, s32[]{:T(128)}, s32[]{:T(128)}, s32[]{:T(128)}) while((s32[]{:T(128)}, f32[512,512]{1,0:T(8,128)S(1)}, s32[]{:T(128)}, bf16[3072,512]{1,0:T(8,128)(2,1)}, ...), condition=%wide.region_11.12_spmd, body=%wide.region_10.11_spmd.sunk | while | flops 268697600 | bytes 3146891 | solution.py:26
  273.0 1.7 convolution_add_fusion.19
  274.7 1.7 convolution_add_fusion.19
  276.5 1.7 convolution_add_fusion.19
  278.1 0.0 collective-permute-done.5
  278.2 0.1 broadcast.10.clone.4
  278.3 10.2 %while.76 = (s32[]{:T(128)}, f32[512,512]{1,0:T(8,128)S(1)}, s32[]{:T(128)}, bf16[3072,512]{1,0:T(8,128)(2,1)}, bf16[3072,512]{1,0:T(8,128)(2,1)}, /*index=5*/s32[]{:T(128)}, s32[]{:T(128)}, s32[]{:T(128)}, s32[]{:T(128)}) while((s32[]{:T(128)}, f32[512,512]{1,0:T(8,128)S(1)}, s32[]{:T(128)}, bf16[3072,512]{1,0:T(8,128)(2,1)}, ...), condition=%wide.region_13.14_spmd, body=%wide.region_12.13_spmd.sunk | while | flops 268697600 | bytes 3146891 | solution.py:26
  278.3 1.7 convolution_add_fusion.20
  280.0 1.7 convolution_add_fusion.20
  281.7 1.7 convolution_add_fusion.20
  283.4 1.7 convolution_add_fusion.20
  285.1 1.7 convolution_add_fusion.20
  286.8 1.7 convolution_add_fusion.20
  288.5 0.0 copy-start
  288.5 0.0 collective-permute-done
  288.5 1.2 broadcast.10.clone.3
  289.8 0.1 copy-done
  289.9 9.0 %while.71 = (s32[]{:T(128)}, f32[512,512]{1,0:T(8,128)}, s32[]{:T(128)}, bf16[3072,512]{1,0:T(8,128)(2,1)}, bf16[3072,512]{1,0:T(8,128)(2,1)}, /*index=5*/s32[]{:T(128)}, s32[]{:T(128)}, s32[]{:T(128)}, s32[]{:T(128)}) while((s32[]{:T(128)}, f32[512,512]{1,0:T(8,128)}, s32[]{:T(128)}, bf16[3072,512]{1,0:T(8,128)(2,1)}, ...), condition=%wide.region_3.4_spmd, body=%wide.region_2.3_spmd.sunk | while | flops 268697600 | bytes 3146891 | solution.py:26
  289.9 3.0 convolution_add_fusion.15
  292.8 3.0 convolution_add_fusion.15
  295.8 3.0 convolution_add_fusion.15
  298.8 0.0 collective-permute-done.1
  298.8 0.1 broadcast.10.clone.2
  298.9 1.7 while.72
  299.0 1.7 convolution_add_fusion.16
  300.7 1.0 copy-done.1
  301.6 0.0 collective-permute-done.2
  301.7 0.1 broadcast.10.clone.1
  301.8 10.2 %while.73 = (s32[]{:T(128)}, f32[512,512]{1,0:T(8,128)S(1)}, s32[]{:T(128)}, bf16[3072,512]{1,0:T(8,128)(2,1)}, bf16[3072,512]{1,0:T(8,128)(2,1)}, /*index=5*/s32[]{:T(128)}, s32[]{:T(128)}, s32[]{:T(128)}, s32[]{:T(128)}) while((s32[]{:T(128)}, f32[512,512]{1,0:T(8,128)S(1)}, s32[]{:T(128)}, bf16[3072,512]{1,0:T(8,128)(2,1)}, ...), condition=%wide.region_7.8_spmd, body=%wide.region_6.7_spmd.sunk | while | flops 268697600 | bytes 3146891 | solution.py:26
  301.8 1.7 convolution_add_fusion.17
  303.5 1.7 convolution_add_fusion.17
  305.2 1.7 convolution_add_fusion.17
  306.9 1.7 convolution_add_fusion.17
  308.6 1.7 convolution_add_fusion.17
  310.3 1.7 convolution_add_fusion.17
  312.0 5.5 %maximum_bitcast_fusion = (f32[1,3,512,512]{3,2,1,0:T(8,128)}, f32[1,3,512,512]{3,2,1,0:T(8,128)}) fusion(f32[1,512,512]{2,1,0:T(8,128)S(1)} %bitcast.24, f32[1,512,512]{2,1,0:T(8,128)} %bitcast.29, f32[1,512,512]{2,1,0:T(8,128)} %bitcast.28, f32[1,512,512]{2,1,0:T(8,128)} %bitcast.27, f32[1,512,512]{2,1,0:T(8,128)S(1)} %bitcast.26, ...), kind=kLoop, calls=%fused_computation.27 | loop fusion | flops 3145728 | bytes 12582912 | tf_op jit(solution)/shard_map/broadcast_in_dim | solution.py:50
  (1 shorter events, 0.0 us)
Async XLA Ops:
  0.6 69.4 %collective-permute-start.3 = (bf16[3072,512]{1,0:T(8,128)(2,1)}, bf16[3072,512]{1,0:T(8,128)(2,1)}, u32[]{:S(2)}, u32[]{:S(2)}) collective-permute-start(bf16[3072,512]{1,0:T(8,128)(2,1)} %param.17), channel_id=1, source_target_pairs={{0,1},{1,2},{2,3},{3,4},{4,5},{5,6},{6,7},{7,8},{8,9},{9,10},{10,1... | collective-permute-start | bytes 9437192 | tf_op jit(solution)/shard_map/ppermute | solution.py:13
  4.3 268.5 %collective-permute-start.4 = (bf16[3072,512]{1,0:T(8,128)(2,1)}, bf16[3072,512]{1,0:T(8,128)(2,1)}, u32[]{:S(2)}, u32[]{:S(2)}) collective-permute-start(bf16[3072,512]{1,0:T(8,128)(2,1)} %param.17), channel_id=1, source_target_pairs={{0,2},{1,3},{2,4},{3,5},{4,6},{5,7},{6,8},{7,9},{8,10},{9,11},{10,... | collective-permute-start | bytes 9437192 | tf_op jit(solution)/shard_map/ppermute | solution.py:13
  7.5 270.6 %collective-permute-start.5 = (bf16[3072,512]{1,0:T(8,128)(2,1)}, bf16[3072,512]{1,0:T(8,128)(2,1)}, u32[]{:S(2)}, u32[]{:S(2)}) collective-permute-start(bf16[3072,512]{1,0:T(8,128)(2,1)} %param.17), channel_id=1, source_target_pairs={{0,3},{1,4},{2,5},{3,6},{4,7},{5,8},{6,9},{7,10},{8,11},{9,12},{10... | collective-permute-start | bytes 9437192 | tf_op jit(solution)/shard_map/ppermute | solution.py:13
  9.8 278.8 %collective-permute-start = (bf16[3072,512]{1,0:T(8,128)(2,1)}, bf16[3072,512]{1,0:T(8,128)(2,1)}, u32[]{:S(2)}, u32[]{:S(2)}) collective-permute-start(bf16[3072,512]{1,0:T(8,128)(2,1)} %param.17), channel_id=1, source_target_pairs={{1,0},{2,1},{3,2},{4,3},{5,4},{6,5},{7,6},{8,7},{9,8},{10,9},{11,1... | collective-permute-start | bytes 9437192 | tf_op jit(solution)/shard_map/ppermute | solution.py:13
  14.6 284.2 %collective-permute-start.1 = (bf16[3072,512]{1,0:T(8,128)(2,1)}, bf16[3072,512]{1,0:T(8,128)(2,1)}, u32[]{:S(2)}, u32[]{:S(2)}) collective-permute-start(bf16[3072,512]{1,0:T(8,128)(2,1)} %param.17), channel_id=1, source_target_pairs={{2,0},{3,1},{4,2},{5,3},{6,4},{7,5},{8,6},{9,7},{10,8},{11,9},{12,... | collective-permute-start | bytes 9437192 | tf_op jit(solution)/shard_map/ppermute | solution.py:13
  45.2 24.9 %copy-start.2 = (f32[512,512]{1,0:T(8,128)}, f32[512,512]{1,0:T(8,128)S(1)}, u32[]{:S(2)}) copy-start(f32[512,512]{1,0:T(8,128)S(1)} %get-tuple-element.194) | copy-start | bytes 3145732
  70.0 231.6 %collective-permute-start.2 = (bf16[3072,512]{1,0:T(8,128)(2,1)}, bf16[3072,512]{1,0:T(8,128)(2,1)}, u32[]{:S(2)}, u32[]{:S(2)}) collective-permute-start(bf16[3072,512]{1,0:T(8,128)(2,1)} %get-tuple-element.693), channel_id=1, source_target_pairs={{3,0},{4,1},{5,2},{6,3},{7,4},{8,5},{9,6},{10,7},{11,8},{12,9},{13... | collective-permute-start | bytes 9437192 | tf_op jit(solution)/shard_map/ppermute | solution.py:13
  288.5 1.3 copy-start
  300.7 1.0 copy-start.1
where the time goes:
time: 323 us; the launch traced here: 318 us
  waiting for transfers between devices  217 us (67%)
  matrix products  54.3 us (17%)
  starting transfers between devices  18 us (6%)
  between operations  15.5 us (5%)
  local copies, waits for them, and re-layouts  6.19 us (2%)
  other arithmetic  5.5 us (2%)
    ppermute x6, waiting for transfers between devices, passed_along(): return lax.ppermute(block, axis, route)  217 us
    dot_general x30, matrix products, add_block(): lax.dot_general(first_rows, second_rows, (((0,), (0,)), ((), ())), prefer...  54.3 us
    ppermute x6, starting transfers between devices, passed_along(): return lax.ppermute(block, axis, route)  18 us
  transfers between devices with their start and end apart: 6, of which 2 were waited for; matrix products, arithmetic and copies ran while one was open for 16% of the time, Pallas kernels for 0%

commit v1 on v0

v1 whole, which is shorter than its diff:
```python
import functools

import jax
import jax.numpy as jnp
from jax import lax
from jax.experimental import pallas as pl
from jax.experimental.pallas import tpu as pltpu
from jax.sharding import PartitionSpec as P

ROWBLK = 512
HOPS = 3
LEVEL = 4
SPLIT = 3
DIRECT = 1


def level_route(block_total, moves):
    levels = block_total // LEVEL
    return [
        (LEVEL * z + place, LEVEL * (z + step) + new)
        for z in range(levels)
        for place, step, new in moves
        if 0 <= z + step < levels
    ]


def tiles_kernel(position_ref, live_ref, sig_ref, *refs, pieces, block_total):
    own_ref = refs[0]
    partner_refs = refs[1 : 1 + 6 * pieces]
    diag_ref, up_ref, low_ref = refs[1 + 6 * pieces : 4 + 6 * pieces]
    own, own_t, held, tile, own_sem, in_sem, out_sem = refs[4 + 6 * pieces :]
    steps = own.shape[0]
    per_piece = steps // pieces
    position = position_ref[0]
    place = lax.rem(position, LEVEL)
    own_count = live_ref[position] // ROWBLK

    upward = place >= 2
    edge = (place == 0) | (place == 3)
    d_core = jnp.where(lax.rem(place, 2) == 0, 1, -1)
    d_y = jnp.where(place < 2, 2, -2)
    d_both = (LEVEL - 1) - 2 * place
    d_far = jnp.where(lax.rem(place, 2) == 0, -3, 3)
    d_relay = jnp.where(upward, 2, -2)
    d_last = jnp.where(edge, jnp.where(upward, 1, -1), jnp.where(upward, 3, -3))
    dists = [d_core, d_y, d_both, d_far, d_relay, d_last]

    def count_of(dist):
        other = position + dist
        inside = (other >= 0) & (other < block_total)
        safe = jnp.clip(other, 0, block_total - 1)
        first = jnp.minimum(position, safe)
        hop = jnp.clip(jnp.abs(dist) - 1, 0, HOPS - 1)
        rows = jnp.minimum(own_count, live_ref[safe] // ROWBLK)
        return jnp.where(inside, rows * sig_ref[first, hop], 0)

    counts = [count_of(d) for d in dists]

    def own_copy(r):
        return pltpu.make_async_copy(own_ref.at[pl.ds(r * ROWBLK, ROWBLK)], own.at[r], own_sem.at[r])

    def held_copy(p, r):
        source = partner_refs[p * pieces + r // per_piece]
        return pltpu.make_async_copy(
            source.at[pl.ds((r % per_piece) * ROWBLK, ROWBLK)], held.at[p % 2, r], in_sem.at[p % 2, r]
        )

    def start_partner(p):
        for r in range(steps):
            @pl.when(r < counts[p])
            def _():
                held_copy(p, r).start()

    def wait_partner(p):
        for r in range(steps):
            @pl.when(r < counts[p])
            def _():
                held_copy(p, r).wait()

    for r in range(steps):
        @pl.when(r < own_count)
        def _():
            own_copy(r).start()
    start_partner(0)
    for r in range(steps):
        @pl.when(r < own_count)
        def _():
            own_copy(r).wait()

    def turn(r, _):
        own_t[r] = own[r].T
        return 0

    lax.fori_loop(0, own_count, turn, 0)

    def make_tile(slot, count, load):
        tile[slot] = jnp.zeros(tile.shape[1:], jnp.float32)

        def add(r, _):
            tile[slot] += jnp.dot(own_t[r], load(r), preferred_element_type=jnp.float32)
            return 0

        lax.fori_loop(0, count, add, 0)

    make_tile(0, own_count, lambda r: own[r])
    pltpu.make_async_copy(tile.at[0], diag_ref.at[0], out_sem.at[0]).start()

    def wait_tile(slot):
        pltpu.make_async_copy(tile.at[slot], diag_ref.at[0], out_sem.at[slot]).wait()

    for p in range(6):
        slot = (p + 1) % 2
        if p < 5:
            start_partner(p + 1)
        wait_partner(p)
        if p >= 1:
            wait_tile(slot)
        make_tile(slot, counts[p], lambda r: held[p % 2, r])
        hop = jnp.clip(jnp.abs(dists[p]) - 1, 0, HOPS - 1)

        @pl.when(dists[p] > 0)
        def _():
            pltpu.make_async_copy(tile.at[slot], up_ref.at[0, hop], out_sem.at[slot]).start()

        @pl.when(dists[p] < 0)
        def _():
            pltpu.make_async_copy(tile.at[slot], low_ref.at[0, hop], out_sem.at[slot]).start()

    wait_tile(1)
    wait_tile(0)


def make_tiles(position, live_rows, significant, own, partners, block_total):
    rows, cols = own.shape
    steps = rows // ROWBLK
    pieces = len(partners[0])
    flat = [piece for partner in partners for piece in partner]
    smem = pl.BlockSpec(memory_space=pltpu.SMEM)
    hbm = pl.BlockSpec(memory_space=pl.ANY)
    return pl.pallas_call(
        functools.partial(tiles_kernel, pieces=pieces, block_total=block_total),
        out_shape=(
            jax.ShapeDtypeStruct((1, cols, cols), jnp.float32),
            jax.ShapeDtypeStruct((1, HOPS, cols, cols), jnp.float32),
            jax.ShapeDtypeStruct((1, HOPS, cols, cols), jnp.float32),
        ),
        in_specs=[smem] * 3 + [hbm] * (1 + len(flat)),
        out_specs=(hbm,) * 3,
        scratch_shapes=[
            pltpu.VMEM((steps, ROWBLK, cols), own.dtype),
            pltpu.VMEM((steps, cols, ROWBLK), own.dtype),
            pltpu.VMEM((2, steps, ROWBLK, cols), own.dtype),
            pltpu.VMEM((2, cols, cols), jnp.float32),
            pltpu.SemaphoreType.DMA((steps,)),
            pltpu.SemaphoreType.DMA((2, steps)),
            pltpu.SemaphoreType.DMA((2,)),
        ],
        compiler_params=pltpu.CompilerParams(vmem_limit_bytes=40 * 2**20),
    )(position, live_rows, significant, own, *flat)


def per_device(b_half, significant, live_rows):
    block_total = lax.axis_size("ao")
    position = lax.axis_index("ao").astype(jnp.int32)
    piece_rows = b_half.shape[0] // SPLIT
    own = [b_half[i * piece_rows : (i + 1) * piece_rows] for i in range(SPLIT)]

    def send(block, moves):
        return lax.ppermute(block, "ao", level_route(block_total, moves))

    cores = [(j, 0, j ^ 1) for j in range(LEVEL)]
    across = [(j, 0, j ^ 2) for j in range(LEVEL)]
    far = [(1, 1, 0), (0, -1, 1), (3, 1, 2), (2, -1, 3)]
    relay = [(0, 1, 0), (1, 1, 1), (2, -1, 2), (3, -1, 3)]
    relay_edges = [(0, 1, 0), (3, -1, 3)]
    far_across = [(2, 0, 0), (1, 0, 3)]
    edges_in = [(0, 0, 1), (3, 0, 2)]

    y_part, both_part, relay_part, last_part = [], [], [], []
    far_part = [send(own[i], far) for i in reversed(range(SPLIT))][::-1]
    core_part = [send(own[i], cores) for i in range(SPLIT)]
    on_inner = (position % LEVEL == 1) | (position % LEVEL == 2)
    for i in range(SPLIT):
        y_part.append(send(own[i], across))
        both_part.append(send(y_part[i], cores))
        if i < SPLIT - DIRECT:
            relay_part.append(send(y_part[i], relay))
            last_part.append(send(relay_part[i], cores))
        else:
            second = send(y_part[i], relay_edges)
            first = send(far_part[i], far_across)
            inner_last = send(second, edges_in)
            inner_relay = send(first, edges_in)
            relay_part.append(jnp.where(on_inner, inner_relay, second))
            last_part.append(jnp.where(on_inner, inner_last, first))
    return make_tiles(
        position[None],
        live_rows,
        significant,
        b_half,
        [core_part, y_part, both_part, far_part, relay_part, last_part],
        block_total,
    )


def solution(mesh):
    in_specs = (P("groups", "ao"), P("groups", None), P("groups"))
    out_specs = (
        P(("groups", "ao"), None, None),
        P(("groups", "ao"), None, None, None),
        P(("groups", "ao"), None, None, None),
    )
    return jax.shard_map(
        per_device, mesh=mesh, in_specs=in_specs, out_specs=out_specs, check_vma=False
    )
```

time: 323 us -> 143 us (0.44); the launches traced: 318 us -> 142 us
  waiting for transfers between devices: 217 us -> 89.1 us
  matrix products: 54.3 us -> 0 us
  Pallas kernels: 0 us -> 19.8 us
  between operations: 15.5 us -> 0.88 us
    ppermute x6 -> x20, waiting for transfers between devices: 217 us -> 89.1 us  [send(): return lax.ppermute(block, 'ao', level_route(block_total, moves))]
    dot_general x30 -> x0, matrix products: 54.3 us -> none  [add_block(): lax.dot_general(first_rows, second_rows, (((0,), (0,)), ((), ())), prefer...]
    pallas_call x0 -> x1, Pallas kernels: none -> 19.8 us  [make_tiles(): pl.pallas_call(functools.partial(tiles_kernel, pieces=pieces, block_total...]
    broadcast_in_dim x1 -> x0, other arithmetic: 5.5 us -> none  [per_device(): jnp.stack(upper_tiles)[None]]
    select_n x0 -> x2, other arithmetic: none -> 4.84 us  [the longest x1 2.5 us: per_device(): relay_part.append(jnp.where(on_inner, inner_relay, second))]
    unnamed x6 -> x29, local copies, waits for them, and re-layouts: 1.04 us -> 4.98 us
    ppermute x6 -> x20, starting transfers between devices: 18 us -> 20.1 us  [send(): return lax.ppermute(block, 'ao', level_route(block_total, moves))]
  transfers between devices with their start and end apart: 6 -> 20, of which waited for: 2 -> 7; matrix products, arithmetic and copies ran while one was open for 16% -> 3% of each run, Pallas kernels for 0% -> 0%
where the time goes in v1:
time: 143 us; the launch traced here: 142 us
  waiting for transfers between devices  89.1 us (62%)
  starting transfers between devices  20.1 us (14%)
  Pallas kernels  19.8 us (14%)
  local copies, waits for them, and re-layouts  7.05 us (5%)
  other arithmetic  4.84 us (3%)
    ppermute x20, waiting for transfers between devices, send(): return lax.ppermute(block, 'ao', level_route(block_total, moves))  89.1 us
    ppermute x20, starting transfers between devices, send(): return lax.ppermute(block, 'ao', level_route(block_total, moves))  20.1 us
    pallas_call x1, Pallas kernels, make_tiles(): pl.pallas_call(functools.partial(tiles_kernel, pieces=pieces, block_total...  19.8 us
    unnamed x29, local copies, waits for them, and re-layouts  4.98 us
  transfers between devices with their start and end apart: 20, of which 7 were waited for; matrix products, arithmetic and copies ran while one was open for 3% of the time, Pallas kernels for 0%

profile of v1, /device:TPU:5, one launch (start us, length us, event | category | flops | bytes accessed | tf_op | source)
XLA Modules:
  0.0 141.7 jit_solution(3240432912207910920)
XLA Ops:
  0.6 0.0 copy-start.13
  0.6 2.1 %fusion = (bf16[1024,512]{1,0:T(8,128)(2,1)S(1)}, bf16[1024,512]{1,0:T(8,128)(2,1)S(1)}, bf16[1024,512]{1,0:T(8,128)(2,1)S(1)}) fusion(bf16[3072,512]{1,0:T(8,128)(2,1)} %refs_0_.1), kind=kLoop, calls=%fused_computation.2 | loop fusion | bytes 6291456 | tf_op jit(solution)/shard_map/slice | solution.py:166
  2.7 3.8 %collective-permute-start.11 = (bf16[1024,512]{1,0:T(8,128)(2,1)S(1)}, bf16[1024,512]{1,0:T(8,128)(2,1)S(1)}, u32[]{:S(2)}, u32[]{:S(2)}) collective-permute-start(bf16[1024,512]{1,0:T(8,128)(2,1)S(1)} %get-tuple-element.3), channel_id=1, source_target_pairs={{1,4},{3,6},{5,8},{4,1},{7,10},{6,3},{9,12},{8,5},{11,14},{10,7},{... | collective-permute-start | bytes 3145736 | tf_op jit(solution)/shard_map/ppermute | solution.py:169
  6.5 0.3 collective-permute-start.5
  6.8 0.0 collective-permute-start.2
  6.8 3.6 %collective-permute-start.10 = (bf16[1024,512]{1,0:T(8,128)(2,1)S(1)}, bf16[1024,512]{1,0:T(8,128)(2,1)S(1)}, u32[]{:S(2)}, u32[]{:S(2)}) collective-permute-start(bf16[1024,512]{1,0:T(8,128)(2,1)S(1)} %get-tuple-element.4), channel_id=1, source_target_pairs={{1,4},{3,6},{5,8},{4,1},{7,10},{6,3},{9,12},{8,5},{11,14},{10,7},{... | collective-permute-start | bytes 3145736 | tf_op jit(solution)/shard_map/ppermute | solution.py:169
  10.4 1.3 collective-permute-start.4
  11.7 7.6 %collective-permute-done.11.refs_12_ = bf16[1024,512]{1,0:T(8,128)(2,1)S(1)} collective-permute-done((bf16[1024,512]{1,0:T(8,128)(2,1)S(1)}, bf16[1024,512]{1,0:T(8,128)(2,1)S(1)}, u32[]{:S(2)}, u32[]{:S(2)}) %collective-permute-start.11) | collective-permute-done | bytes 1048608 | tf_op jit(solution)/shard_map/ppermute | solution.py:169
  19.2 0.0 collective-permute-start.1
  19.2 12.6 %collective-permute-done.5.refs_6_ = bf16[1024,512]{1,0:T(8,128)(2,1)S(1)} collective-permute-done((bf16[1024,512]{1,0:T(8,128)(2,1)S(1)}, bf16[1024,512]{1,0:T(8,128)(2,1)S(1)}, u32[]{:S(2)}, u32[]{:S(2)}) %collective-permute-start.5) | collective-permute-done | bytes 1048608 | tf_op jit(solution)/shard_map/ppermute | solution.py:169
  31.9 1.9 %collective-permute-start.9 = (bf16[1024,512]{1,0:T(8,128)(2,1)S(1)}, bf16[1024,512]{1,0:T(8,128)(2,1)S(1)}, u32[]{:S(2)}, u32[]{:S(2)}) collective-permute-start(bf16[1024,512]{1,0:T(8,128)(2,1)S(1)} %get-tuple-element.5), channel_id=1, source_target_pairs={{1,4},{3,6},{5,8},{4,1},{7,10},{6,3},{9,12},{8,5},{11,14},{10,7},{... | collective-permute-start | bytes 3145736 | tf_op jit(solution)/shard_map/ppermute | solution.py:169
  33.8 0.0 collective-permute-done.2.refs_3_
  33.8 0.3 collective-permute-start.3
  34.1 0.0 collective-permute-done.10.refs_11_
  34.1 1.1 copy-done
  35.2 1.3 collective-permute-start.14
  36.5 17.9 %collective-permute-done.4.refs_5_ = bf16[1024,512]{1,0:T(8,128)(2,1)} collective-permute-done((bf16[1024,512]{1,0:T(8,128)(2,1)S(1)}, bf16[1024,512]{1,0:T(8,128)(2,1)}, u32[]{:S(2)}, u32[]{:S(2)}) %collective-permute-start.4) | collective-permute-done | bytes 1048608 | tf_op jit(solution)/shard_map/ppermute | solution.py:169
  54.4 1.3 collective-permute-start.16
  55.7 0.0 collective-permute-done.1.refs_2_
  55.7 0.0 copy-start.2
  55.7 1.0 copy-done.2
  56.6 0.0 collective-permute-start
  56.6 0.0 collective-permute-done.9.refs_10_
  56.6 1.0 copy-done.4
  57.6 1.3 collective-permute-start.13
  58.9 16.0 %collective-permute-done.3.refs_4_ = bf16[1024,512]{1,0:T(8,128)(2,1)} collective-permute-done((bf16[1024,512]{1,0:T(8,128)(2,1)S(1)}, bf16[1024,512]{1,0:T(8,128)(2,1)}, u32[]{:S(2)}, u32[]{:S(2)}) %collective-permute-start.3) | collective-permute-done | bytes 1048608 | tf_op jit(solution)/shard_map/ppermute | solution.py:169
  74.9 1.3 collective-permute-start.12
  76.2 9.9 %collective-permute-done.14 = bf16[1024,512]{1,0:T(8,128)(2,1)S(1)} collective-permute-done((bf16[1024,512]{1,0:T(8,128)(2,1)S(1)}, bf16[1024,512]{1,0:T(8,128)(2,1)S(1)}, u32[]{:S(2)}, u32[]{:S(2)}) %collective-permute-start.14) | collective-permute-done | bytes 1048608 | tf_op jit(solution)/shard_map/ppermute | solution.py:169
  86.1 1.3 collective-permute-start.15
  87.5 0.0 collective-permute-done.16
  87.5 0.0 copy-start.10
  87.5 1.4 collective-permute-start.19
  88.8 0.0 collective-permute-done.refs_1_
  88.9 0.0 copy-done.9
  88.9 0.0 copy-start.6
  88.9 1.0 copy-done.6
  89.8 0.0 collective-permute-start.8
  89.8 9.3 %collective-permute-done.13.refs_14_ = bf16[1024,512]{1,0:T(8,128)(2,1)} collective-permute-done((bf16[1024,512]{1,0:T(8,128)(2,1)}, bf16[1024,512]{1,0:T(8,128)(2,1)}, u32[]{:S(2)}, u32[]{:S(2)}) %collective-permute-start.13) | collective-permute-done | bytes 1048608 | tf_op jit(solution)/shard_map/ppermute | solution.py:169
  99.2 0.0 collective-permute-start.7
  99.2 15.8 %collective-permute-done.12.refs_13_ = bf16[1024,512]{1,0:T(8,128)(2,1)} collective-permute-done((bf16[1024,512]{1,0:T(8,128)(2,1)}, bf16[1024,512]{1,0:T(8,128)(2,1)}, u32[]{:S(2)}, u32[]{:S(2)}) %collective-permute-start.12) | collective-permute-done | bytes 1048608 | tf_op jit(solution)/shard_map/ppermute | solution.py:169
  114.9 0.0 collective-permute-start.6
  114.9 0.0 collective-permute-done.15
  114.9 0.0 copy-done.10
  115.0 0.0 copy-start.11
  115.0 0.6 collective-permute-start.18
  115.5 0.0 collective-permute-done.19
  115.5 0.4 copy-done.11
  115.9 0.5 collective-permute-start.17
  116.4 0.5 copy-done.12
  116.9 0.0 copy-done.13
  116.9 0.1 copy.6.sig_ref
  117.0 0.0 copy-start.8
  117.0 2.5 %broadcast_select_fusion.1.refs_15_ = bf16[1024,512]{1,0:T(8,128)(2,1)} fusion(bf16[1024,512]{1,0:T(8,128)(2,1)} %copy-done.11, bf16[1024,512]{1,0:T(8,128)(2,1)} %copy-done.10, pred[]{:T(512)S(6)} %or.3), kind=kLoop, calls=%fused_computation.1 | loop fusion | flops 524288 | bytes 3145729 | tf_op jit(solution)/shard_map/jit(_where)/select_n | solution.py:194
  119.5 2.3 %broadcast_select_fusion.refs_18_ = bf16[1024,512]{1,0:T(8,128)(2,1)} fusion(bf16[1024,512]{1,0:T(8,128)(2,1)} %copy-done.12, bf16[1024,512]{1,0:T(8,128)(2,1)} %copy-done.9, pred[]{:T(512)S(6)} %or.3), kind=kLoop, calls=%fused_computation | loop fusion | flops 524288 | bytes 3145729 | tf_op jit(solution)/shard_map/jit(_where)/select_n | solution.py:195
  121.9 0.0 collective-permute-done.8.refs_9_
  121.9 0.0 collective-permute-done.7.refs_8_
  121.9 0.0 collective-permute-done.6.refs_7_
  121.9 0.0 collective-permute-done.18.refs_17_
  121.9 0.0 collective-permute-done.17.refs_16_
  121.9 0.0 copy-done.1
  121.9 0.0 copy-done.3
  121.9 0.0 copy-done.5
  121.9 0.0 copy-done.7
  122.0 19.8 %shard_map.58 = (f32[1,512,512]{2,1,0:T(8,128)}, f32[1,3,512,512]{3,2,1,0:T(8,128)}, f32[1,3,512,512]{3,2,1,0:T(8,128)}) custom-call(s32[1]{0:T(128)} %bitcast.position_ref, s32[16]{0:T(128)S(1)} %copy-done.8, s32[16,3]{1,0:T(8,128)S(1)} %copy.6.sig_ref, bf16[3072,512]{1,0:T(8,128)(2,1)} %refs_0_.1, bf16[1024,512]{1,0:T(8,128)(2,1)S(1)} %copy-done.7, ...), custom_call_target="tpu_custom_call" | custom-call | tf_op jit(solution)/shard_map/pallas_call | solution.py:140
  (9 shorter events, 0.0 us)
Async XLA Ops:
  0.6 116.3 %copy-start.13 = (s32[16,3]{0,1:T(4,128)S(1)}, s32[16,3]{0,1:T(4,128)}, u32[]{:S(2)}) copy-start(s32[16,3]{0,1:T(4,128)} %param.4) | copy-start | bytes 580
  2.7 16.5 %collective-permute-start.11 = (bf16[1024,512]{1,0:T(8,128)(2,1)S(1)}, bf16[1024,512]{1,0:T(8,128)(2,1)S(1)}, u32[]{:S(2)}, u32[]{:S(2)}) collective-permute-start(bf16[1024,512]{1,0:T(8,128)(2,1)S(1)} %get-tuple-element.3), channel_id=1, source_target_pairs={{1,4},{3,6},{5,8},{4,1},{7,10},{6,3},{9,12},{8,5},{11,14},{10,7},{... | collective-permute-start | bytes 3145736 | tf_op jit(solution)/shard_map/ppermute | solution.py:169
  6.5 25.4 %collective-permute-start.5 = (bf16[1024,512]{1,0:T(8,128)(2,1)S(1)}, bf16[1024,512]{1,0:T(8,128)(2,1)S(1)}, u32[]{:S(2)}, u32[]{:S(2)}) collective-permute-start(bf16[1024,512]{1,0:T(8,128)(2,1)S(1)} %get-tuple-element.3), channel_id=1, source_target_pairs={{0,2},{1,3},{2,0},{3,1},{4,6},{5,7},{6,4},{7,5},{8,10},{9,11},{10,... | collective-permute-start | bytes 3145736 | tf_op jit(solution)/shard_map/ppermute | solution.py:169
  6.8 27.1 %collective-permute-start.2 = (bf16[1024,512]{1,0:T(8,128)(2,1)S(1)}, bf16[1024,512]{1,0:T(8,128)(2,1)S(1)}, u32[]{:S(2)}, u32[]{:S(2)}) collective-permute-start(bf16[1024,512]{1,0:T(8,128)(2,1)S(1)} %get-tuple-element.3), channel_id=1, source_target_pairs={{0,1},{1,0},{2,3},{3,2},{4,5},{5,4},{6,7},{7,6},{8,9},{9,8},{10,11... | collective-permute-start | bytes 3145736 | tf_op jit(solution)/shard_map/ppermute | solution.py:169
  6.8 27.4 %collective-permute-start.10 = (bf16[1024,512]{1,0:T(8,128)(2,1)S(1)}, bf16[1024,512]{1,0:T(8,128)(2,1)S(1)}, u32[]{:S(2)}, u32[]{:S(2)}) collective-permute-start(bf16[1024,512]{1,0:T(8,128)(2,1)S(1)} %get-tuple-element.4), channel_id=1, source_target_pairs={{1,4},{3,6},{5,8},{4,1},{7,10},{6,3},{9,12},{8,5},{11,14},{10,7},{... | collective-permute-start | bytes 3145736 | tf_op jit(solution)/shard_map/ppermute | solution.py:169
  10.4 44.0 %collective-permute-start.4 = (bf16[1024,512]{1,0:T(8,128)(2,1)S(1)}, bf16[1024,512]{1,0:T(8,128)(2,1)}, u32[]{:S(2)}, u32[]{:S(2)}) collective-permute-start(bf16[1024,512]{1,0:T(8,128)(2,1)S(1)} %get-tuple-element.4), channel_id=1, source_target_pairs={{0,2},{1,3},{2,0},{3,1},{4,6},{5,7},{6,4},{7,5},{8,10},{9,11},{10,... | collective-permute-start | bytes 3145736 | tf_op jit(solution)/shard_map/ppermute | solution.py:169
  19.2 36.4 %collective-permute-start.1 = (bf16[1024,512]{1,0:T(8,128)(2,1)S(1)}, bf16[1024,512]{1,0:T(8,128)(2,1)S(1)}, u32[]{:S(2)}, u32[]{:S(2)}) collective-permute-start(bf16[1024,512]{1,0:T(8,128)(2,1)S(1)} %get-tuple-element.4), channel_id=1, source_target_pairs={{0,1},{1,0},{2,3},{3,2},{4,5},{5,4},{6,7},{7,6},{8,9},{9,8},{10,11... | collective-permute-start | bytes 3145736 | tf_op jit(solution)/shard_map/ppermute | solution.py:169
  31.9 24.7 %collective-permute-start.9 = (bf16[1024,512]{1,0:T(8,128)(2,1)S(1)}, bf16[1024,512]{1,0:T(8,128)(2,1)S(1)}, u32[]{:S(2)}, u32[]{:S(2)}) collective-permute-start(bf16[1024,512]{1,0:T(8,128)(2,1)S(1)} %get-tuple-element.5), channel_id=1, source_target_pairs={{1,4},{3,6},{5,8},{4,1},{7,10},{6,3},{9,12},{8,5},{11,14},{10,7},{... | collective-permute-start | bytes 3145736 | tf_op jit(solution)/shard_map/ppermute | solution.py:169
  33.8 41.0 %collective-permute-start.3 = (bf16[1024,512]{1,0:T(8,128)(2,1)S(1)}, bf16[1024,512]{1,0:T(8,128)(2,1)}, u32[]{:S(2)}, u32[]{:S(2)}) collective-permute-start(bf16[1024,512]{1,0:T(8,128)(2,1)S(1)} %get-tuple-element.5), channel_id=1, source_target_pairs={{0,2},{1,3},{2,0},{3,1},{4,6},{5,7},{6,4},{7,5},{8,10},{9,11},{10,... | collective-permute-start | bytes 3145736 | tf_op jit(solution)/shard_map/ppermute | solution.py:169
  34.1 1.1 copy-start
  35.2 50.9 %collective-permute-start.14 = (bf16[1024,512]{1,0:T(8,128)(2,1)S(1)}, bf16[1024,512]{1,0:T(8,128)(2,1)S(1)}, u32[]{:S(2)}, u32[]{:S(2)}) collective-permute-start(bf16[1024,512]{1,0:T(8,128)(2,1)S(1)} %collective-permute-done.11.refs_12_), channel_id=1, source_target_pairs={{2,0},{1,3},{6,4},{5,7},{10,8},{9,11},{14,12},{13,15},{18,16},{17,... | collective-permute-start | bytes 3145736 | tf_op jit(solution)/shard_map/ppermute | solution.py:169
  54.4 33.1 %collective-permute-start.16 = (bf16[1024,512]{1,0:T(8,128)(2,1)S(1)}, bf16[1024,512]{1,0:T(8,128)(2,1)S(1)}, u32[]{:S(2)}, u32[]{:S(2)}) collective-permute-start(bf16[1024,512]{1,0:T(8,128)(2,1)S(1)} %collective-permute-done.5.refs_6_), channel_id=1, source_target_pairs={{0,4},{4,8},{7,3},{8,12},{11,7},{15,11},{16,20},{20,24},{23,19},{2... | collective-permute-start | bytes 3145736 | tf_op jit(solution)/shard_map/ppermute | solution.py:169
  55.7 1.0 copy-start.2
  56.6 32.2 %collective-permute-start = (bf16[1024,512]{1,0:T(8,128)(2,1)S(1)}, bf16[1024,512]{1,0:T(8,128)(2,1)S(1)}, u32[]{:S(2)}, u32[]{:S(2)}) collective-permute-start(bf16[1024,512]{1,0:T(8,128)(2,1)S(1)} %get-tuple-element.5), channel_id=1, source_target_pairs={{0,1},{1,0},{2,3},{3,2},{4,5},{5,4},{6,7},{7,6},{8,9},{9,8},{10,11... | collective-permute-start | bytes 3145736 | tf_op jit(solution)/shard_map/ppermute | solution.py:169
  56.6 1.0 copy-start.4
  57.6 41.5 %collective-permute-start.13 = (bf16[1024,512]{1,0:T(8,128)(2,1)}, bf16[1024,512]{1,0:T(8,128)(2,1)}, u32[]{:S(2)}, u32[]{:S(2)}) collective-permute-start(bf16[1024,512]{1,0:T(8,128)(2,1)} %collective-permute-done.4.refs_5_), channel_id=1, source_target_pairs={{0,4},{1,5},{4,8},{5,9},{6,2},{7,3},{8,12},{9,13},{10,6},{11,7},{1... | collective-permute-start | bytes 3145736 | tf_op jit(solution)/shard_map/ppermute | solution.py:169
  74.9 40.1 %collective-permute-start.12 = (bf16[1024,512]{1,0:T(8,128)(2,1)}, bf16[1024,512]{1,0:T(8,128)(2,1)}, u32[]{:S(2)}, u32[]{:S(2)}) collective-permute-start(bf16[1024,512]{1,0:T(8,128)(2,1)} %collective-permute-done.3.refs_4_), channel_id=1, source_target_pairs={{0,4},{1,5},{4,8},{5,9},{6,2},{7,3},{8,12},{9,13},{10,6},{11,7},{1... | collective-permute-start | bytes 3145736 | tf_op jit(solution)/shard_map/ppermute | solution.py:169
  86.1 2.8 %copy-start.9 = (bf16[1024,512]{1,0:T(8,128)(2,1)}, bf16[1024,512]{1,0:T(8,128)(2,1)S(1)}, u32[]{:S(2)}) copy-start(bf16[1024,512]{1,0:T(8,128)(2,1)S(1)} %collective-permute-done.14) | copy-start | bytes 3145732
  86.1 28.8 %collective-permute-start.15 = (bf16[1024,512]{1,0:T(8,128)(2,1)S(1)}, bf16[1024,512]{1,0:T(8,128)(2,1)S(1)}, u32[]{:S(2)}, u32[]{:S(2)}) collective-permute-start(bf16[1024,512]{1,0:T(8,128)(2,1)S(1)} %collective-permute-done.14), channel_id=1, source_target_pairs={{0,1},{3,2},{4,5},{7,6},{8,9},{11,10},{12,13},{15,14},{16,17},{19,... | collective-permute-start | bytes 3145736 | tf_op jit(solution)/shard_map/ppermute | solution.py:169
  87.5 27.5 %copy-start.10 = (bf16[1024,512]{1,0:T(8,128)(2,1)}, bf16[1024,512]{1,0:T(8,128)(2,1)S(1)}, u32[]{:S(2)}) copy-start(bf16[1024,512]{1,0:T(8,128)(2,1)S(1)} %collective-permute-done.16) | copy-start | bytes 3145732
  87.5 28.0 %collective-permute-start.19 = (bf16[1024,512]{1,0:T(8,128)(2,1)S(1)}, bf16[1024,512]{1,0:T(8,128)(2,1)S(1)}, u32[]{:S(2)}, u32[]{:S(2)}) collective-permute-start(bf16[1024,512]{1,0:T(8,128)(2,1)S(1)} %collective-permute-done.16), channel_id=1, source_target_pairs={{0,1},{3,2},{4,5},{7,6},{8,9},{11,10},{12,13},{15,14},{16,17},{19,... | collective-permute-start | bytes 3145736 | tf_op jit(solution)/shard_map/ppermute | solution.py:169
  88.9 1.0 copy-start.6
  89.8 32.0 %collective-permute-start.8 = (bf16[1024,512]{1,0:T(8,128)(2,1)S(1)}, bf16[1024,512]{1,0:T(8,128)(2,1)}, u32[]{:S(2)}, u32[]{:S(2)}) collective-permute-start(bf16[1024,512]{1,0:T(8,128)(2,1)S(1)} %collective-permute-done.5.refs_6_), channel_id=1, source_target_pairs={{0,1},{1,0},{2,3},{3,2},{4,5},{5,4},{6,7},{7,6},{8,9},{9,8},{10,11... | collective-permute-start | bytes 3145736 | tf_op jit(solution)/shard_map/ppermute | solution.py:169
  99.2 22.7 %collective-permute-start.7 = (bf16[1024,512]{1,0:T(8,128)(2,1)}, bf16[1024,512]{1,0:T(8,128)(2,1)}, u32[]{:S(2)}, u32[]{:S(2)}) collective-permute-start(bf16[1024,512]{1,0:T(8,128)(2,1)} %collective-permute-done.4.refs_5_), channel_id=1, source_target_pairs={{0,1},{1,0},{2,3},{3,2},{4,5},{5,4},{6,7},{7,6},{8,9},{9,8},{10,11... | collective-permute-start | bytes 3145736 | tf_op jit(solution)/shard_map/ppermute | solution.py:169
  114.9 6.9 %collective-permute-start.6 = (bf16[1024,512]{1,0:T(8,128)(2,1)}, bf16[1024,512]{1,0:T(8,128)(2,1)}, u32[]{:S(2)}, u32[]{:S(2)}) collective-permute-start(bf16[1024,512]{1,0:T(8,128)(2,1)} %collective-permute-done.3.refs_4_), channel_id=1, source_target_pairs={{0,1},{1,0},{2,3},{3,2},{4,5},{5,4},{6,7},{7,6},{8,9},{9,8},{10,11... | collective-permute-start | bytes 3145736 | tf_op jit(solution)/shard_map/ppermute | solution.py:169
  115.0 1.0 copy-start.11
  115.0 6.9 %collective-permute-start.18 = (bf16[1024,512]{1,0:T(8,128)(2,1)}, bf16[1024,512]{1,0:T(8,128)(2,1)}, u32[]{:S(2)}, u32[]{:S(2)}) collective-permute-start(bf16[1024,512]{1,0:T(8,128)(2,1)} %collective-permute-done.13.refs_14_), channel_id=1, source_target_pairs={{0,1},{1,0},{2,3},{3,2},{4,5},{5,4},{6,7},{7,6},{8,9},{9,8},{10,11... | collective-permute-start | bytes 3145736 | tf_op jit(solution)/shard_map/ppermute | solution.py:169
  115.9 1.0 copy-start.12
  115.9 5.9 %collective-permute-start.17 = (bf16[1024,512]{1,0:T(8,128)(2,1)}, bf16[1024,512]{1,0:T(8,128)(2,1)}, u32[]{:S(2)}, u32[]{:S(2)}) collective-permute-start(bf16[1024,512]{1,0:T(8,128)(2,1)} %collective-permute-done.12.refs_13_), channel_id=1, source_target_pairs={{0,1},{1,0},{2,3},{3,2},{4,5},{5,4},{6,7},{7,6},{8,9},{9,8},{10,11... | collective-permute-start | bytes 3145736 | tf_op jit(solution)/shard_map/ppermute | solution.py:169
  117.0 4.9 %copy-start.1 = (bf16[1024,512]{1,0:T(8,128)(2,1)S(1)}, bf16[1024,512]{1,0:T(8,128)(2,1)}, u32[]{:S(2)}) copy-start(bf16[1024,512]{1,0:T(8,128)(2,1)} %copy-done) | copy-start | bytes 3145732
  117.0 4.9 %copy-start.3 = (bf16[1024,512]{1,0:T(8,128)(2,1)S(1)}, bf16[1024,512]{1,0:T(8,128)(2,1)}, u32[]{:S(2)}) copy-start(bf16[1024,512]{1,0:T(8,128)(2,1)} %copy-done.2) | copy-start | bytes 3145732
  117.0 4.9 %copy-start.5 = (bf16[1024,512]{1,0:T(8,128)(2,1)S(1)}, bf16[1024,512]{1,0:T(8,128)(2,1)}, u32[]{:S(2)}) copy-start(bf16[1024,512]{1,0:T(8,128)(2,1)} %copy-done.4) | copy-start | bytes 3145732
  117.0 4.9 %copy-start.7 = (bf16[1024,512]{1,0:T(8,128)(2,1)S(1)}, bf16[1024,512]{1,0:T(8,128)(2,1)}, u32[]{:S(2)}) copy-start(bf16[1024,512]{1,0:T(8,128)(2,1)} %copy-done.6) | copy-start | bytes 3145732
  117.0 4.9 %copy-start.8 = (s32[16]{0:T(128)S(1)}, s32[16]{0:T(128)}, u32[]{:S(2)}) copy-start(s32[16]{0:T(128)} %live_ref.1) | copy-start | bytes 196

commit v2 on v0

v2 whole, which is shorter than its diff:
```python
import functools

import jax
import jax.numpy as jnp
from jax import lax
from jax.experimental import pallas as pl
from jax.experimental.pallas import tpu as pltpu
from jax.sharding import PartitionSpec as P

ROWBLK = 512
HOPS = 3
VMEM_LIMIT = 63 * 2**20
LEVEL = 4
HEAD = 3
TURNS = (2, 1)

SMEM = pl.BlockSpec(memory_space=pltpu.SMEM)
HBM = pl.BlockSpec(memory_space=pltpu.HBM)


def level_route(block_total, moves):
    levels = block_total // LEVEL
    return [
        (LEVEL * z + place, LEVEL * (z + step) + new)
        for z in range(levels)
        for place, step, new in moves
        if 0 <= z + step < levels
    ]


class Geometry:
    def __init__(self, position_ref, live_ref, sig_ref, block_total):
        self.live_ref, self.sig_ref, self.block_total = live_ref, sig_ref, block_total
        self.me = position_ref[0]
        self.place = lax.rem(self.me, LEVEL)
        even = lax.rem(self.place, 2) == 0
        self.upper = self.place >= 2
        self.edge = (self.place == 0) | (self.place == 3)
        self.core = self.me + jnp.where(even, 1, -1)
        self.across = self.me + jnp.where(self.upper, -2, 2)
        self.far = self.me + jnp.where(even, -3, 3)
        self.relay = self.me + jnp.where(self.upper, 2, -2)
        self.both = self.me + (LEVEL - 1) - 2 * self.place
        self.last = self.me + jnp.where(self.edge, 1, 3) * jnp.where(self.upper, 1, -1)

    def live(self, block):
        return self.live_ref[jnp.clip(block, 0, self.block_total - 1)] // ROWBLK

    def count(self, first, second):
        low = jnp.clip(jnp.minimum(first, second), 0, self.block_total - 1)
        hop = jnp.clip(jnp.abs(first - second) - 1, 0, HOPS - 1)
        inside = (second >= 0) & (second < self.block_total)
        rows = jnp.minimum(self.live(first), self.live(second))
        return jnp.where(inside, rows * self.sig_ref[low, hop], 0)

    def place_tile(self, tile, other, up_ref, low_ref, sem, enable=True):
        dist = other - self.me
        hop = jnp.clip(jnp.abs(dist) - 1, 0, HOPS - 1)

        @pl.when(enable & (dist > 0))
        def _():
            pltpu.make_async_copy(tile, up_ref.at[0, hop], sem).start()

        @pl.when(enable & (dist < 0))
        def _():
            pltpu.make_async_copy(tile, low_ref.at[0, hop], sem).start()

    def wait_tile(self, tile, up_ref, sem):
        pltpu.make_async_copy(tile, up_ref.at[0, 0], sem).wait()


def rows_at(ref, r):
    return ref.at[pl.ds(r * ROWBLK, ROWBLK)]


def dot_into(total, left, right):
    total[...] += jnp.dot(left, right, preferred_element_type=jnp.float32)


def gate_kernel(*refs):
    del refs


def after(array, *tokens):
    return pl.pallas_call(
        gate_kernel,
        out_shape=jax.ShapeDtypeStruct(array.shape, array.dtype),
        in_specs=[HBM] * (1 + len(tokens)),
        out_specs=HBM,
        input_output_aliases={0: 0},
        compiler_params=pltpu.CompilerParams(vmem_limit_bytes=VMEM_LIMIT),
    )(array, *tokens)


def pick_kernel(position_ref, edge_ref, inner_ref, *refs, low, sizes):
    outs, (held, in_sem, out_sem) = refs[: len(sizes)], refs[len(sizes) :]
    place = lax.rem(position_ref[0], LEVEL)
    inner = (place == 1) | (place == 2)
    places = [(out, k) for out, size in zip(outs, sizes) for k in range(size)]
    copies = []
    for k, (out, at) in enumerate(places):
        pl.when(inner)(pltpu.make_async_copy(rows_at(inner_ref, low + k), held.at[k], in_sem.at[k]).start)
        pl.when(jnp.logical_not(inner))(pltpu.make_async_copy(rows_at(edge_ref, k), held.at[k], in_sem.at[k]).start)
        copies.append(pltpu.make_async_copy(held.at[k], rows_at(out, at), out_sem.at[k]))
    for k, copy in enumerate(copies):
        pltpu.make_async_copy(rows_at(edge_ref, k), held.at[k], in_sem.at[k]).wait()
        copy.start()
    for copy in copies:
        copy.wait()


def pick(position, edge, inner, low, sizes, *tokens):
    rows, cols = edge.shape
    total = rows // ROWBLK

    def body(position_ref, edge_ref, inner_ref, *refs):
        pick_kernel(position_ref, edge_ref, inner_ref, *refs[len(tokens) :], low=low, sizes=sizes)

    return pl.pallas_call(
        body,
        out_shape=tuple(jax.ShapeDtypeStruct((size * ROWBLK, cols), edge.dtype) for size in sizes),
        in_specs=[SMEM] + [HBM] * (2 + len(tokens)),
        out_specs=(HBM,) * len(sizes),
        scratch_shapes=[
            pltpu.VMEM((total, ROWBLK, cols), edge.dtype),
            pltpu.SemaphoreType.DMA((total,)),
            pltpu.SemaphoreType.DMA((total,)),
        ],
        compiler_params=pltpu.CompilerParams(vmem_limit_bytes=VMEM_LIMIT),
    )(position, edge, inner, *tokens)


def own_kernel(position_ref, live_ref, sig_ref, own_ref, diag_ref, own_t_ref, own, own_t, tile, in_sem, turned_sem, out_sem, *, block_total):
    steps = own.shape[0]
    geo = Geometry(position_ref, live_ref, sig_ref, block_total)
    count = geo.live(geo.me)

    def in_copy(r):
        return pltpu.make_async_copy(rows_at(own_ref, r), own.at[r], in_sem.at[r])

    def turned_copy(r):
        return pltpu.make_async_copy(own_t.at[r], own_t_ref.at[r], turned_sem.at[r])

    for r in range(steps):
        pl.when(r < count)(in_copy(r).start)
    tile[...] = jnp.zeros_like(tile)

    @pl.loop(0, count)
    def _(r):
        in_copy(r).wait()
        own_t[r] = own[r].T
        turned_copy(r).start()
        dot_into(tile, own_t[r], own[r])

    out_copy = pltpu.make_async_copy(tile, diag_ref.at[0], out_sem.at[0])
    out_copy.start()

    @pl.loop(0, count)
    def _(r):
        turned_copy(r).wait()

    out_copy.wait()


def own_tile(scalars, own, block_total):
    rows, cols = own.shape
    steps = rows // ROWBLK
    return pl.pallas_call(
        functools.partial(own_kernel, block_total=block_total),
        out_shape=(
            jax.ShapeDtypeStruct((1, cols, cols), jnp.float32),
            jax.ShapeDtypeStruct((steps, cols, ROWBLK), own.dtype),
        ),
        in_specs=[SMEM] * 3 + [HBM],
        out_specs=(HBM,) * 2,
        scratch_shapes=[
            pltpu.VMEM((steps, ROWBLK, cols), own.dtype),
            pltpu.VMEM((steps, cols, ROWBLK), own.dtype),
            pltpu.VMEM((cols, cols), jnp.float32),
            pltpu.SemaphoreType.DMA((steps,)),
            pltpu.SemaphoreType.DMA((steps,)),
            pltpu.SemaphoreType.DMA((1,)),
        ],
        compiler_params=pltpu.CompilerParams(vmem_limit_bytes=VMEM_LIMIT),
        cost_estimate=pl.CostEstimate(
            flops=2 * rows * cols * cols, bytes_accessed=4 * rows * cols + 4 * cols * cols, transcendentals=0
        ),
    )(*scalars, own)


def core_kernel(
    position_ref, live_ref, sig_ref, core_ref, own_t_ref, up_ref, low_ref, core_t_ref, own_t, core, core_t, tile, sems,
    turned_sem, out_sem, *, block_total,
):
    steps = core.shape[0]
    geo = Geometry(position_ref, live_ref, sig_ref, block_total)
    core_count = geo.live(geo.core)
    pair_count = geo.count(geo.me, geo.core)

    def core_copy(r):
        return pltpu.make_async_copy(rows_at(core_ref, r), core.at[r], sems.at[0, r])

    def own_copy(r):
        return pltpu.make_async_copy(own_t_ref.at[r], own_t.at[r], sems.at[1, r])

    def turned_copy(r):
        return pltpu.make_async_copy(core_t.at[r], core_t_ref.at[r], turned_sem.at[r])

    for r in range(steps):
        pl.when(r < core_count)(core_copy(r).start)
        pl.when(r < pair_count)(own_copy(r).start)
    tile[...] = jnp.zeros_like(tile)

    @pl.loop(0, core_count)
    def _(r):
        core_copy(r).wait()
        core_t[r] = core[r].T
        turned_copy(r).start()

        @pl.when(r < pair_count)
        def _():
            own_copy(r).wait()
            dot_into(tile, own_t[r], core[r])

    geo.place_tile(tile, geo.core, up_ref, low_ref, out_sem.at[0])

    @pl.loop(0, core_count)
    def _(r):
        turned_copy(r).wait()

    geo.wait_tile(tile, up_ref, out_sem.at[0])


def core_tile(scalars, core, own_t, block_total):
    rows, cols = core.shape
    steps = rows // ROWBLK
    three = jax.ShapeDtypeStruct((1, HOPS, cols, cols), jnp.float32)
    return pl.pallas_call(
        functools.partial(core_kernel, block_total=block_total),
        out_shape=(three, three, jax.ShapeDtypeStruct(own_t.shape, own_t.dtype)),
        in_specs=[SMEM] * 3 + [HBM] * 2,
        out_specs=(HBM,) * 3,
        scratch_shapes=[
            pltpu.VMEM((steps, cols, ROWBLK), core.dtype),
            pltpu.VMEM((steps, ROWBLK, cols), core.dtype),
            pltpu.VMEM((steps, cols, ROWBLK), core.dtype),
            pltpu.VMEM((cols, cols), jnp.float32),
            pltpu.SemaphoreType.DMA((2, steps)),
            pltpu.SemaphoreType.DMA((steps,)),
            pltpu.SemaphoreType.DMA((1,)),
        ],
        compiler_params=pltpu.CompilerParams(vmem_limit_bytes=VMEM_LIMIT),
        cost_estimate=pl.CostEstimate(
            flops=2 * rows * cols * cols, bytes_accessed=6 * rows * cols + 4 * cols * cols, transcendentals=0
        ),
    )(*scalars, core, own_t)


def pair_kernel(
    position_ref, live_ref, sig_ref, own_t_ref, core_t_ref, piece_refs, before, outs, own_t, core_t, held, tiles, sems,
    before_sem, out_sem, *, which, low, high, sources, final, block_total,
):
    geo = Geometry(position_ref, live_ref, sig_ref, block_total)
    other = getattr(geo, which)
    shared = which != "far"
    count = geo.count(geo.me, other)
    core_count = geo.count(geo.core, other) if shared else 0
    either = jnp.maximum(count, core_count)

    for r in range(low, high):
        at, (ref, offset) = r - low, sources[r]
        own_copy = pltpu.make_async_copy(own_t_ref.at[r], own_t.at[at], sems.at[0, at])
        pl.when(r < count)(own_copy.start)
        if shared:
            core_copy = pltpu.make_async_copy(core_t_ref.at[r], core_t.at[at], sems.at[1, at])
            pl.when(r < core_count)(core_copy.start)
        held_copy = pltpu.make_async_copy(rows_at(piece_refs[ref], offset), held.at[at], sems.at[2, at])
        pl.when(r < either)(held_copy.start)

    if before:
        loads = [pltpu.make_async_copy(before[i], tiles.at[i], before_sem.at[i]) for i in range(2)]
        for load in loads:
            load.start()
        for load in loads:
            load.wait()
    else:
        tiles[...] = jnp.zeros_like(tiles)

    @pl.loop(0, high - low)
    def _(at):
        r = at + low

        @pl.when(r < either)
        def _():
            pltpu.make_async_copy(rows_at(piece_refs[0], 0), held.at[at], sems.at[2, at]).wait()

        @pl.when(r < count)
        def _():
            pltpu.make_async_copy(own_t_ref.at[0], own_t.at[at], sems.at[0, at]).wait()
            dot_into(tiles.at[0], own_t[at], held[at])

        if shared:
            @pl.when(r < core_count)
            def _():
                pltpu.make_async_copy(core_t_ref.at[0], core_t.at[at], sems.at[1, at]).wait()
                dot_into(tiles.at[1], core_t[at], held[at])

    if shared:
        swap_copy = pltpu.make_async_copy(tiles.at[1], outs[-1], out_sem.at[1])
        swap_copy.start()
    if final:
        geo.place_tile(tiles.at[0], other, outs[0], outs[1], out_sem.at[0])
        geo.wait_tile(tiles.at[0], outs[0], out_sem.at[0])
    else:
        own_out = pltpu.make_async_copy(tiles.at[0], outs[0], out_sem.at[0])
        own_out.start()
        own_out.wait()
    if shared:
        swap_copy.wait()


def pair_tiles(scalars, turned, which, pieces, low, high, before, outputs, block_total):
    steps, cols, _ = turned[0].shape
    tile = jax.ShapeDtypeStruct((cols, cols), jnp.float32)
    final = outputs is not None
    places = [(i, k) for i, piece in enumerate(pieces) for k in range(piece.shape[0] // ROWBLK)]
    sources = dict(zip(range(low, high), places))
    before, chained = list(before or ()), list(outputs or ())
    n_in, n_before = len(pieces), len(before)
    n_out = (2 if final else 1) + (which != "far")

    def body(position_ref, live_ref, sig_ref, own_t_ref, core_t_ref, *refs):
        outs_at = n_in + n_before + len(chained)
        pair_kernel(
            position_ref, live_ref, sig_ref, own_t_ref, core_t_ref, refs[:n_in], refs[n_in : n_in + n_before],
            refs[outs_at : outs_at + n_out], *refs[outs_at + n_out :],
            which=which, low=low, high=high, sources=sources, final=final, block_total=block_total,
        )

    span = high - low
    return pl.pallas_call(
        body,
        out_shape=tuple(jax.ShapeDtypeStruct(c.shape, c.dtype) for c in chained) + (tile,) * (n_out - len(chained)),
        in_specs=[SMEM] * 3 + [HBM] * (2 + n_in + n_before + len(chained)),
        out_specs=(HBM,) * n_out,
        scratch_shapes=[pltpu.VMEM((span, cols, ROWBLK), turned[0].dtype)] * 2
        + [
            pltpu.VMEM((span, ROWBLK, cols), turned[0].dtype),
            pltpu.VMEM((2, cols, cols), jnp.float32),
            pltpu.SemaphoreType.DMA((3, span)),
            pltpu.SemaphoreType.DMA((2,)),
            pltpu.SemaphoreType.DMA((2,)),
        ],
        input_output_aliases={5 + n_in + n_before + i: i for i in range(len(chained))},
        compiler_params=pltpu.CompilerParams(vmem_limit_bytes=VMEM_LIMIT),
        cost_estimate=pl.CostEstimate(
            flops=4 * span * ROWBLK * cols * cols,
            bytes_accessed=6 * span * ROWBLK * cols + 16 * cols * cols,
            transcendentals=0,
        ),
    )(*scalars, *turned, *pieces, *before, *chained)


def place_kernel(position_ref, live_ref, sig_ref, tile_ref, _up, _low, up_ref, low_ref, tile, in_sem, out_sem, *, block_total):
    geo = Geometry(position_ref, live_ref, sig_ref, block_total)
    copy = pltpu.make_async_copy(tile_ref, tile, in_sem.at[0])
    copy.start()
    copy.wait()
    geo.place_tile(tile, geo.both, up_ref, low_ref, out_sem.at[0])
    geo.wait_tile(tile, up_ref, out_sem.at[0])


def place_both(scalars, tile, outputs, block_total):
    return pl.pallas_call(
        functools.partial(place_kernel, block_total=block_total),
        out_shape=tuple(jax.ShapeDtypeStruct(o.shape, o.dtype) for o in outputs),
        in_specs=[SMEM] * 3 + [HBM] * 3,
        out_specs=(HBM,) * 2,
        scratch_shapes=[
            pltpu.VMEM(tile.shape, jnp.float32),
            pltpu.SemaphoreType.DMA((1,)),
            pltpu.SemaphoreType.DMA((1,)),
        ],
        input_output_aliases={4: 0, 5: 1},
        compiler_params=pltpu.CompilerParams(vmem_limit_bytes=VMEM_LIMIT),
    )(*scalars, tile, *outputs)


def end_kernel(
    position_ref, live_ref, sig_ref, own_t_ref, piece_refs, before, outs, own_t, held, tiles, sems, own_sem, before_sem,
    out_sem, *, low, sources, block_total,
):
    span = own_t.shape[0]
    geo = Geometry(position_ref, live_ref, sig_ref, block_total)
    others = (geo.relay, geo.last)
    counts = [geo.count(geo.me, other) for other in others]
    either = jnp.maximum(*counts)

    def own_copy(at):
        return pltpu.make_async_copy(own_t_ref.at[low + at], own_t.at[at], own_sem.at[at])

    loads = [pltpu.make_async_copy(before[i], tiles.at[i], before_sem.at[i]) for i in range(2)]
    for at in range(span):
        pl.when(low + at < either)(own_copy(at).start)
    for i in range(2):
        loads[i].start()
        for at in range(span):
            ref, offset = sources[i][at]
            held_copy = pltpu.make_async_copy(rows_at(piece_refs[ref], offset), held.at[i, at], sems.at[i, at])
            pl.when(low + at < counts[i])(held_copy.start)
    for at in range(span):
        pl.when(low + at < either)(own_copy(at).wait)
    for i in range(2):
        loads[i].wait()

        @pl.loop(0, jnp.maximum(counts[i] - low, 0))
        def _(at):
            pltpu.make_async_copy(rows_at(piece_refs[0], 0), held.at[i, at], sems.at[i, at]).wait()
            dot_into(tiles.at[i], own_t[at], held[i, at])

        geo.place_tile(tiles.at[i], others[i], outs[0], outs[1], out_sem.at[i])
    for i in range(2):
        geo.wait_tile(tiles.at[i], outs[0], out_sem.at[i])


def end_tiles(scalars, own_t, pieces, swapped, low, before, outputs, block_total):
    steps, cols, _ = own_t.shape
    span = steps - low
    arrays = [*pieces, *swapped]
    sources = [
        [(i + first, k) for i, piece in enumerate(group) for k in range(piece.shape[0] // ROWBLK)]
        for first, group in ((0, pieces), (len(pieces), swapped))
    ]
    n_in = len(arrays)

    def body(position_ref, live_ref, sig_ref, own_t_ref, *refs):
        end_kernel(
            position_ref, live_ref, sig_ref, own_t_ref, refs[:n_in], refs[n_in : n_in + 2], refs[n_in + 4 : n_in + 6],
            *refs[n_in + 6 :], low=low, sources=sources, block_total=block_total,
        )

    return pl.pallas_call(
        body,
        out_shape=tuple(jax.ShapeDtypeStruct(o.shape, o.dtype) for o in outputs),
        in_specs=[SMEM] * 3 + [HBM] * (5 + n_in),
        out_specs=(HBM,) * 2,
        scratch_shapes=[
            pltpu.VMEM((span, cols, ROWBLK), own_t.dtype),
            pltpu.VMEM((2, span, ROWBLK, cols), own_t.dtype),
            pltpu.VMEM((2, cols, cols), jnp.float32),
            pltpu.SemaphoreType.DMA((2, span)),
            pltpu.SemaphoreType.DMA((span,)),
            pltpu.SemaphoreType.DMA((2,)),
            pltpu.SemaphoreType.DMA((2,)),
        ],
        input_output_aliases={6 + n_in: 0, 7 + n_in: 1},
        compiler_params=pltpu.CompilerParams(vmem_limit_bytes=VMEM_LIMIT),
    )(*scalars, own_t, *arrays, *before, *outputs)


def per_device(b_half, significant, live_rows):
    block_total = lax.axis_size("ao")
    position = lax.axis_index("ao").astype(jnp.int32)[None]
    scalars = (position, live_rows, significant)
    steps = b_half.shape[0] // ROWBLK

    def send(block, moves):
        return lax.ppermute(block, "ao", level_route(block_total, moves))

    cores = [(j, 0, j ^ 1) for j in range(LEVEL)]
    across = [(j, 0, j ^ 2) for j in range(LEVEL)]
    far = [(1, 1, 0), (0, -1, 1), (3, 1, 2), (2, -1, 3)]
    relay = [(0, 1, 0), (1, 1, 1), (2, -1, 2), (3, -1, 3)]
    turn = [(0, 1, 0), (3, -1, 3), (1, 0, 2), (2, 0, 1)]

    y_head = send(b_half[: HEAD * ROWBLK], across)
    y_tail = send(b_half[HEAD * ROWBLK :], across)
    core = send(b_half, cores)
    far_block = send(b_half, far)

    diagonal, own_t = own_tile(scalars, b_half, block_total)
    upper, lower, core_t = core_tile(scalars, core, own_t, block_total)
    turned = (own_t, core_t)
    y_head = after(y_head, core_t)
    relayed = send(y_head, relay)
    upper, lower = pair_tiles(scalars, turned, "far", [far_block], 0, steps, None, (upper, lower), block_total)
    y_partial = pair_tiles(scalars, turned, "across", [y_head], 0, HEAD, None, None, block_total)

    turns = [send(piece, turn) for piece in pick(position, y_tail, far_block, HEAD, TURNS, upper, y_partial[0])]
    own_part, core_part = pair_tiles(scalars, turned, "relay", [relayed], 0, HEAD, None, None, block_total)
    upper, lower, both = pair_tiles(
        scalars, turned, "across", [y_tail], HEAD, steps, y_partial, (upper, lower), block_total
    )
    upper, lower = place_both(scalars, send(both, cores), (upper, lower), block_total)
    swapped = [send(piece, cores) for piece in turns]
    upper, lower = end_tiles(
        scalars, own_t, turns, swapped, HEAD, (own_part, send(core_part, cores)), (upper, lower), block_total
    )
    return diagonal, upper, lower


def solution(mesh):
    in_specs = (P("groups", "ao"), P("groups", None), P("groups"))
    out_specs = (
        P(("groups", "ao"), None, None),
        P(("groups", "ao"), None, None, None),
        P(("groups", "ao"), None, None, None),
    )
    return jax.shard_map(
        per_device, mesh=mesh, in_specs=in_specs, out_specs=out_specs, check_vma=False
    )
```

time: 323 us -> 113 us (0.35)
  the two profiles are of different devices: /device:TPU:5 before, /device:TPU:16 now
where the time goes in v2:
time: 113 us
  waiting for transfers between devices  52.4 us (46%)
  Pallas kernels  40.3 us (36%)
  starting transfers between devices  14.6 us (13%)
  local copies, waits for them, and re-layouts  4.45 us (4%)
    ppermute x11, waiting for transfers between devices, send(): return lax.ppermute(block, 'ao', level_route(block_total, moves))  52.4 us
    pallas_call x4, Pallas kernels, pair_tiles(): pl.pallas_call(body, out_shape=tuple((jax.ShapeDtypeStruct(c.shape, c.dty...  20.1 us
    ppermute x11, starting transfers between devices, send(): return lax.ppermute(block, 'ao', level_route(block_total, moves))  14.6 us
    pallas_call x1, Pallas kernels, end_tiles(): pl.pallas_call(body, out_shape=tuple((jax.ShapeDtypeStruct(o.shape, o.dty...  5.29 us
    pallas_call x1, Pallas kernels, own_tile(): pl.pallas_call(functools.partial(own_kernel, block_total=block_total), ou...  5.28 us
    pallas_call x1, Pallas kernels, core_tile(): pl.pallas_call(functools.partial(core_kernel, block_total=block_total), o...  4.32 us
    slice x1, local copies, waits for them, and re-layouts, per_device(): y_head = send(b_half[:HEAD * ROWBLK], across)  3.76 us
    pallas_call x1, Pallas kernels, place_both(): pl.pallas_call(functools.partial(place_kernel, block_total=block_total),...  3.01 us
  transfers between devices with their start and end apart: 11, of which 3 were waited for; matrix products, arithmetic and copies ran while one was open for 4% of the time, Pallas kernels for 31%

profile of v2, /device:TPU:16, one launch (start us, length us, event | category | flops | bytes accessed | tf_op | source)
XLA Modules:
  0.0 112.6 jit_solution(13927603330105114880)
XLA Ops:
  0.6 0.0 copy-start.1
  0.6 0.1 collective-permute-start.2
  0.7 2.4 %collective-permute-start.1 = (bf16[3072,512]{1,0:T(8,128)(2,1)}, bf16[3072,512]{1,0:T(8,128)(2,1)}, u32[]{:S(2)}, u32[]{:S(2)}) collective-permute-start(bf16[3072,512]{1,0:T(8,128)(2,1)} %own_ref.1), channel_id=1, source_target_pairs={{1,4},{3,6},{5,8},{4,1},{7,10},{6,3},{9,12},{8,5},{11,14},{10,7},{... | collective-permute-start | bytes 9437192 | tf_op jit(solution)/shard_map/ppermute | solution.py:468
  3.2 3.8 %fusion = (bf16[1536,512]{1,0:T(8,128)(2,1)}, bf16[1536,512]{1,0:T(8,128)(2,1)}) fusion(bf16[3072,512]{1,0:T(8,128)(2,1)} %own_ref.1), kind=kLoop, calls=%fused_computation | loop fusion | bytes 6291456 | tf_op jit(solution)/shard_map/slice | solution.py:476
  6.9 1.5 %collective-permute-start.3 = (bf16[1536,512]{1,0:T(8,128)(2,1)}, bf16[1536,512]{1,0:T(8,128)(2,1)}, u32[]{:S(2)}, u32[]{:S(2)}) collective-permute-start(bf16[1536,512]{1,0:T(8,128)(2,1)} %get-tuple-element.43), channel_id=1, source_target_pairs={{0,2},{1,3},{2,0},{3,1},{4,6},{5,7},{6,4},{7,5},{8,10},{9,11},{10,... | collective-permute-start | bytes 4718600 | tf_op jit(solution)/shard_map/ppermute | solution.py:468
  8.5 0.5 collective-permute-start
  9.0 0.0 copy-done.1
  9.0 0.7 copy.15.sig_ref
  9.7 5.3 %shard_map.58 = (f32[1,512,512]{2,1,0:T(8,128)}, bf16[6,512,512]{2,1,0:T(8,128)(2,1)}) custom-call(s32[1]{0:T(128)} %bitcast.position_ref, s32[16]{0:T(128)} %live_ref.15, s32[16,3]{1,0:T(8,128)} %copy.15.sig_ref, bf16[3072,512]{1,0:T(8,128)(2,1)} %own_ref.1), custom_call_target="tpu_custom_call" | custom-call | flops 1610612736 | bytes 7340032 | tf_op jit(solution)/shard_map/pallas_call | solution.py:168
  14.9 0.0 collective-permute-done.2.core_ref
  14.9 4.3 %shard_map.59 = (f32[1,3,512,512]{3,2,1,0:T(8,128)}, f32[1,3,512,512]{3,2,1,0:T(8,128)}, bf16[6,512,512]{2,1,0:T(8,128)(2,1)}) custom-call(s32[1]{0:T(128)} %bitcast.position_ref, s32[16]{0:T(128)} %live_ref.15, s32[16,3]{1,0:T(8,128)} %copy.15.sig_ref, bf16[3072,512]{1,0:T(8,128)(2,1)} %collective-permute-done.2.core_ref, ...), custom_call_target="tpu_custom_call" | custom-call | flops 1610612736 | bytes 10485760 | tf_op jit(solution)/shard_map/pallas_call | solution.py:238
  19.3 25.1 %collective-permute-done.3.refs_0_ = bf16[1536,512]{1,0:T(8,128)(2,1)} collective-permute-done((bf16[1536,512]{1,0:T(8,128)(2,1)}, bf16[1536,512]{1,0:T(8,128)(2,1)}, u32[]{:S(2)}, u32[]{:S(2)}) %collective-permute-start.3) | collective-permute-done | bytes 1572896 | tf_op jit(solution)/shard_map/ppermute | solution.py:468
  44.3 3.6 %collective-permute-start.8 = (bf16[1536,512]{1,0:T(8,128)(2,1)}, bf16[1536,512]{1,0:T(8,128)(2,1)}, u32[]{:S(2)}, u32[]{:S(2)}) collective-permute-start(bf16[1536,512]{1,0:T(8,128)(2,1)} %shard_map.61.refs_0_), channel_id=1, source_target_pairs={{0,4},{1,5},{4,8},{5,9},{6,2},{7,3},{8,12},{9,13},{10,6},{11,7},{1... | collective-permute-start | bytes 4718600 | tf_op jit(solution)/shard_map/ppermute | solution.py:468
  47.9 6.3 %shard_map.62 = (f32[512,512]{1,0:T(8,128)}, f32[512,512]{1,0:T(8,128)}) custom-call(s32[1]{0:T(128)} %bitcast.position_ref, s32[16]{0:T(128)} %live_ref.15, s32[16,3]{1,0:T(8,128)} %copy.15.sig_ref, bf16[6,512,512]{2,1,0:T(8,128)(2,1)} %get-tuple-element.24.own_t_ref, bf16[6,512,512]{2,1,0:T(8,128)(2,1)} %get-tuple-element.25.core_t_ref.refs_1_, ...), custom_call_target="tpu_custom_call" | custom-call | flops 1610612736 | bytes 8912896 | tf_op jit(solution)/shard_map/pallas_call | solution.py:341
  54.2 0.0 collective-permute-done.1.refs_0_.inner_ref
  54.2 3.7 %shard_map.60 = (f32[1,3,512,512]{3,2,1,0:T(8,128)}, f32[1,3,512,512]{3,2,1,0:T(8,128)}) custom-call(s32[1]{0:T(128)} %bitcast.position_ref, s32[16]{0:T(128)} %live_ref.15, s32[16,3]{1,0:T(8,128)} %copy.15.sig_ref, bf16[6,512,512]{2,1,0:T(8,128)(2,1)} %get-tuple-element.24.own_t_ref, ...), custom_call_target="tpu_custom_call", output_to_operand_aliasing={{0}: (6, {}), {1}: (7, {})} | custom-call | flops 3221225472 | bytes 13631488 | tf_op jit(solution)/shard_map/pallas_call | solution.py:341
  57.9 20.1 %collective-permute-done.edge_ref.refs_0_ = bf16[1536,512]{1,0:T(8,128)(2,1)} collective-permute-done((bf16[1536,512]{1,0:T(8,128)(2,1)}, bf16[1536,512]{1,0:T(8,128)(2,1)}, u32[]{:S(2)}, u32[]{:S(2)}) %collective-permute-start) | collective-permute-done | bytes 1572896 | tf_op jit(solution)/shard_map/ppermute | solution.py:468
  78.0 2.2 %shard_map.63 = (bf16[1024,512]{1,0:T(8,128)(2,1)}, bf16[512,512]{1,0:T(8,128)(2,1)}) custom-call(s32[1]{0:T(128)} %bitcast.position_ref, bf16[1536,512]{1,0:T(8,128)(2,1)} %collective-permute-done.edge_ref.refs_0_, bf16[3072,512]{1,0:T(8,128)(2,1)} %collective-permute-done.1.refs_0_.inner_ref, f32[1,3,512,512]{3,2,1,0:T(8,128)} %get-tuple-element.28.refs_0_.refs_3_, ...), custom_call_target="tpu_custom_call" | custom-call | tf_op jit(solution)/shard_map/pallas_call | solution.py:119
  80.3 3.2 %collective-permute-start.4 = (bf16[1024,512]{1,0:T(8,128)(2,1)}, bf16[1024,512]{1,0:T(8,128)(2,1)}, u32[]{:S(2)}, u32[]{:S(2)}) collective-permute-start(bf16[1024,512]{1,0:T(8,128)(2,1)} %get-tuple-element.30), channel_id=1, source_target_pairs={{0,4},{1,2},{2,1},{4,8},{7,3},{5,6},{6,5},{8,12},{11,7},{9,10},{10... | collective-permute-start | bytes 3145736 | tf_op jit(solution)/shard_map/ppermute | solution.py:468
  83.5 1.9 %collective-permute-start.5 = (bf16[512,512]{1,0:T(8,128)(2,1)}, bf16[512,512]{1,0:T(8,128)(2,1)S(1)}, u32[]{:S(2)}, u32[]{:S(2)}) collective-permute-start(bf16[512,512]{1,0:T(8,128)(2,1)} %get-tuple-element.31), channel_id=1, source_target_pairs={{0,4},{1,2},{2,1},{4,8},{7,3},{5,6},{6,5},{8,12},{11,7},{9,10},{10... | collective-permute-start | bytes 1572872 | tf_op jit(solution)/shard_map/ppermute | solution.py:468
  85.4 3.8 %shard_map.65 = (f32[1,3,512,512]{3,2,1,0:T(8,128)}, f32[1,3,512,512]{3,2,1,0:T(8,128)}, f32[512,512]{1,0:T(8,128)}) custom-call(s32[1]{0:T(128)} %bitcast.position_ref, s32[16]{0:T(128)} %live_ref.15, s32[16,3]{1,0:T(8,128)} %copy.15.sig_ref, bf16[6,512,512]{2,1,0:T(8,128)(2,1)} %get-tuple-element.24.own_t_ref, ...), custom_call_target="tpu_custom_call", output_to_operand_aliasing={{0}: (8, {}), {1}: (9, {})} | custom-call | flops 1610612736 | bytes 8912896 | tf_op jit(solution)/shard_map/pallas_call | solution.py:341
  89.2 0.8 collective-permute-start.10
  90.1 7.2 %collective-permute-done.4.refs_0_ = bf16[1024,512]{1,0:T(8,128)(2,1)} collective-permute-done((bf16[1024,512]{1,0:T(8,128)(2,1)}, bf16[1024,512]{1,0:T(8,128)(2,1)}, u32[]{:S(2)}, u32[]{:S(2)}) %collective-permute-start.4) | collective-permute-done | bytes 1048608 | tf_op jit(solution)/shard_map/ppermute | solution.py:468
  97.3 0.0 collective-permute-start.6
  97.3 0.0 collective-permute-done.8.refs_0_
  97.3 6.3 %shard_map.64 = (f32[512,512]{1,0:T(8,128)}, f32[512,512]{1,0:T(8,128)}) custom-call(s32[1]{0:T(128)} %bitcast.position_ref, s32[16]{0:T(128)} %live_ref.15, s32[16,3]{1,0:T(8,128)} %copy.15.sig_ref, bf16[6,512,512]{2,1,0:T(8,128)(2,1)} %get-tuple-element.24.own_t_ref, bf16[6,512,512]{2,1,0:T(8,128)(2,1)} %get-tuple-element.25.core_t_ref.refs_1_, ...), custom_call_target="tpu_custom_call" | custom-call | flops 1610612736 | bytes 8912896 | tf_op jit(solution)/shard_map/pallas_call | solution.py:341
  103.7 0.1 collective-permute-start.9
  103.7 0.0 collective-permute-done.5.refs_1_
  103.7 0.0 copy-start
  103.8 0.5 collective-permute-start.7
  104.2 0.0 collective-permute-done.10.tile_ref
  104.2 3.0 %shard_map.66 = (f32[1,3,512,512]{3,2,1,0:T(8,128)}, f32[1,3,512,512]{3,2,1,0:T(8,128)}) custom-call(s32[1]{0:T(128)} %bitcast.position_ref, s32[16]{0:T(128)} %live_ref.15, s32[16,3]{1,0:T(8,128)} %copy.15.sig_ref, f32[512,512]{1,0:T(8,128)} %collective-permute-done.10.tile_ref, ...), custom_call_target="tpu_custom_call", output_to_operand_aliasing={{0}: (4, {}), {1}: (5, {})} | custom-call | tf_op jit(solution)/shard_map/pallas_call | solution.py:374
  107.3 0.0 copy-done
  107.3 0.0 collective-permute-done.7.refs_3_
  107.3 0.0 collective-permute-done.6.refs_2_
  107.3 0.0 collective-permute-done.9.refs_5_
  107.3 5.3 %shard_map.67 = (f32[1,3,512,512]{3,2,1,0:T(8,128)}, f32[1,3,512,512]{3,2,1,0:T(8,128)}) custom-call(s32[1]{0:T(128)} %bitcast.position_ref, s32[16]{0:T(128)} %live_ref.15, s32[16,3]{1,0:T(8,128)} %copy.15.sig_ref, bf16[6,512,512]{2,1,0:T(8,128)(2,1)} %get-tuple-element.24.own_t_ref, ...), custom_call_target="tpu_custom_call", output_to_operand_aliasing={{0}: (10, {}), {1}: (11, {})} | custom-call | tf_op jit(solution)/shard_map/pallas_call | solution.py:442
  (1 shorter events, 0.0 us)
Async XLA Ops:
  0.6 8.3 %copy-start.1 = (s32[16,3]{0,1:T(4,128)S(1)}, s32[16,3]{0,1:T(4,128)}, u32[]{:S(2)}) copy-start(s32[16,3]{0,1:T(4,128)} %param.4) | copy-start | bytes 580
  0.6 14.3 %collective-permute-start.2 = (bf16[3072,512]{1,0:T(8,128)(2,1)}, bf16[3072,512]{1,0:T(8,128)(2,1)}, u32[]{:S(2)}, u32[]{:S(2)}) collective-permute-start(bf16[3072,512]{1,0:T(8,128)(2,1)} %own_ref.1), channel_id=1, source_target_pairs={{0,1},{1,0},{2,3},{3,2},{4,5},{5,4},{6,7},{7,6},{8,9},{9,8},{10,11... | collective-permute-start | bytes 9437192 | tf_op jit(solution)/shard_map/ppermute | solution.py:468
  0.7 53.5 %collective-permute-start.1 = (bf16[3072,512]{1,0:T(8,128)(2,1)}, bf16[3072,512]{1,0:T(8,128)(2,1)}, u32[]{:S(2)}, u32[]{:S(2)}) collective-permute-start(bf16[3072,512]{1,0:T(8,128)(2,1)} %own_ref.1), channel_id=1, source_target_pairs={{1,4},{3,6},{5,8},{4,1},{7,10},{6,3},{9,12},{8,5},{11,14},{10,7},{... | collective-permute-start | bytes 9437192 | tf_op jit(solution)/shard_map/ppermute | solution.py:468
  6.9 37.4 %collective-permute-start.3 = (bf16[1536,512]{1,0:T(8,128)(2,1)}, bf16[1536,512]{1,0:T(8,128)(2,1)}, u32[]{:S(2)}, u32[]{:S(2)}) collective-permute-start(bf16[1536,512]{1,0:T(8,128)(2,1)} %get-tuple-element.43), channel_id=1, source_target_pairs={{0,2},{1,3},{2,0},{3,1},{4,6},{5,7},{6,4},{7,5},{8,10},{9,11},{10,... | collective-permute-start | bytes 4718600 | tf_op jit(solution)/shard_map/ppermute | solution.py:468
  8.5 69.6 %collective-permute-start = (bf16[1536,512]{1,0:T(8,128)(2,1)}, bf16[1536,512]{1,0:T(8,128)(2,1)}, u32[]{:S(2)}, u32[]{:S(2)}) collective-permute-start(bf16[1536,512]{1,0:T(8,128)(2,1)} %get-tuple-element.44), channel_id=1, source_target_pairs={{0,2},{1,3},{2,0},{3,1},{4,6},{5,7},{6,4},{7,5},{8,10},{9,11},{10,... | collective-permute-start | bytes 4718600 | tf_op jit(solution)/shard_map/ppermute | solution.py:468
  44.3 53.0 %collective-permute-start.8 = (bf16[1536,512]{1,0:T(8,128)(2,1)}, bf16[1536,512]{1,0:T(8,128)(2,1)}, u32[]{:S(2)}, u32[]{:S(2)}) collective-permute-start(bf16[1536,512]{1,0:T(8,128)(2,1)} %shard_map.61.refs_0_), channel_id=1, source_target_pairs={{0,4},{1,5},{4,8},{5,9},{6,2},{7,3},{8,12},{9,13},{10,6},{11,7},{1... | collective-permute-start | bytes 4718600 | tf_op jit(solution)/shard_map/ppermute | solution.py:468
  80.3 17.0 %collective-permute-start.4 = (bf16[1024,512]{1,0:T(8,128)(2,1)}, bf16[1024,512]{1,0:T(8,128)(2,1)}, u32[]{:S(2)}, u32[]{:S(2)}) collective-permute-start(bf16[1024,512]{1,0:T(8,128)(2,1)} %get-tuple-element.30), channel_id=1, source_target_pairs={{0,4},{1,2},{2,1},{4,8},{7,3},{5,6},{6,5},{8,12},{11,7},{9,10},{10... | collective-permute-start | bytes 3145736 | tf_op jit(solution)/shard_map/ppermute | solution.py:468
  83.5 20.3 %collective-permute-start.5 = (bf16[512,512]{1,0:T(8,128)(2,1)}, bf16[512,512]{1,0:T(8,128)(2,1)S(1)}, u32[]{:S(2)}, u32[]{:S(2)}) collective-permute-start(bf16[512,512]{1,0:T(8,128)(2,1)} %get-tuple-element.31), channel_id=1, source_target_pairs={{0,4},{1,2},{2,1},{4,8},{7,3},{5,6},{6,5},{8,12},{11,7},{9,10},{10... | collective-permute-start | bytes 1572872 | tf_op jit(solution)/shard_map/ppermute | solution.py:468
  89.2 15.0 %collective-permute-start.10 = (f32[512,512]{1,0:T(8,128)}, f32[512,512]{1,0:T(8,128)}, u32[]{:S(2)}, u32[]{:S(2)}) collective-permute-start(f32[512,512]{1,0:T(8,128)} %get-tuple-element.36), channel_id=1, source_target_pairs={{0,1},{1,0},{2,3},{3,2},{4,5},{5,4},{6,7},{7,6},{8,9},{9,8},{10,11... | collective-permute-start | bytes 3145736 | tf_op jit(solution)/shard_map/ppermute | solution.py:468
  97.3 10.0 %collective-permute-start.6 = (bf16[1024,512]{1,0:T(8,128)(2,1)}, bf16[1024,512]{1,0:T(8,128)(2,1)}, u32[]{:S(2)}, u32[]{:S(2)}) collective-permute-start(bf16[1024,512]{1,0:T(8,128)(2,1)} %collective-permute-done.4.refs_0_), channel_id=1, source_target_pairs={{0,1},{1,0},{2,3},{3,2},{4,5},{5,4},{6,7},{7,6},{8,9},{9,8},{10,11... | collective-permute-start | bytes 3145736 | tf_op jit(solution)/shard_map/ppermute | solution.py:468
  103.7 3.6 %collective-permute-start.9 = (f32[512,512]{1,0:T(8,128)}, f32[512,512]{1,0:T(8,128)}, u32[]{:S(2)}, u32[]{:S(2)}) collective-permute-start(f32[512,512]{1,0:T(8,128)} %get-tuple-element.33), channel_id=1, source_target_pairs={{0,1},{1,0},{2,3},{3,2},{4,5},{5,4},{6,7},{7,6},{8,9},{9,8},{10,11... | collective-permute-start | bytes 3145736 | tf_op jit(solution)/shard_map/ppermute | solution.py:468
  103.7 3.5 %copy-start = (bf16[512,512]{1,0:T(8,128)(2,1)}, bf16[512,512]{1,0:T(8,128)(2,1)S(1)}, u32[]{:S(2)}) copy-start(bf16[512,512]{1,0:T(8,128)(2,1)S(1)} %collective-permute-done.5.refs_1_) | copy-start | bytes 1572868
  103.8 3.5 %collective-permute-start.7 = (bf16[512,512]{1,0:T(8,128)(2,1)S(1)}, bf16[512,512]{1,0:T(8,128)(2,1)}, u32[]{:S(2)}, u32[]{:S(2)}) collective-permute-start(bf16[512,512]{1,0:T(8,128)(2,1)S(1)} %collective-permute-done.5.refs_1_), channel_id=1, source_target_pairs={{0,1},{1,0},{2,3},{3,2},{4,5},{5,4},{6,7},{7,6},{8,9},{9,8},{10,11... | collective-permute-start | bytes 1572872 | tf_op jit(solution)/shard_map/ppermute | solution.py:468

commit v3 on v2

--- a/solution.py
+++ b/solution.py
@@ -9,13 +9,17 @@
 
 ROWBLK = 512
 HOPS = 3
-VMEM_LIMIT = 63 * 2**20
+VMEM_LIMIT = 28 * 2**20
+VMEM_ALL = 63 * 2**20
 LEVEL = 4
+PARTS = 4
+TURNS = (2, 1)
 HEAD = 3
-TURNS = (2, 1)
 
 SMEM = pl.BlockSpec(memory_space=pltpu.SMEM)
 HBM = pl.BlockSpec(memory_space=pltpu.HBM)
+ANY = pl.BlockSpec(memory_space=pl.ANY)
+TOKEN = jax.ShapeDtypeStruct((8, 128), jnp.float32)
 
 
 def level_route(block_total, moves):
@@ -26,6 +30,17 @@
         for place, step, new in moves
         if 0 <= z + step < levels
     ]
+
+
+def start_tile(source, target, sem):
+    rows = source.shape[0] // PARTS
+    for part in range(PARTS):
+        at = pl.ds(part * rows, rows)
+        pltpu.make_async_copy(source.at[at], target.at[at], sem).start()
+
+
+def wait_tile(tile, sem):
+    pltpu.make_async_copy(tile, tile, sem).wait()
 
 
 class Geometry:
@@ -59,14 +74,11 @@
 
         @pl.when(enable & (dist > 0))
         def _():
-            pltpu.make_async_copy(tile, up_ref.at[0, hop], sem).start()
+            start_tile(tile, up_ref.at[0, hop], sem)
 
         @pl.when(enable & (dist < 0))
         def _():
-            pltpu.make_async_copy(tile, low_ref.at[0, hop], sem).start()
-
-    def wait_tile(self, tile, up_ref, sem):
-        pltpu.make_async_copy(tile, up_ref.at[0, 0], sem).wait()
+            start_tile(tile, low_ref.at[0, hop], sem)
 
 
 def rows_at(ref, r):
@@ -85,21 +97,51 @@
     return pl.pallas_call(
         gate_kernel,
         out_shape=jax.ShapeDtypeStruct(array.shape, array.dtype),
-        in_specs=[HBM] * (1 + len(tokens)),
-        out_specs=HBM,
+        in_specs=[ANY] * (1 + len(tokens)),
+        out_specs=ANY,
         input_output_aliases={0: 0},
         compiler_params=pltpu.CompilerParams(vmem_limit_bytes=VMEM_LIMIT),
     )(array, *tokens)
 
 
-def pick_kernel(position_ref, edge_ref, inner_ref, *refs, low, sizes):
+def rows_kernel(block_ref, *refs, low):
+    out_ref, held, in_sem, out_sem = refs[-4:]
+    size = held.shape[0]
+    ins = [pltpu.make_async_copy(rows_at(block_ref, low + k), held.at[k], in_sem.at[k]) for k in range(size)]
+    outs = [pltpu.make_async_copy(held.at[k], rows_at(out_ref, k), out_sem.at[k]) for k in range(size)]
+    for copy in ins:
+        copy.start()
+    for copy, out in zip(ins, outs):
+        copy.wait()
+        out.start()
+    for out in outs:
+        out.wait()
+
+
+def rows_after(block, low, size, *tokens):
+    cols = block.shape[1]
+    return pl.pallas_call(
+        functools.partial(rows_kernel, low=low),
+        out_shape=jax.ShapeDtypeStruct((size * ROWBLK, cols), block.dtype),
+        in_specs=[HBM] + [ANY] * len(tokens),
+        out_specs=ANY,
+        scratch_shapes=[
+            pltpu.VMEM((size, ROWBLK, cols), block.dtype),
+            pltpu.SemaphoreType.DMA((size,)),
+            pltpu.SemaphoreType.DMA((size,)),
+        ],
+        compiler_params=pltpu.CompilerParams(vmem_limit_bytes=VMEM_ALL),
+    )(block, *tokens)
+
+
+def pick_kernel(position_ref, edge_ref, inner_ref, *refs, sizes):
     outs, (held, in_sem, out_sem) = refs[: len(sizes)], refs[len(sizes) :]
     place = lax.rem(position_ref[0], LEVEL)
     inner = (place == 1) | (place == 2)
-    places = [(out, k) for out, size in zip(outs, sizes) for k in range(size)]
     copies = []
-    for k, (out, at) in enumerate(places):
-        pl.when(inner)(pltpu.make_async_copy(rows_at(inner_ref, low + k), held.at[k], in_sem.at[k]).start)
+    for out, at in [(out, at) for out, size in zip(outs, sizes) for at in range(size)]:
+        k = len(copies)
+        pl.when(inner)(pltpu.make_async_copy(rows_at(inner_ref, k), held.at[k], in_sem.at[k]).start)
         pl.when(jnp.logical_not(inner))(pltpu.make_async_copy(rows_at(edge_ref, k), held.at[k], in_sem.at[k]).start)
         copies.append(pltpu.make_async_copy(held.at[k], rows_at(out, at), out_sem.at[k]))
     for k, copy in enumerate(copies):
@@ -109,18 +151,18 @@
         copy.wait()
 
 
-def pick(position, edge, inner, low, sizes, *tokens):
+def pick(position, edge, inner, sizes, *tokens):
     rows, cols = edge.shape
     total = rows // ROWBLK
 
     def body(position_ref, edge_ref, inner_ref, *refs):
-        pick_kernel(position_ref, edge_ref, inner_ref, *refs[len(tokens) :], low=low, sizes=sizes)
+        pick_kernel(position_ref, edge_ref, inner_ref, *refs[len(tokens) :], sizes=sizes)
 
     return pl.pallas_call(
         body,
         out_shape=tuple(jax.ShapeDtypeStruct((size * ROWBLK, cols), edge.dtype) for size in sizes),
-        in_specs=[SMEM] + [HBM] * (2 + len(tokens)),
-        out_specs=(HBM,) * len(sizes),
+        in_specs=[SMEM] + [ANY] * (2 + len(tokens)),
+        out_specs=(ANY,) * len(sizes),
         scratch_shapes=[
             pltpu.VMEM((total, ROWBLK, cols), edge.dtype),
             pltpu.SemaphoreType.DMA((total,)),
@@ -152,14 +194,13 @@
         turned_copy(r).start()
         dot_into(tile, own_t[r], own[r])
 
-    out_copy = pltpu.make_async_copy(tile, diag_ref.at[0], out_sem.at[0])
-    out_copy.start()
+    start_tile(tile, diag_ref.at[0], out_sem.at[0])
 
     @pl.loop(0, count)
     def _(r):
         turned_copy(r).wait()
 
-    out_copy.wait()
+    wait_tile(tile, out_sem.at[0])
 
 
 def own_tile(scalars, own, block_total):
@@ -171,8 +212,8 @@
             jax.ShapeDtypeStruct((1, cols, cols), jnp.float32),
             jax.ShapeDtypeStruct((steps, cols, ROWBLK), own.dtype),
         ),
-        in_specs=[SMEM] * 3 + [HBM],
-        out_specs=(HBM,) * 2,
+        in_specs=[SMEM] * 3 + [ANY],
+        out_specs=(ANY,) * 2,
         scratch_shapes=[
             pltpu.VMEM((steps, ROWBLK, cols), own.dtype),
             pltpu.VMEM((steps, cols, ROWBLK), own.dtype),
@@ -189,7 +230,7 @@
 
 
 def core_kernel(
-    position_ref, live_ref, sig_ref, core_ref, own_t_ref, up_ref, low_ref, core_t_ref, own_t, core, core_t, tile, sems,
+    position_ref, live_ref, sig_ref, core_ref, own_t_ref, up_ref, low_ref, core_t_ref, _token, own_t, core, core_t, tile, sems,
     turned_sem, out_sem, *, block_total,
 ):
     steps = core.shape[0]
@@ -228,7 +269,7 @@
     def _(r):
         turned_copy(r).wait()
 
-    geo.wait_tile(tile, up_ref, out_sem.at[0])
+    wait_tile(tile, out_sem.at[0])
 
 
 def core_tile(scalars, core, own_t, block_total):
@@ -237,9 +278,9 @@
     three = jax.ShapeDtypeStruct((1, HOPS, cols, cols), jnp.float32)
     return pl.pallas_call(
         functools.partial(core_kernel, block_total=block_total),
-        out_shape=(three, three, jax.ShapeDtypeStruct(own_t.shape, own_t.dtype)),
-        in_specs=[SMEM] * 3 + [HBM] * 2,
-        out_specs=(HBM,) * 3,
+        out_shape=(three, three, jax.ShapeDtypeStruct(own_t.shape, own_t.dtype), TOKEN),
+        in_specs=[SMEM] * 3 + [ANY] * 2,
+        out_specs=(ANY,) * 4,
         scratch_shapes=[
             pltpu.VMEM((steps, cols, ROWBLK), core.dtype),
             pltpu.VMEM((steps, ROWBLK, cols), core.dtype),
@@ -278,11 +319,10 @@
         pl.when(r < either)(held_copy.start)
 
     if before:
-        loads = [pltpu.make_async_copy(before[i], tiles.at[i], before_sem.at[i]) for i in range(2)]
-        for load in loads:
-            load.start()
-        for load in loads:
-            load.wait()
+        for i in range(2):
+            start_tile(before[i], tiles.at[i], before_sem.at[i])
+        for i in range(2):
+            wait_tile(tiles.at[i], before_sem.at[i])
     else:
         tiles[...] = jnp.zeros_like(tiles)
 
@@ -306,17 +346,15 @@
                 dot_into(tiles.at[1], core_t[at], held[at])
 
     if shared:
-        swap_copy = pltpu.make_async_copy(tiles.at[1], outs[-1], out_sem.at[1])
-        swap_copy.start()
+        start_tile(tiles.at[1], outs[-1], out_sem.at[1])
     if final:
         geo.place_tile(tiles.at[0], other, outs[0], outs[1], out_sem.at[0])
-        geo.wait_tile(tiles.at[0], outs[0], out_sem.at[0])
+        wait_tile(tiles.at[0], out_sem.at[0])
     else:
-        own_out = pltpu.make_async_copy(tiles.at[0], outs[0], out_sem.at[0])
-        own_out.start()
-        own_out.wait()
+        start_tile(tiles.at[0], outs[0], out_sem.at[0])
+        wait_tile(tiles.at[0], out_sem.at[0])
     if shared:
-        swap_copy.wait()
+        wait_tile(tiles.at[1], out_sem.at[1])
 
 
 def pair_tiles(scalars, turned, which, pieces, low, high, before, outputs, block_total):
@@ -333,16 +371,16 @@
         outs_at = n_in + n_before + len(chained)
         pair_kernel(
             position_ref, live_ref, sig_ref, own_t_ref, core_t_ref, refs[:n_in], refs[n_in : n_in + n_before],
-            refs[outs_at : outs_at + n_out], *refs[outs_at + n_out :],
+            refs[outs_at : outs_at + n_out], *refs[outs_at + n_out + 1 :],
             which=which, low=low, high=high, sources=sources, final=final, block_total=block_total,
         )
 
     span = high - low
     return pl.pallas_call(
         body,
-        out_shape=tuple(jax.ShapeDtypeStruct(c.shape, c.dtype) for c in chained) + (tile,) * (n_out - len(chained)),
-        in_specs=[SMEM] * 3 + [HBM] * (2 + n_in + n_before + len(chained)),
-        out_specs=(HBM,) * n_out,
+        out_shape=tuple(jax.ShapeDtypeStruct(c.shape, c.dtype) for c in chained) + (tile,) * (n_out - len(chained)) + (TOKEN,),
+        in_specs=[SMEM] * 3 + [ANY] * (2 + n_in + n_before + len(chained)),
+        out_specs=(ANY,) * (n_out + 1),
         scratch_shapes=[pltpu.VMEM((span, cols, ROWBLK), turned[0].dtype)] * 2
         + [
             pltpu.VMEM((span, ROWBLK, cols), turned[0].dtype),
@@ -361,101 +399,82 @@
     )(*scalars, *turned, *pieces, *before, *chained)
 
 
-def place_kernel(position_ref, live_ref, sig_ref, tile_ref, _up, _low, up_ref, low_ref, tile, in_sem, out_sem, *, block_total):
-    geo = Geometry(position_ref, live_ref, sig_ref, block_total)
-    copy = pltpu.make_async_copy(tile_ref, tile, in_sem.at[0])
-    copy.start()
-    copy.wait()
-    geo.place_tile(tile, geo.both, up_ref, low_ref, out_sem.at[0])
-    geo.wait_tile(tile, up_ref, out_sem.at[0])
-
-
-def place_both(scalars, tile, outputs, block_total):
-    return pl.pallas_call(
-        functools.partial(place_kernel, block_total=block_total),
-        out_shape=tuple(jax.ShapeDtypeStruct(o.shape, o.dtype) for o in outputs),
-        in_specs=[SMEM] * 3 + [HBM] * 3,
-        out_specs=(HBM,) * 2,
-        scratch_shapes=[
-            pltpu.VMEM(tile.shape, jnp.float32),
-            pltpu.SemaphoreType.DMA((1,)),
-            pltpu.SemaphoreType.DMA((1,)),
-        ],
-        input_output_aliases={4: 0, 5: 1},
-        compiler_params=pltpu.CompilerParams(vmem_limit_bytes=VMEM_LIMIT),
-    )(*scalars, tile, *outputs)
-
-
 def end_kernel(
-    position_ref, live_ref, sig_ref, own_t_ref, piece_refs, before, outs, own_t, held, tiles, sems, own_sem, before_sem,
-    out_sem, *, low, sources, block_total,
+    position_ref, live_ref, sig_ref, own_t_ref, pieces, before, up_ref, low_ref, _token, own_t, held, tiles, own_sem, held_sem,
+    before_sem, out_sem, *, names, low, block_total,
 ):
     span = own_t.shape[0]
     geo = Geometry(position_ref, live_ref, sig_ref, block_total)
-    others = (geo.relay, geo.last)
-    counts = [geo.count(geo.me, other) for other in others]
-    either = jnp.maximum(*counts)
+    others = [getattr(geo, name) for name in names]
+    counts = [geo.count(geo.me, other) - low for other in others]
+    either = functools.reduce(jnp.maximum, counts)
 
     def own_copy(at):
         return pltpu.make_async_copy(own_t_ref.at[low + at], own_t.at[at], own_sem.at[at])
 
-    loads = [pltpu.make_async_copy(before[i], tiles.at[i], before_sem.at[i]) for i in range(2)]
+    def held_copy(rows, i, at):
+        return pltpu.make_async_copy(rows, held.at[i, at], held_sem.at[i, at])
+
+    for i in range(len(names)):
+        start_tile(before[i], tiles.at[i], before_sem.at[i])
+        for at in range(span):
+            if i == 0:
+                pl.when(at < either)(own_copy(at).start)
+            pl.when(at < counts[i])(held_copy(pieces[i][at], i, at).start)
     for at in range(span):
-        pl.when(low + at < either)(own_copy(at).start)
-    for i in range(2):
-        loads[i].start()
-        for at in range(span):
-            ref, offset = sources[i][at]
-            held_copy = pltpu.make_async_copy(rows_at(piece_refs[ref], offset), held.at[i, at], sems.at[i, at])
-            pl.when(low + at < counts[i])(held_copy.start)
-    for at in range(span):
-        pl.when(low + at < either)(own_copy(at).wait)
-    for i in range(2):
-        loads[i].wait()
-
-        @pl.loop(0, jnp.maximum(counts[i] - low, 0))
+        pl.when(at < either)(own_copy(at).wait)
+    for i in range(len(names)):
+        wait_tile(tiles.at[i], before_sem.at[i])
+
+        @pl.loop(0, jnp.maximum(counts[i], 0))
         def _(at):
-            pltpu.make_async_copy(rows_at(piece_refs[0], 0), held.at[i, at], sems.at[i, at]).wait()
+            held_copy(pieces[i][0], i, at).wait()
             dot_into(tiles.at[i], own_t[at], held[i, at])
 
-        geo.place_tile(tiles.at[i], others[i], outs[0], outs[1], out_sem.at[i])
-    for i in range(2):
-        geo.wait_tile(tiles.at[i], outs[0], out_sem.at[i])
-
-
-def end_tiles(scalars, own_t, pieces, swapped, low, before, outputs, block_total):
+        geo.place_tile(tiles.at[i], others[i], up_ref, low_ref, out_sem.at[i])
+    for i in range(len(names)):
+        wait_tile(tiles.at[i], out_sem.at[i])
+
+
+def end_tiles(scalars, own_t, jobs, low, outputs, block_total):
     steps, cols, _ = own_t.shape
-    span = steps - low
-    arrays = [*pieces, *swapped]
-    sources = [
-        [(i + first, k) for i, piece in enumerate(group) for k in range(piece.shape[0] // ROWBLK)]
-        for first, group in ((0, pieces), (len(pieces), swapped))
-    ]
-    n_in = len(arrays)
+    span, n = steps - low, len(jobs)
+    names = [job[0] for job in jobs]
+    pieces = [piece for job in jobs for piece in job[1]]
+    before = [job[2] for job in jobs]
+    places = [(p, k) for p, piece in enumerate(pieces) for k in range(piece.shape[0] // ROWBLK)]
+    n_in = len(pieces)
 
     def body(position_ref, live_ref, sig_ref, own_t_ref, *refs):
+        rows = [rows_at(refs[p], k) for p, k in places]
         end_kernel(
-            position_ref, live_ref, sig_ref, own_t_ref, refs[:n_in], refs[n_in : n_in + 2], refs[n_in + 4 : n_in + 6],
-            *refs[n_in + 6 :], low=low, sources=sources, block_total=block_total,
+            position_ref, live_ref, sig_ref, own_t_ref, [rows[i * span : (i + 1) * span] for i in range(n)],
+            refs[n_in : n_in + n], *refs[n_in + n + 2 :],
+            names=names, low=low, block_total=block_total,
         )
 
     return pl.pallas_call(
         body,
-        out_shape=tuple(jax.ShapeDtypeStruct(o.shape, o.dtype) for o in outputs),
-        in_specs=[SMEM] * 3 + [HBM] * (5 + n_in),
-        out_specs=(HBM,) * 2,
+        out_shape=(*(jax.ShapeDtypeStruct(o.shape, o.dtype) for o in outputs), TOKEN),
+        in_specs=[SMEM] * 3 + [ANY] * (3 + n_in + n),
+        out_specs=(ANY,) * 3,
         scratch_shapes=[
             pltpu.VMEM((span, cols, ROWBLK), own_t.dtype),
-            pltpu.VMEM((2, span, ROWBLK, cols), own_t.dtype),
-            pltpu.VMEM((2, cols, cols), jnp.float32),
-            pltpu.SemaphoreType.DMA((2, span)),
+            pltpu.VMEM((n, span, ROWBLK, cols), own_t.dtype),
+            pltpu.VMEM((n, cols, cols), jnp.float32),
             pltpu.SemaphoreType.DMA((span,)),
-            pltpu.SemaphoreType.DMA((2,)),
-            pltpu.SemaphoreType.DMA((2,)),
+            pltpu.SemaphoreType.DMA((n, span)),
+            pltpu.SemaphoreType.DMA((n,)),
+            pltpu.SemaphoreType.DMA((n,)),
         ],
-        input_output_aliases={6 + n_in: 0, 7 + n_in: 1},
+        input_output_aliases={4 + n_in + n: 0, 5 + n_in + n: 1},
         compiler_params=pltpu.CompilerParams(vmem_limit_bytes=VMEM_LIMIT),
-    )(*scalars, own_t, *arrays, *before, *outputs)
+        cost_estimate=pl.CostEstimate(
+            flops=2 * n * span * ROWBLK * cols * cols,
+            bytes_accessed=2 * (n + 1) * span * ROWBLK * cols + 8 * n * cols * cols,
+            transcendentals=0,
+        ),
+    )(*scalars, own_t, *pieces, *before, *outputs)
 
 
 def per_device(b_half, significant, live_rows):
@@ -473,29 +492,38 @@
     relay = [(0, 1, 0), (1, 1, 1), (2, -1, 2), (3, -1, 3)]
     turn = [(0, 1, 0), (3, -1, 3), (1, 0, 2), (2, 0, 1)]
 
-    y_head = send(b_half[: HEAD * ROWBLK], across)
-    y_tail = send(b_half[HEAD * ROWBLK :], across)
+    head = rows_after(b_half, 0, HEAD)
+    y_head = send(head, across)
+    tail = rows_after(b_half, HEAD, steps - HEAD, head)
+    y_tail = send(tail, across)
+    far_head, far_tail = send(head, far), send(tail, far)
     core = send(b_half, cores)
-    far_block = send(b_half, far)
 
     diagonal, own_t = own_tile(scalars, b_half, block_total)
-    upper, lower, core_t = core_tile(scalars, core, own_t, block_total)
+    upper, lower, core_t, made_core = core_tile(scalars, core, own_t, block_total)
     turned = (own_t, core_t)
-    y_head = after(y_head, core_t)
+    y_head = after(y_head, made_core)
     relayed = send(y_head, relay)
-    upper, lower = pair_tiles(scalars, turned, "far", [far_block], 0, steps, None, (upper, lower), block_total)
-    y_partial = pair_tiles(scalars, turned, "across", [y_head], 0, HEAD, None, None, block_total)
-
-    turns = [send(piece, turn) for piece in pick(position, y_tail, far_block, HEAD, TURNS, upper, y_partial[0])]
-    own_part, core_part = pair_tiles(scalars, turned, "relay", [relayed], 0, HEAD, None, None, block_total)
-    upper, lower, both = pair_tiles(
-        scalars, turned, "across", [y_tail], HEAD, steps, y_partial, (upper, lower), block_total
+    y_part, both_part, made_y = pair_tiles(scalars, turned, "across", [y_head], 0, HEAD, None, None, block_total)
+    both_part = send(both_part, cores)
+    upper, lower, made_far = pair_tiles(
+        scalars, turned, "far", [far_head, far_tail], 0, steps, None, (upper, lower), block_total
     )
-    upper, lower = place_both(scalars, send(both, cores), (upper, lower), block_total)
-    swapped = [send(piece, cores) for piece in turns]
-    upper, lower = end_tiles(
-        scalars, own_t, turns, swapped, HEAD, (own_part, send(core_part, cores)), (upper, lower), block_total
+
+    y_tail = after(y_tail, made_y, made_far)
+    relay_tail = [send(piece, turn) for piece in pick(position, y_tail, far_tail, TURNS)]
+    both_tail = send(y_tail, cores)
+    relay_part, last_part, made_relay = pair_tiles(
+        scalars, turned, "relay", [relayed], 0, HEAD, None, None, block_total
     )
+    last_part = send(last_part, cores)
+    jobs = [("across", [y_tail], y_part), ("both", [both_tail], both_part)]
+    upper, lower, made_across = end_tiles(scalars, own_t, jobs, HEAD, (upper, lower), block_total)
+
+    relay_tail[0] = after(relay_tail[0], made_across, made_relay)
+    last_tail = [send(piece, cores) for piece in relay_tail]
+    jobs = [("relay", relay_tail, relay_part), ("last", last_tail, last_part)]
+    upper, lower, _ = end_tiles(scalars, own_t, jobs, HEAD, (upper, lower), block_total)
     return diagonal, upper, lower
 
 

time: 113 us -> 103 us (0.912)
  the two profiles are of different devices: /device:TPU:16 before, /device:TPU:5 now
where the time goes in v3:
time: 103 us; the launch traced here: 101 us
  waiting for transfers between devices  53.4 us (52%)
  Pallas kernels  30.7 us (30%)
  starting transfers between devices  14.1 us (14%)
  local copies, waits for them, and re-layouts  1.99 us (2%)
    ppermute x13, waiting for transfers between devices, send(): return lax.ppermute(block, 'ao', level_route(block_total, moves))  53.4 us
    ppermute x13, starting transfers between devices, send(): return lax.ppermute(block, 'ao', level_route(block_total, moves))  14.1 us
    pallas_call x3, Pallas kernels, pair_tiles(): pl.pallas_call(body, out_shape=tuple((jax.ShapeDtypeStruct(c.shape, c.dty...  10.8 us
    pallas_call x1, Pallas kernels, own_tile(): pl.pallas_call(functools.partial(own_kernel, block_total=block_total), ou...  6.04 us
    pallas_call x2, Pallas kernels, end_tiles(): pl.pallas_call(body, out_shape=(*(jax.ShapeDtypeStruct(o.shape, o.dtype)...  4.86 us
    pallas_call x2, Pallas kernels, rows_after(): pl.pallas_call(functools.partial(rows_kernel, low=low), out_shape=jax.Sha...  4.53 us
    pallas_call x1, Pallas kernels, core_tile(): pl.pallas_call(functools.partial(core_kernel, block_total=block_total), o...  4.2 us
  transfers between devices with their start and end apart: 13, of which 6 were waited for; matrix products, arithmetic and copies ran while one was open for 0% of the time, Pallas kernels for 28%

profile of v3, /device:TPU:5, one launch (start us, length us, event | category | flops | bytes accessed | tf_op | source)
XLA Modules:
  0.0 101.0 jit_solution(16693798557843488675)
XLA Ops:
  0.6 0.7 collective-permute-start.1
  1.4 2.3 %shard_map.59.refs_0_ = bf16[1536,512]{1,0:T(8,128)(2,1)} custom-call(bf16[3072,512]{1,0:T(8,128)(2,1)} %block_ref.3), custom_call_target="tpu_custom_call" | custom-call | tf_op jit(solution)/shard_map/pallas_call | solution.py:123
  3.6 0.0 copy-start.2
  3.6 0.0 copy-start.1
  3.7 0.1 collective-permute-start.2
  3.7 2.3 %shard_map.60 = bf16[1536,512]{1,0:T(8,128)(2,1)} custom-call(bf16[3072,512]{1,0:T(8,128)(2,1)} %block_ref.3, bf16[1536,512]{1,0:T(8,128)(2,1)} %shard_map.59.refs_0_), custom_call_target="tpu_custom_call" | custom-call | tf_op jit(solution)/shard_map/pallas_call | solution.py:123
  6.0 3.6 %collective-permute-start.4 = (bf16[1536,512]{1,0:T(8,128)(2,1)}, bf16[1536,512]{1,0:T(8,128)(2,1)S(1)}, u32[]{:S(2)}, u32[]{:S(2)}) collective-permute-start(bf16[1536,512]{1,0:T(8,128)(2,1)} %shard_map.60), channel_id=1, source_target_pairs={{1,4},{3,6},{5,8},{4,1},{7,10},{6,3},{9,12},{8,5},{11,14},{10,7},{... | collective-permute-start | bytes 4718600 | tf_op jit(solution)/shard_map/ppermute | solution.py:487
  9.6 2.0 %collective-permute-start.3 = (bf16[1536,512]{1,0:T(8,128)(2,1)}, bf16[1536,512]{1,0:T(8,128)(2,1)}, u32[]{:S(2)}, u32[]{:S(2)}) collective-permute-start(bf16[1536,512]{1,0:T(8,128)(2,1)} %shard_map.59.refs_0_), channel_id=1, source_target_pairs={{1,4},{3,6},{5,8},{4,1},{7,10},{6,3},{9,12},{8,5},{11,14},{10,7},{... | collective-permute-start | bytes 4718600 | tf_op jit(solution)/shard_map/ppermute | solution.py:487
  11.6 1.5 %collective-permute-start = (bf16[1536,512]{1,0:T(8,128)(2,1)}, bf16[1536,512]{1,0:T(8,128)(2,1)S(1)}, u32[]{:S(2)}, u32[]{:S(2)}) collective-permute-start(bf16[1536,512]{1,0:T(8,128)(2,1)} %shard_map.60), channel_id=1, source_target_pairs={{0,2},{1,3},{2,0},{3,1},{4,6},{5,7},{6,4},{7,5},{8,10},{9,11},{10,... | collective-permute-start | bytes 4718600 | tf_op jit(solution)/shard_map/ppermute | solution.py:487
  13.1 0.0 copy-done.2
  13.1 0.1 copy.15.sig_ref
  13.2 0.0 copy-done.1
  13.2 0.0 copy-start
  13.2 1.9 %copy-done = bf16[3072,512]{1,0:T(8,128)(2,1)S(1)} copy-done((bf16[3072,512]{1,0:T(8,128)(2,1)S(1)}, bf16[3072,512]{1,0:T(8,128)(2,1)}, u32[]{:S(2)}) %copy-start) | copy-done | bytes 3145752
  15.1 6.0 %shard_map.58 = (f32[1,512,512]{2,1,0:T(8,128)}, bf16[6,512,512]{2,1,0:T(8,128)(2,1)S(1)}) custom-call(s32[1]{0:T(128)} %bitcast.position_ref, s32[16]{0:T(128)S(1)} %copy-done.1, s32[16,3]{1,0:T(8,128)S(1)} %copy.15.sig_ref, bf16[3072,512]{1,0:T(8,128)(2,1)S(1)} %copy-done), custom_call_target="tpu_custom_call" | custom-call | flops 1610612736 | bytes 7340032 | tf_op jit(solution)/shard_map/pallas_call | solution.py:209
  21.1 0.0 collective-permute-done.1.core_ref
  21.1 4.2 %shard_map.61 = (f32[1,3,512,512]{3,2,1,0:T(8,128)}, f32[1,3,512,512]{3,2,1,0:T(8,128)}, bf16[6,512,512]{2,1,0:T(8,128)(2,1)S(1)}, f32[8,128]{1,0:T(8,128)S(1)}) custom-call(s32[1]{0:T(128)} %bitcast.position_ref, s32[16]{0:T(128)S(1)} %copy-done.1, s32[16,3]{1,0:T(8,128)S(1)} %copy.15.sig_ref, bf16[3072,512]{1,0:T(8,128)(2,1)} %collective-permute-done.1.core_ref, ...), custom_call_target="tpu_custom_call" | custom-call | flops 1610612736 | bytes 10485760 | tf_op jit(solution)/shard_map/pallas_call | solution.py:279
  25.4 14.7 %collective-permute-done.2.refs_0_ = bf16[1536,512]{1,0:T(8,128)(2,1)} collective-permute-done((bf16[1536,512]{1,0:T(8,128)(2,1)}, bf16[1536,512]{1,0:T(8,128)(2,1)}, u32[]{:S(2)}, u32[]{:S(2)}) %collective-permute-start.2) | collective-permute-done | bytes 1572896 | tf_op jit(solution)/shard_map/ppermute | solution.py:487
  40.0 1.3 %collective-permute-start.8 = (bf16[1536,512]{1,0:T(8,128)(2,1)}, bf16[1536,512]{1,0:T(8,128)(2,1)S(1)}, u32[]{:S(2)}, u32[]{:S(2)}) collective-permute-start(bf16[1536,512]{1,0:T(8,128)(2,1)} %shard_map.62.refs_0_), channel_id=1, source_target_pairs={{0,4},{1,5},{4,8},{5,9},{6,2},{7,3},{8,12},{9,13},{10,6},{11,7},{1... | collective-permute-start | bytes 4718600 | tf_op jit(solution)/shard_map/ppermute | solution.py:487
  41.3 0.0 collective-permute-done.4.refs_1_.inner_ref
  41.3 4.0 %collective-permute-done.3.refs_0_ = bf16[1536,512]{1,0:T(8,128)(2,1)} collective-permute-done((bf16[1536,512]{1,0:T(8,128)(2,1)}, bf16[1536,512]{1,0:T(8,128)(2,1)}, u32[]{:S(2)}, u32[]{:S(2)}) %collective-permute-start.3) | collective-permute-done | bytes 1572896 | tf_op jit(solution)/shard_map/ppermute | solution.py:487
  45.3 5.6 %shard_map.64 = (f32[1,3,512,512]{3,2,1,0:T(8,128)}, f32[1,3,512,512]{3,2,1,0:T(8,128)}, f32[8,128]{1,0:T(8,128)S(1)}) custom-call(s32[1]{0:T(128)} %bitcast.position_ref, s32[16]{0:T(128)S(1)} %copy-done.1, s32[16,3]{1,0:T(8,128)S(1)} %copy.15.sig_ref, ...), custom_call_target="tpu_custom_call", output_to_operand_aliasing={{0}: (7, {}), {1}: (8, {})} | custom-call | flops 3221225472 | bytes 13631488 | tf_op jit(solution)/shard_map/pallas_call | solution.py:379
  50.9 3.0 %shard_map.63 = (f32[512,512]{1,0:T(8,128)S(1)}, f32[512,512]{1,0:T(8,128)S(1)}, f32[8,128]{1,0:T(8,128)S(1)}) custom-call(s32[1]{0:T(128)} %bitcast.position_ref, s32[16]{0:T(128)S(1)} %copy-done.1, s32[16,3]{1,0:T(8,128)S(1)} %copy.15.sig_ref, bf16[6,512,512]{2,1,0:T(8,128)(2,1)S(1)} %get-tuple-element.26.own_t_ref, ...), custom_call_target="tpu_custom_call" | custom-call | flops 1610612736 | bytes 8912896 | tf_op jit(solution)/shard_map/pallas_call | solution.py:379
  53.9 19.8 %collective-permute-done.refs_0_ = bf16[1536,512]{1,0:T(8,128)(2,1)S(1)} collective-permute-done((bf16[1536,512]{1,0:T(8,128)(2,1)}, bf16[1536,512]{1,0:T(8,128)(2,1)S(1)}, u32[]{:S(2)}, u32[]{:S(2)}) %collective-permute-start) | collective-permute-done | bytes 1572896 | tf_op jit(solution)/shard_map/ppermute | solution.py:487
  73.6 0.8 collective-permute-start.6
  74.5 0.0 collective-permute-start.7
  74.5 0.3 shard_map.66
  74.7 1.3 %collective-permute-start.5 = (bf16[1024,512]{1,0:T(8,128)(2,1)S(1)}, bf16[1024,512]{1,0:T(8,128)(2,1)S(1)}, u32[]{:S(2)}, u32[]{:S(2)}) collective-permute-start(bf16[1024,512]{1,0:T(8,128)(2,1)S(1)} %get-tuple-element.33), channel_id=1, source_target_pairs={{0,4},{1,2},{2,1},{4,8},{7,3},{5,6},{6,5},{8,12},{11,7},{9,10},{10... | collective-permute-start | bytes 3145736 | tf_op jit(solution)/shard_map/ppermute | solution.py:487
  76.0 1.3 %collective-permute-start.9 = (bf16[512,512]{1,0:T(8,128)(2,1)S(1)}, bf16[512,512]{1,0:T(8,128)(2,1)S(1)}, u32[]{:S(2)}, u32[]{:S(2)}) collective-permute-start(bf16[512,512]{1,0:T(8,128)(2,1)S(1)} %get-tuple-element.40), channel_id=1, source_target_pairs={{0,4},{1,2},{2,1},{4,8},{7,3},{5,6},{6,5},{8,12},{11,7},{9,10},{10... | collective-permute-start | bytes 1572872 | tf_op jit(solution)/shard_map/ppermute | solution.py:487
  77.3 0.0 collective-permute-done.8.refs_0_
  77.4 2.2 %shard_map.68 = (f32[512,512]{1,0:T(8,128)S(1)}, f32[512,512]{1,0:T(8,128)S(1)}, f32[8,128]{1,0:T(8,128)S(1)}) custom-call(s32[1]{0:T(128)} %bitcast.position_ref, s32[16]{0:T(128)S(1)} %copy-done.1, s32[16,3]{1,0:T(8,128)S(1)} %copy.15.sig_ref, bf16[6,512,512]{2,1,0:T(8,128)(2,1)S(1)} %get-tuple-element.26.own_t_ref, ...), custom_call_target="tpu_custom_call" | custom-call | flops 1610612736 | bytes 8912896 | tf_op jit(solution)/shard_map/pallas_call | solution.py:379
  79.6 0.0 collective-permute-done.7.refs_3_
  79.6 0.0 collective-permute-done.6.refs_1_
  79.6 2.3 %shard_map.67 = (f32[1,3,512,512]{3,2,1,0:T(8,128)}, f32[1,3,512,512]{3,2,1,0:T(8,128)}, f32[8,128]{1,0:T(8,128)S(1)}) custom-call(s32[1]{0:T(128)} %bitcast.position_ref, s32[16]{0:T(128)S(1)} %copy-done.1, s32[16,3]{1,0:T(8,128)S(1)} %copy.15.sig_ref, ...), custom_call_target="tpu_custom_call", output_to_operand_aliasing={{0}: (8, {}), {1}: (9, {})} | custom-call | flops 1610612736 | bytes 8912896 | tf_op jit(solution)/shard_map/pallas_call | solution.py:456
  81.9 8.6 %collective-permute-done.5.refs_0_ = bf16[1024,512]{1,0:T(8,128)(2,1)S(1)} collective-permute-done((bf16[1024,512]{1,0:T(8,128)(2,1)S(1)}, bf16[1024,512]{1,0:T(8,128)(2,1)S(1)}, u32[]{:S(2)}, u32[]{:S(2)}) %collective-permute-start.5) | collective-permute-done | bytes 1048608 | tf_op jit(solution)/shard_map/ppermute | solution.py:487
  90.6 0.8 collective-permute-start.10
  91.4 0.0 collective-permute-start.12
  91.4 4.8 %collective-permute-done.9.refs_1_ = bf16[512,512]{1,0:T(8,128)(2,1)S(1)} collective-permute-done((bf16[512,512]{1,0:T(8,128)(2,1)S(1)}, bf16[512,512]{1,0:T(8,128)(2,1)S(1)}, u32[]{:S(2)}, u32[]{:S(2)}) %collective-permute-start.9) | collective-permute-done | bytes 524320 | tf_op jit(solution)/shard_map/ppermute | solution.py:487
  96.2 0.8 collective-permute-start.11
  97.0 1.5 %collective-permute-done.11.refs_3_ = bf16[512,512]{1,0:T(8,128)(2,1)S(1)} collective-permute-done((bf16[512,512]{1,0:T(8,128)(2,1)S(1)}, bf16[512,512]{1,0:T(8,128)(2,1)S(1)}, u32[]{:S(2)}, u32[]{:S(2)}) %collective-permute-start.11) | collective-permute-done | bytes 524320 | tf_op jit(solution)/shard_map/ppermute | solution.py:487
  98.5 0.0 collective-permute-done.10.refs_2_
  98.5 0.0 collective-permute-done.12.refs_5_
  98.5 2.5 %shard_map.70 = (f32[1,3,512,512]{3,2,1,0:T(8,128)}, f32[1,3,512,512]{3,2,1,0:T(8,128)}, f32[8,128]{1,0:T(8,128)}) custom-call(s32[1]{0:T(128)} %bitcast.position_ref, s32[16]{0:T(128)S(1)} %copy-done.1, s32[16,3]{1,0:T(8,128)S(1)} %copy.15.sig_ref, ...), custom_call_target="tpu_custom_call", output_to_operand_aliasing={{0}: (10, {}), {1}: (11, {})} | custom-call | flops 1610612736 | bytes 8912896 | tf_op jit(solution)/shard_map/pallas_call | solution.py:456
  (3 shorter events, 0.0 us)
Async XLA Ops:
  0.6 20.5 %collective-permute-start.1 = (bf16[3072,512]{1,0:T(8,128)(2,1)}, bf16[3072,512]{1,0:T(8,128)(2,1)}, u32[]{:S(2)}, u32[]{:S(2)}) collective-permute-start(bf16[3072,512]{1,0:T(8,128)(2,1)} %block_ref.3), channel_id=1, source_target_pairs={{0,1},{1,0},{2,3},{3,2},{4,5},{5,4},{6,7},{7,6},{8,9},{9,8},{10,11... | collective-permute-start | bytes 9437192 | tf_op jit(solution)/shard_map/ppermute | solution.py:487
  3.6 9.5 %copy-start.2 = (s32[16,3]{0,1:T(4,128)S(1)}, s32[16,3]{0,1:T(4,128)}, u32[]{:S(2)}) copy-start(s32[16,3]{0,1:T(4,128)} %param.4) | copy-start | bytes 580
  3.6 9.6 %copy-start.1 = (s32[16]{0:T(128)S(1)}, s32[16]{0:T(128)}, u32[]{:S(2)}) copy-start(s32[16]{0:T(128)} %live_ref.13) | copy-start | bytes 196
  3.7 36.4 %collective-permute-start.2 = (bf16[1536,512]{1,0:T(8,128)(2,1)}, bf16[1536,512]{1,0:T(8,128)(2,1)}, u32[]{:S(2)}, u32[]{:S(2)}) collective-permute-start(bf16[1536,512]{1,0:T(8,128)(2,1)} %shard_map.59.refs_0_), channel_id=1, source_target_pairs={{0,2},{1,3},{2,0},{3,1},{4,6},{5,7},{6,4},{7,5},{8,10},{9,11},{10,... | collective-permute-start | bytes 4718600 | tf_op jit(solution)/shard_map/ppermute | solution.py:487
  6.0 35.3 %collective-permute-start.4 = (bf16[1536,512]{1,0:T(8,128)(2,1)}, bf16[1536,512]{1,0:T(8,128)(2,1)S(1)}, u32[]{:S(2)}, u32[]{:S(2)}) collective-permute-start(bf16[1536,512]{1,0:T(8,128)(2,1)} %shard_map.60), channel_id=1, source_target_pairs={{1,4},{3,6},{5,8},{4,1},{7,10},{6,3},{9,12},{8,5},{11,14},{10,7},{... | collective-permute-start | bytes 4718600 | tf_op jit(solution)/shard_map/ppermute | solution.py:487
  9.6 35.7 %collective-permute-start.3 = (bf16[1536,512]{1,0:T(8,128)(2,1)}, bf16[1536,512]{1,0:T(8,128)(2,1)}, u32[]{:S(2)}, u32[]{:S(2)}) collective-permute-start(bf16[1536,512]{1,0:T(8,128)(2,1)} %shard_map.59.refs_0_), channel_id=1, source_target_pairs={{1,4},{3,6},{5,8},{4,1},{7,10},{6,3},{9,12},{8,5},{11,14},{10,7},{... | collective-permute-start | bytes 4718600 | tf_op jit(solution)/shard_map/ppermute | solution.py:487
  11.6 62.0 %collective-permute-start = (bf16[1536,512]{1,0:T(8,128)(2,1)}, bf16[1536,512]{1,0:T(8,128)(2,1)S(1)}, u32[]{:S(2)}, u32[]{:S(2)}) collective-permute-start(bf16[1536,512]{1,0:T(8,128)(2,1)} %shard_map.60), channel_id=1, source_target_pairs={{0,2},{1,3},{2,0},{3,1},{4,6},{5,7},{6,4},{7,5},{8,10},{9,11},{10,... | collective-permute-start | bytes 4718600 | tf_op jit(solution)/shard_map/ppermute | solution.py:487
  13.2 1.9 %copy-start = (bf16[3072,512]{1,0:T(8,128)(2,1)S(1)}, bf16[3072,512]{1,0:T(8,128)(2,1)}, u32[]{:S(2)}) copy-start(bf16[3072,512]{1,0:T(8,128)(2,1)} %block_ref.3) | copy-start | bytes 9437188
  40.0 37.3 %collective-permute-start.8 = (bf16[1536,512]{1,0:T(8,128)(2,1)}, bf16[1536,512]{1,0:T(8,128)(2,1)S(1)}, u32[]{:S(2)}, u32[]{:S(2)}) collective-permute-start(bf16[1536,512]{1,0:T(8,128)(2,1)} %shard_map.62.refs_0_), channel_id=1, source_target_pairs={{0,4},{1,5},{4,8},{5,9},{6,2},{7,3},{8,12},{9,13},{10,6},{11,7},{1... | collective-permute-start | bytes 4718600 | tf_op jit(solution)/shard_map/ppermute | solution.py:487
  73.6 5.9 %collective-permute-start.6 = (bf16[1536,512]{1,0:T(8,128)(2,1)S(1)}, bf16[1536,512]{1,0:T(8,128)(2,1)S(1)}, u32[]{:S(2)}, u32[]{:S(2)}) collective-permute-start(bf16[1536,512]{1,0:T(8,128)(2,1)S(1)} %shard_map.65.edge_ref.refs_0_), channel_id=1, source_target_pairs={{0,1},{1,0},{2,3},{3,2},{4,5},{5,4},{6,7},{7,6},{8,9},{9,8},{10,11... | collective-permute-start | bytes 4718600 | tf_op jit(solution)/shard_map/ppermute | solution.py:487
  74.5 5.1 %collective-permute-start.7 = (f32[512,512]{1,0:T(8,128)S(1)}, f32[512,512]{1,0:T(8,128)S(1)}, u32[]{:S(2)}, u32[]{:S(2)}) collective-permute-start(f32[512,512]{1,0:T(8,128)S(1)} %get-tuple-element.35), channel_id=1, source_target_pairs={{0,1},{1,0},{2,3},{3,2},{4,5},{5,4},{6,7},{7,6},{8,9},{9,8},{10,11... | collective-permute-start | bytes 3145736 | tf_op jit(solution)/shard_map/ppermute | solution.py:487
  74.7 15.8 %collective-permute-start.5 = (bf16[1024,512]{1,0:T(8,128)(2,1)S(1)}, bf16[1024,512]{1,0:T(8,128)(2,1)S(1)}, u32[]{:S(2)}, u32[]{:S(2)}) collective-permute-start(bf16[1024,512]{1,0:T(8,128)(2,1)S(1)} %get-tuple-element.33), channel_id=1, source_target_pairs={{0,4},{1,2},{2,1},{4,8},{7,3},{5,6},{6,5},{8,12},{11,7},{9,10},{10... | collective-permute-start | bytes 3145736 | tf_op jit(solution)/shard_map/ppermute | solution.py:487
  76.0 20.2 %collective-permute-start.9 = (bf16[512,512]{1,0:T(8,128)(2,1)S(1)}, bf16[512,512]{1,0:T(8,128)(2,1)S(1)}, u32[]{:S(2)}, u32[]{:S(2)}) collective-permute-start(bf16[512,512]{1,0:T(8,128)(2,1)S(1)} %get-tuple-element.40), channel_id=1, source_target_pairs={{0,4},{1,2},{2,1},{4,8},{7,3},{5,6},{6,5},{8,12},{11,7},{9,10},{10... | collective-permute-start | bytes 1572872 | tf_op jit(solution)/shard_map/ppermute | solution.py:487
  90.6 7.9 %collective-permute-start.10 = (bf16[1024,512]{1,0:T(8,128)(2,1)S(1)}, bf16[1024,512]{1,0:T(8,128)(2,1)S(1)}, u32[]{:S(2)}, u32[]{:S(2)}) collective-permute-start(bf16[1024,512]{1,0:T(8,128)(2,1)S(1)} %shard_map.69.refs_0_), channel_id=1, source_target_pairs={{0,1},{1,0},{2,3},{3,2},{4,5},{5,4},{6,7},{7,6},{8,9},{9,8},{10,11... | collective-permute-start | bytes 3145736 | tf_op jit(solution)/shard_map/ppermute | solution.py:487
  91.4 7.2 %collective-permute-start.12 = (f32[512,512]{1,0:T(8,128)S(1)}, f32[512,512]{1,0:T(8,128)S(1)}, u32[]{:S(2)}, u32[]{:S(2)}) collective-permute-start(f32[512,512]{1,0:T(8,128)S(1)} %get-tuple-element.42), channel_id=1, source_target_pairs={{0,1},{1,0},{2,3},{3,2},{4,5},{5,4},{6,7},{7,6},{8,9},{9,8},{10,11... | collective-permute-start | bytes 3145736 | tf_op jit(solution)/shard_map/ppermute | solution.py:487
  96.2 2.3 %collective-permute-start.11 = (bf16[512,512]{1,0:T(8,128)(2,1)S(1)}, bf16[512,512]{1,0:T(8,128)(2,1)S(1)}, u32[]{:S(2)}, u32[]{:S(2)}) collective-permute-start(bf16[512,512]{1,0:T(8,128)(2,1)S(1)} %collective-permute-done.9.refs_1_), channel_id=1, source_target_pairs={{0,1},{1,0},{2,3},{3,2},{4,5},{5,4},{6,7},{7,6},{8,9},{9,8},{10,11... | collective-permute-start | bytes 1572872 | tf_op jit(solution)/shard_map/ppermute | solution.py:487

commit v4 on v3

--- a/solution.py
+++ b/solution.py
@@ -13,12 +13,11 @@
 VMEM_ALL = 63 * 2**20
 LEVEL = 4
 PARTS = 4
-TURNS = (2, 1)
-HEAD = 3
 
 SMEM = pl.BlockSpec(memory_space=pltpu.SMEM)
 HBM = pl.BlockSpec(memory_space=pltpu.HBM)
 ANY = pl.BlockSpec(memory_space=pl.ANY)
+VMEM = pl.BlockSpec(memory_space=pltpu.VMEM)
 TOKEN = jax.ShapeDtypeStruct((8, 128), jnp.float32)
 
 
@@ -46,7 +45,7 @@
 class Geometry:
     def __init__(self, position_ref, live_ref, sig_ref, block_total):
         self.live_ref, self.sig_ref, self.block_total = live_ref, sig_ref, block_total
-        self.me = position_ref[0]
+        self.me = position_ref if live_ref is None else position_ref[0]
         self.place = lax.rem(self.me, LEVEL)
         even = lax.rem(self.place, 2) == 0
         self.upper = self.place >= 2
@@ -107,8 +106,12 @@
 def rows_kernel(block_ref, *refs, low):
     out_ref, held, in_sem, out_sem = refs[-4:]
     size = held.shape[0]
-    ins = [pltpu.make_async_copy(rows_at(block_ref, low + k), held.at[k], in_sem.at[k]) for k in range(size)]
-    outs = [pltpu.make_async_copy(held.at[k], rows_at(out_ref, k), out_sem.at[k]) for k in range(size)]
+    part = held.shape[1]
+    ins, outs = [], []
+    for k in range(size):
+        source, target = pl.ds(low * ROWBLK + k * part, part), pl.ds(k * part, part)
+        ins.append(pltpu.make_async_copy(block_ref.at[source], held.at[k], in_sem.at[k]))
+        outs.append(pltpu.make_async_copy(held.at[k], out_ref.at[target], out_sem.at[k]))
     for copy in ins:
         copy.start()
     for copy, out in zip(ins, outs):
@@ -126,9 +129,9 @@
         in_specs=[HBM] + [ANY] * len(tokens),
         out_specs=ANY,
         scratch_shapes=[
-            pltpu.VMEM((size, ROWBLK, cols), block.dtype),
-            pltpu.SemaphoreType.DMA((size,)),
-            pltpu.SemaphoreType.DMA((size,)),
+            pltpu.VMEM((4 * size, ROWBLK // 4, cols), block.dtype),
+            pltpu.SemaphoreType.DMA((4 * size,)),
+            pltpu.SemaphoreType.DMA((4 * size,)),
         ],
         compiler_params=pltpu.CompilerParams(vmem_limit_bytes=VMEM_ALL),
     )(block, *tokens)
@@ -151,17 +154,13 @@
         copy.wait()
 
 
-def pick(position, edge, inner, sizes, *tokens):
-    rows, cols = edge.shape
-    total = rows // ROWBLK
-
-    def body(position_ref, edge_ref, inner_ref, *refs):
-        pick_kernel(position_ref, edge_ref, inner_ref, *refs[len(tokens) :], sizes=sizes)
-
-    return pl.pallas_call(
-        body,
+def pick(position, edge, inner, sizes):
+    cols = edge.shape[1]
+    total = sum(sizes)
+    return pl.pallas_call(
+        functools.partial(pick_kernel, sizes=sizes),
         out_shape=tuple(jax.ShapeDtypeStruct((size * ROWBLK, cols), edge.dtype) for size in sizes),
-        in_specs=[SMEM] + [ANY] * (2 + len(tokens)),
+        in_specs=[SMEM] + [ANY] * 2,
         out_specs=(ANY,) * len(sizes),
         scratch_shapes=[
             pltpu.VMEM((total, ROWBLK, cols), edge.dtype),
@@ -169,7 +168,7 @@
             pltpu.SemaphoreType.DMA((total,)),
         ],
         compiler_params=pltpu.CompilerParams(vmem_limit_bytes=VMEM_LIMIT),
-    )(position, edge, inner, *tokens)
+    )(position, edge, inner)
 
 
 def own_kernel(position_ref, live_ref, sig_ref, own_ref, diag_ref, own_t_ref, own, own_t, tile, in_sem, turned_sem, out_sem, *, block_total):
@@ -400,88 +399,146 @@
 
 
 def end_kernel(
-    position_ref, live_ref, sig_ref, own_t_ref, pieces, before, up_ref, low_ref, _token, own_t, held, tiles, own_sem, held_sem,
-    before_sem, out_sem, *, names, low, block_total,
+    position_ref, live_ref, sig_ref, own_t_ref, pieces, before, up_ref, low_ref, _token, tiles, out_sem, *, names, low,
+    block_total,
 ):
-    span = own_t.shape[0]
     geo = Geometry(position_ref, live_ref, sig_ref, block_total)
-    others = [getattr(geo, name) for name in names]
-    counts = [geo.count(geo.me, other) - low for other in others]
-    either = functools.reduce(jnp.maximum, counts)
-
-    def own_copy(at):
-        return pltpu.make_async_copy(own_t_ref.at[low + at], own_t.at[at], own_sem.at[at])
-
-    def held_copy(rows, i, at):
-        return pltpu.make_async_copy(rows, held.at[i, at], held_sem.at[i, at])
-
-    for i in range(len(names)):
-        start_tile(before[i], tiles.at[i], before_sem.at[i])
-        for at in range(span):
-            if i == 0:
-                pl.when(at < either)(own_copy(at).start)
-            pl.when(at < counts[i])(held_copy(pieces[i][at], i, at).start)
-    for at in range(span):
-        pl.when(at < either)(own_copy(at).wait)
-    for i in range(len(names)):
-        wait_tile(tiles.at[i], before_sem.at[i])
-
-        @pl.loop(0, jnp.maximum(counts[i], 0))
-        def _(at):
-            held_copy(pieces[i][0], i, at).wait()
-            dot_into(tiles.at[i], own_t[at], held[i, at])
-
-        geo.place_tile(tiles.at[i], others[i], up_ref, low_ref, out_sem.at[i])
+    for i, name in enumerate(names):
+        other = getattr(geo, name)
+        count = geo.count(geo.me, other) - low
+        tiles[i] = before[i][...]
+        for at, rows in enumerate(pieces[i]):
+            @pl.when(at < count)
+            def _():
+                dot_into(tiles.at[i], own_t_ref[low + at], rows[...])
+
+        geo.place_tile(tiles.at[i], other, up_ref, low_ref, out_sem.at[i])
     for i in range(len(names)):
         wait_tile(tiles.at[i], out_sem.at[i])
 
 
+def add_kernel(
+    position_ref, live_ref, sig_ref, own_t_ref, pieces, before, outs, *, names, low, left, block_total,
+):
+    geo = Geometry(position_ref, live_ref, sig_ref, block_total)
+    tiles, masked = outs[: len(names)], outs[len(names) :]
+    for i, name in enumerate(names):
+        count = geo.count(geo.me, getattr(geo, name)) - low
+        tiles[i][...] = before[i][...]
+        for at, rows in enumerate(pieces[i]):
+            @pl.when(at < count)
+            def _():
+                dot_into(tiles[i], own_t_ref[low + at], rows[...])
+
+        for k in range(left):
+            at = len(pieces[i]) + k
+            kept = own_t_ref[low + at]
+            masked[i][k] = jnp.where(at < count, kept, jnp.zeros_like(kept))
+
+
+def last_kernel(masked, pieces, before, up_ref, low_ref, tiles, out_sem, *, names, block_total):
+    geo = Geometry(lax.axis_index("ao"), None, None, block_total)
+    for i, name in enumerate(names):
+        total = before[i][...]
+        for k, rows in enumerate(pieces[i]):
+            total += jnp.dot(masked[i][k], rows[...], preferred_element_type=jnp.float32)
+        tiles[i] = total
+        geo.place_tile(tiles.at[i], getattr(geo, name), up_ref, low_ref, out_sem.at[i])
+    for i in range(len(names)):
+        wait_tile(tiles.at[i], out_sem.at[i])
+
+
+def split_jobs(jobs):
+    pieces = [piece for job in jobs for piece in job[1]]
+    places = [(p, k) for p, piece in enumerate(pieces) for k in range(piece.shape[0] // ROWBLK)]
+    span = len(places) // len(jobs)
+
+    def rows_of(refs):
+        rows = [rows_at(refs[p], k) for p, k in places]
+        return [rows[i * span : (i + 1) * span] for i in range(len(jobs))]
+
+    return [job[0] for job in jobs], pieces, [job[2] for job in jobs], span, rows_of
+
+
+def end_cost(n, span, cols):
+    return pl.CostEstimate(
+        flops=2 * n * span * ROWBLK * cols * cols,
+        bytes_accessed=2 * (n + 1) * span * ROWBLK * cols + 8 * n * cols * cols,
+        transcendentals=0,
+    )
+
+
 def end_tiles(scalars, own_t, jobs, low, outputs, block_total):
-    steps, cols, _ = own_t.shape
-    span, n = steps - low, len(jobs)
-    names = [job[0] for job in jobs]
-    pieces = [piece for job in jobs for piece in job[1]]
-    before = [job[2] for job in jobs]
-    places = [(p, k) for p, piece in enumerate(pieces) for k in range(piece.shape[0] // ROWBLK)]
+    cols, n = own_t.shape[1], len(jobs)
+    names, pieces, before, span, rows_of = split_jobs(jobs)
     n_in = len(pieces)
 
     def body(position_ref, live_ref, sig_ref, own_t_ref, *refs):
-        rows = [rows_at(refs[p], k) for p, k in places]
         end_kernel(
-            position_ref, live_ref, sig_ref, own_t_ref, [rows[i * span : (i + 1) * span] for i in range(n)],
-            refs[n_in : n_in + n], *refs[n_in + n + 2 :],
+            position_ref, live_ref, sig_ref, own_t_ref, rows_of(refs), refs[n_in : n_in + n], *refs[n_in + n + 2 :],
             names=names, low=low, block_total=block_total,
         )
 
     return pl.pallas_call(
         body,
         out_shape=(*(jax.ShapeDtypeStruct(o.shape, o.dtype) for o in outputs), TOKEN),
-        in_specs=[SMEM] * 3 + [ANY] * (3 + n_in + n),
+        in_specs=[SMEM] * 3 + [VMEM] * (1 + n_in + n) + [ANY] * 2,
         out_specs=(ANY,) * 3,
-        scratch_shapes=[
-            pltpu.VMEM((span, cols, ROWBLK), own_t.dtype),
-            pltpu.VMEM((n, span, ROWBLK, cols), own_t.dtype),
-            pltpu.VMEM((n, cols, cols), jnp.float32),
-            pltpu.SemaphoreType.DMA((span,)),
-            pltpu.SemaphoreType.DMA((n, span)),
-            pltpu.SemaphoreType.DMA((n,)),
-            pltpu.SemaphoreType.DMA((n,)),
-        ],
+        scratch_shapes=[pltpu.VMEM((n, cols, cols), jnp.float32), pltpu.SemaphoreType.DMA((n,))],
         input_output_aliases={4 + n_in + n: 0, 5 + n_in + n: 1},
         compiler_params=pltpu.CompilerParams(vmem_limit_bytes=VMEM_LIMIT),
-        cost_estimate=pl.CostEstimate(
-            flops=2 * n * span * ROWBLK * cols * cols,
-            bytes_accessed=2 * (n + 1) * span * ROWBLK * cols + 8 * n * cols * cols,
-            transcendentals=0,
-        ),
+        cost_estimate=end_cost(n, span, cols),
     )(*scalars, own_t, *pieces, *before, *outputs)
 
 
-def per_device(b_half, significant, live_rows):
-    block_total = lax.axis_size("ao")
-    position = lax.axis_index("ao").astype(jnp.int32)[None]
+def add_rows(scalars, own_t, jobs, low, left, block_total):
+    cols, n = own_t.shape[1], len(jobs)
+    names, pieces, before, span, rows_of = split_jobs(jobs)
+    n_in = len(pieces)
+
+    def body(position_ref, live_ref, sig_ref, own_t_ref, *refs):
+        add_kernel(
+            position_ref, live_ref, sig_ref, own_t_ref, rows_of(refs), refs[n_in : n_in + n], refs[n_in + n :],
+            names=names, low=low, left=left, block_total=block_total,
+        )
+
+    masked = jax.ShapeDtypeStruct((left, *own_t.shape[1:]), own_t.dtype)
+    outs = pl.pallas_call(
+        body,
+        out_shape=tuple(jax.ShapeDtypeStruct(tile.shape, tile.dtype) for tile in before) + (masked,) * n,
+        in_specs=[SMEM] * 3 + [VMEM] * (1 + n_in + n),
+        out_specs=(VMEM,) * (2 * n),
+        compiler_params=pltpu.CompilerParams(vmem_limit_bytes=VMEM_LIMIT),
+        cost_estimate=end_cost(n, span, cols),
+    )(*scalars, own_t, *pieces, *before)
+    return outs[:n], outs[n:]
+
+
+def last_tiles(masked, jobs, outputs, block_total):
+    cols, n = masked[0].shape[1], len(jobs)
+    names, pieces, before, span, rows_of = split_jobs(jobs)
+    n_in = len(pieces)
+
+    def body(*refs):
+        last_kernel(
+            refs[:n], rows_of(refs[n:]), refs[n + n_in : 2 * n + n_in], *refs[2 * n + n_in + 2 :],
+            names=names, block_total=block_total,
+        )
+
+    return pl.pallas_call(
+        body,
+        out_shape=tuple(jax.ShapeDtypeStruct(o.shape, o.dtype) for o in outputs),
+        in_specs=[VMEM] * (2 * n + n_in) + [ANY] * 2,
+        out_specs=(ANY,) * 2,
+        scratch_shapes=[pltpu.VMEM((n, cols, cols), jnp.float32), pltpu.SemaphoreType.DMA((n,))],
+        input_output_aliases={2 * n + n_in: 0, 2 * n + n_in + 1: 1},
+        compiler_params=pltpu.CompilerParams(vmem_limit_bytes=VMEM_LIMIT),
+        cost_estimate=end_cost(n, span, cols),
+    )(*masked, *pieces, *before, *outputs)
+
+
+def plan(total, head, turns, block_total, b_half, position, live_rows, significant):
     scalars = (position, live_rows, significant)
-    steps = b_half.shape[0] // ROWBLK
 
     def send(block, moves):
         return lax.ppermute(block, "ao", level_route(block_total, moves))
@@ -492,11 +549,11 @@
     relay = [(0, 1, 0), (1, 1, 1), (2, -1, 2), (3, -1, 3)]
     turn = [(0, 1, 0), (3, -1, 3), (1, 0, 2), (2, 0, 1)]
 
-    head = rows_after(b_half, 0, HEAD)
-    y_head = send(head, across)
-    tail = rows_after(b_half, HEAD, steps - HEAD, head)
-    y_tail = send(tail, across)
-    far_head, far_tail = send(head, far), send(tail, far)
+    first = rows_after(b_half, 0, head)
+    y_head = send(first, across)
+    later = rows_after(b_half, head, total - head, first)
+    y_tail = send(later, across)
+    far_head, far_tail = send(first, far), send(later, far)
     core = send(b_half, cores)
 
     diagonal, own_t = own_tile(scalars, b_half, block_total)
@@ -504,27 +561,36 @@
     turned = (own_t, core_t)
     y_head = after(y_head, made_core)
     relayed = send(y_head, relay)
-    y_part, both_part, made_y = pair_tiles(scalars, turned, "across", [y_head], 0, HEAD, None, None, block_total)
+    y_part, both_part, made_y = pair_tiles(scalars, turned, "across", [y_head], 0, head, None, None, block_total)
     both_part = send(both_part, cores)
     upper, lower, made_far = pair_tiles(
-        scalars, turned, "far", [far_head, far_tail], 0, steps, None, (upper, lower), block_total
+        scalars, turned, "far", [far_head, far_tail], 0, total, None, (upper, lower), block_total
     )
 
     y_tail = after(y_tail, made_y, made_far)
-    relay_tail = [send(piece, turn) for piece in pick(position, y_tail, far_tail, TURNS)]
+    relay_tail = [send(piece, turn) for piece in pick(position, y_tail, far_tail, turns)]
     both_tail = send(y_tail, cores)
     relay_part, last_part, made_relay = pair_tiles(
-        scalars, turned, "relay", [relayed], 0, HEAD, None, None, block_total
+        scalars, turned, "relay", [relayed], 0, head, None, None, block_total
     )
     last_part = send(last_part, cores)
     jobs = [("across", [y_tail], y_part), ("both", [both_tail], both_part)]
-    upper, lower, made_across = end_tiles(scalars, own_t, jobs, HEAD, (upper, lower), block_total)
-
-    relay_tail[0] = after(relay_tail[0], made_across, made_relay)
+    upper, lower, made_across = end_tiles(scalars, own_t, jobs, head, (upper, lower), block_total)
+
+    relay_tail[:2] = [after(piece, made_across, made_relay) for piece in relay_tail[:2]]
     last_tail = [send(piece, cores) for piece in relay_tail]
-    jobs = [("relay", relay_tail, relay_part), ("last", last_tail, last_part)]
-    upper, lower, _ = end_tiles(scalars, own_t, jobs, HEAD, (upper, lower), block_total)
+    jobs = [("relay", relay_tail[:-1], relay_part), ("last", last_tail[:-1], last_part)]
+    (relay_part, last_part), masked = add_rows(scalars, own_t, jobs, head, turns[-1], block_total)
+    jobs = [("relay", relay_tail[-1:], relay_part), ("last", last_tail[-1:], last_part)]
+    upper, lower = last_tiles(masked, jobs, (upper, lower), block_total)
     return diagonal, upper, lower
+
+
+def per_device(b_half, significant, live_rows):
+    block_total = lax.axis_size("ao")
+    position = lax.axis_index("ao").astype(jnp.int32)[None]
+    steps = b_half.shape[0] // ROWBLK
+    return plan(steps, 3, (1, 1, 1), block_total, b_half, position, live_rows, significant)
 
 
 def solution(mesh):

time: 103 us -> 102 us (level)
  starting transfers between devices: 14.1 us -> 19.9 us
  Pallas kernels: 30.7 us -> 27.5 us
  waiting for transfers between devices: 53.4 us -> 50.2 us
    ppermute x13 -> x15, starting transfers between devices: 14.1 us -> 19.9 us  [send(): return lax.ppermute(block, 'ao', level_route(block_total, moves))]
    ppermute x13 -> x15, waiting for transfers between devices: 53.4 us -> 50.2 us  [send(): return lax.ppermute(block, 'ao', level_route(block_total, moves))]
    pallas_call x1 -> x3, Pallas kernels: 0.27 us -> 2.99 us  [the longest x1 1.76 us: last_tiles(): pl.pallas_call(body, out_shape=tuple((jax.ShapeDtypeStruct(o.shape, o.dty...]
    pallas_call x2 -> x1, Pallas kernels: 4.86 us -> 2.25 us  [end_tiles(): pl.pallas_call(body, out_shape=(*(jax.ShapeDtypeStruct(o.shape, o.dtype)...]
    pallas_call x3, Pallas kernels: 10.8 us -> 8.65 us  [pair_tiles(): pl.pallas_call(body, out_shape=tuple((jax.ShapeDtypeStruct(c.shape, c.dty...]
  transfers between devices with their start and end apart: 13 -> 15, of which waited for: 6 -> 7; matrix products, arithmetic and copies ran while one was open for 0% -> 0% of each run, Pallas kernels for 28% -> 26%
where the time goes in v4:
time: 102 us; the launch traced here: 100 us
  waiting for transfers between devices  50.2 us (49%)
  Pallas kernels  27.5 us (27%)
  starting transfers between devices  19.9 us (20%)
  local copies, waits for them, and re-layouts  1.99 us (2%)
    ppermute x15, waiting for transfers between devices, send(): return lax.ppermute(block, 'ao', level_route(block_total, moves))  50.2 us
    ppermute x15, starting transfers between devices, send(): return lax.ppermute(block, 'ao', level_route(block_total, moves))  19.9 us
    pallas_call x3, Pallas kernels, pair_tiles(): pl.pallas_call(body, out_shape=tuple((jax.ShapeDtypeStruct(c.shape, c.dty...  8.65 us
    pallas_call x1, Pallas kernels, own_tile(): pl.pallas_call(functools.partial(own_kernel, block_total=block_total), ou...  5.34 us
    pallas_call x2, Pallas kernels, rows_after(): pl.pallas_call(functools.partial(rows_kernel, low=low), out_shape=jax.Sha...  4.71 us
    pallas_call x1, Pallas kernels, core_tile(): pl.pallas_call(functools.partial(core_kernel, block_total=block_total), o...  3.54 us
    pallas_call x1, Pallas kernels, end_tiles(): pl.pallas_call(body, out_shape=(*(jax.ShapeDtypeStruct(o.shape, o.dtype)...  2.25 us
  transfers between devices with their start and end apart: 15, of which 7 were waited for; matrix products, arithmetic and copies ran while one was open for 0% of the time, Pallas kernels for 26%

profile of v4, /device:TPU:5, one launch (start us, length us, event | category | flops | bytes accessed | tf_op | source)
XLA Modules:
  0.0 100.4 jit_solution(17127399586161469493)
XLA Ops:
  0.6 0.7 collective-permute-start.1
  1.4 2.3 %shard_map.59.refs_0_ = bf16[1536,512]{1,0:T(8,128)(2,1)} custom-call(bf16[3072,512]{1,0:T(8,128)(2,1)} %block_ref.3), custom_call_target="tpu_custom_call" | custom-call | tf_op jit(solution)/shard_map/pallas_call | solution.py:126
  3.7 0.0 copy-start.2
  3.7 0.0 copy-start.1
  3.7 0.1 collective-permute-start.2
  3.8 2.4 %shard_map.60 = bf16[1536,512]{1,0:T(8,128)(2,1)} custom-call(bf16[3072,512]{1,0:T(8,128)(2,1)} %block_ref.3, bf16[1536,512]{1,0:T(8,128)(2,1)} %shard_map.59.refs_0_), custom_call_target="tpu_custom_call" | custom-call | tf_op jit(solution)/shard_map/pallas_call | solution.py:126
  6.2 3.6 %collective-permute-start.4 = (bf16[1536,512]{1,0:T(8,128)(2,1)}, bf16[1536,512]{1,0:T(8,128)(2,1)S(1)}, u32[]{:S(2)}, u32[]{:S(2)}) collective-permute-start(bf16[1536,512]{1,0:T(8,128)(2,1)} %shard_map.60), channel_id=1, source_target_pairs={{1,4},{3,6},{5,8},{4,1},{7,10},{6,3},{9,12},{8,5},{11,14},{10,7},{... | collective-permute-start | bytes 4718600 | tf_op jit(solution)/shard_map/ppermute | solution.py:544
  9.8 2.0 %collective-permute-start.3 = (bf16[1536,512]{1,0:T(8,128)(2,1)}, bf16[1536,512]{1,0:T(8,128)(2,1)}, u32[]{:S(2)}, u32[]{:S(2)}) collective-permute-start(bf16[1536,512]{1,0:T(8,128)(2,1)} %shard_map.59.refs_0_), channel_id=1, source_target_pairs={{1,4},{3,6},{5,8},{4,1},{7,10},{6,3},{9,12},{8,5},{11,14},{10,7},{... | collective-permute-start | bytes 4718600 | tf_op jit(solution)/shard_map/ppermute | solution.py:544
  11.8 1.5 %collective-permute-start = (bf16[1536,512]{1,0:T(8,128)(2,1)}, bf16[1536,512]{1,0:T(8,128)(2,1)S(1)}, u32[]{:S(2)}, u32[]{:S(2)}) collective-permute-start(bf16[1536,512]{1,0:T(8,128)(2,1)} %shard_map.60), channel_id=1, source_target_pairs={{0,2},{1,3},{2,0},{3,1},{4,6},{5,7},{6,4},{7,5},{8,10},{9,11},{10,... | collective-permute-start | bytes 4718600 | tf_op jit(solution)/shard_map/ppermute | solution.py:544
  13.3 0.0 copy-done.2
  13.3 0.1 copy.16.sig_ref
  13.4 0.0 copy-done.1
  13.4 0.0 copy-start
  13.4 1.9 %copy-done = bf16[3072,512]{1,0:T(8,128)(2,1)S(1)} copy-done((bf16[3072,512]{1,0:T(8,128)(2,1)S(1)}, bf16[3072,512]{1,0:T(8,128)(2,1)}, u32[]{:S(2)}) %copy-start) | copy-done | bytes 3145752
  15.3 5.3 %shard_map.58 = (f32[1,512,512]{2,1,0:T(8,128)}, bf16[6,512,512]{2,1,0:T(8,128)(2,1)S(1)}) custom-call(s32[1]{0:T(128)} %bitcast.position_ref, s32[16]{0:T(128)S(1)} %copy-done.1, s32[16,3]{1,0:T(8,128)S(1)} %copy.16.sig_ref, bf16[3072,512]{1,0:T(8,128)(2,1)S(1)} %copy-done), custom_call_target="tpu_custom_call" | custom-call | flops 1610612736 | bytes 7340032 | tf_op jit(solution)/shard_map/pallas_call | solution.py:208
  20.6 0.0 collective-permute-done.1.core_ref
  20.6 3.5 %shard_map.61 = (f32[1,3,512,512]{3,2,1,0:T(8,128)}, f32[1,3,512,512]{3,2,1,0:T(8,128)}, bf16[6,512,512]{2,1,0:T(8,128)(2,1)S(1)}, f32[8,128]{1,0:T(8,128)S(1)}) custom-call(s32[1]{0:T(128)} %bitcast.position_ref, s32[16]{0:T(128)S(1)} %copy-done.1, s32[16,3]{1,0:T(8,128)S(1)} %copy.16.sig_ref, bf16[3072,512]{1,0:T(8,128)(2,1)} %collective-permute-done.1.core_ref, ...), custom_call_target="tpu_custom_call" | custom-call | flops 1610612736 | bytes 10485760 | tf_op jit(solution)/shard_map/pallas_call | solution.py:278
  24.2 16.0 %collective-permute-done.2.refs_0_ = bf16[1536,512]{1,0:T(8,128)(2,1)} collective-permute-done((bf16[1536,512]{1,0:T(8,128)(2,1)}, bf16[1536,512]{1,0:T(8,128)(2,1)}, u32[]{:S(2)}, u32[]{:S(2)}) %collective-permute-start.2) | collective-permute-done | bytes 1572896 | tf_op jit(solution)/shard_map/ppermute | solution.py:544
  40.1 1.3 %collective-permute-start.8 = (bf16[1536,512]{1,0:T(8,128)(2,1)}, bf16[1536,512]{1,0:T(8,128)(2,1)S(1)}, u32[]{:S(2)}, u32[]{:S(2)}) collective-permute-start(bf16[1536,512]{1,0:T(8,128)(2,1)} %shard_map.62.refs_0_), channel_id=1, source_target_pairs={{0,4},{1,5},{4,8},{5,9},{6,2},{7,3},{8,12},{9,13},{10,6},{11,7},{1... | collective-permute-start | bytes 4718600 | tf_op jit(solution)/shard_map/ppermute | solution.py:544
  41.4 2.5 %shard_map.63 = (f32[512,512]{1,0:T(8,128)S(1)}, f32[512,512]{1,0:T(8,128)S(1)}, f32[8,128]{1,0:T(8,128)S(1)}) custom-call(s32[1]{0:T(128)} %bitcast.position_ref, s32[16]{0:T(128)S(1)} %copy-done.1, s32[16,3]{1,0:T(8,128)S(1)} %copy.16.sig_ref, bf16[6,512,512]{2,1,0:T(8,128)(2,1)S(1)} %get-tuple-element.31.own_t_ref, ...), custom_call_target="tpu_custom_call" | custom-call | flops 1610612736 | bytes 8912896 | tf_op jit(solution)/shard_map/pallas_call | solution.py:378
  44.0 0.0 collective-permute-done.4.refs_1_.inner_ref
  44.0 1.6 %collective-permute-done.3.refs_0_ = bf16[1536,512]{1,0:T(8,128)(2,1)} collective-permute-done((bf16[1536,512]{1,0:T(8,128)(2,1)}, bf16[1536,512]{1,0:T(8,128)(2,1)}, u32[]{:S(2)}, u32[]{:S(2)}) %collective-permute-start.3) | collective-permute-done | bytes 1572896 | tf_op jit(solution)/shard_map/ppermute | solution.py:544
  45.6 3.4 %shard_map.64 = (f32[1,3,512,512]{3,2,1,0:T(8,128)}, f32[1,3,512,512]{3,2,1,0:T(8,128)}, f32[8,128]{1,0:T(8,128)S(1)}) custom-call(s32[1]{0:T(128)} %bitcast.position_ref, s32[16]{0:T(128)S(1)} %copy-done.1, s32[16,3]{1,0:T(8,128)S(1)} %copy.16.sig_ref, ...), custom_call_target="tpu_custom_call", output_to_operand_aliasing={{0}: (7, {}), {1}: (8, {})} | custom-call | flops 3221225472 | bytes 13631488 | tf_op jit(solution)/shard_map/pallas_call | solution.py:378
  49.0 24.7 %collective-permute-done.refs_0_ = bf16[1536,512]{1,0:T(8,128)(2,1)S(1)} collective-permute-done((bf16[1536,512]{1,0:T(8,128)(2,1)}, bf16[1536,512]{1,0:T(8,128)(2,1)S(1)}, u32[]{:S(2)}, u32[]{:S(2)}) %collective-permute-start) | collective-permute-done | bytes 1572896 | tf_op jit(solution)/shard_map/ppermute | solution.py:544
  73.7 0.8 collective-permute-start.6
  74.5 0.0 collective-permute-start.7
  74.5 0.3 shard_map.66
  74.8 1.3 %collective-permute-start.9 = (bf16[512,512]{1,0:T(8,128)(2,1)S(1)}, bf16[512,512]{1,0:T(8,128)(2,1)S(1)}, u32[]{:S(2)}, u32[]{:S(2)}) collective-permute-start(bf16[512,512]{1,0:T(8,128)(2,1)S(1)} %get-tuple-element.45), channel_id=1, source_target_pairs={{0,4},{1,2},{2,1},{4,8},{7,3},{5,6},{6,5},{8,12},{11,7},{9,10},{10... | collective-permute-start | bytes 1572872 | tf_op jit(solution)/shard_map/ppermute | solution.py:544
  76.1 1.3 %collective-permute-start.5 = (bf16[512,512]{1,0:T(8,128)(2,1)S(1)}, bf16[512,512]{1,0:T(8,128)(2,1)S(1)}, u32[]{:S(2)}, u32[]{:S(2)}) collective-permute-start(bf16[512,512]{1,0:T(8,128)(2,1)S(1)} %get-tuple-element.38), channel_id=1, source_target_pairs={{0,4},{1,2},{2,1},{4,8},{7,3},{5,6},{6,5},{8,12},{11,7},{9,10},{10... | collective-permute-start | bytes 1572872 | tf_op jit(solution)/shard_map/ppermute | solution.py:544
  77.4 0.2 collective-permute-done.8.refs_0_
  77.6 2.7 %shard_map.68 = (f32[512,512]{1,0:T(8,128)S(1)}, f32[512,512]{1,0:T(8,128)S(1)}, f32[8,128]{1,0:T(8,128)S(1)}) custom-call(s32[1]{0:T(128)} %bitcast.position_ref, s32[16]{0:T(128)S(1)} %copy-done.1, s32[16,3]{1,0:T(8,128)S(1)} %copy.16.sig_ref, bf16[6,512,512]{2,1,0:T(8,128)(2,1)S(1)} %get-tuple-element.31.own_t_ref, ...), custom_call_target="tpu_custom_call" | custom-call | flops 1610612736 | bytes 8912896 | tf_op jit(solution)/shard_map/pallas_call | solution.py:378
  80.3 1.9 %collective-permute-start.12 = (f32[512,512]{1,0:T(8,128)S(1)}, f32[512,512]{1,0:T(8,128)S(1)}, u32[]{:S(2)}, u32[]{:S(2)}) collective-permute-start(f32[512,512]{1,0:T(8,128)S(1)} %get-tuple-element.47), channel_id=1, source_target_pairs={{0,1},{1,0},{2,3},{3,2},{4,5},{5,4},{6,7},{7,6},{8,9},{9,8},{10,11... | collective-permute-start | bytes 3145736 | tf_op jit(solution)/shard_map/ppermute | solution.py:544
  82.2 0.0 collective-permute-done.7.refs_3_
  82.2 1.3 %collective-permute-start.13 = (bf16[512,512]{1,0:T(8,128)(2,1)S(1)}, bf16[512,512]{1,0:T(8,128)(2,1)S(1)}, u32[]{:S(2)}, u32[]{:S(2)}) collective-permute-start(bf16[512,512]{1,0:T(8,128)(2,1)S(1)} %get-tuple-element.50), channel_id=1, source_target_pairs={{0,4},{1,2},{2,1},{4,8},{7,3},{5,6},{6,5},{8,12},{11,7},{9,10},{10... | collective-permute-start | bytes 1572872 | tf_op jit(solution)/shard_map/ppermute | solution.py:544
  83.5 0.0 collective-permute-done.6.refs_1_
  83.5 2.2 %shard_map.67 = (f32[1,3,512,512]{3,2,1,0:T(8,128)}, f32[1,3,512,512]{3,2,1,0:T(8,128)}, f32[8,128]{1,0:T(8,128)S(1)}) custom-call(s32[1]{0:T(128)} %bitcast.position_ref, s32[16]{0:T(128)S(1)} %copy-done.1, s32[16,3]{1,0:T(8,128)S(1)} %copy.16.sig_ref, ...), custom_call_target="tpu_custom_call", output_to_operand_aliasing={{0}: (8, {}), {1}: (9, {})} | custom-call | flops 1610612736 | bytes 8912896 | tf_op jit(solution)/shard_map/pallas_call | solution.py:482
  85.8 0.0 collective-permute-done.9.refs_0_
  85.8 2.6 %collective-permute-start.11 = (bf16[512,512]{1,0:T(8,128)(2,1)S(1)}, bf16[512,512]{1,0:T(8,128)(2,1)S(1)}, u32[]{:S(2)}, u32[]{:S(2)}) collective-permute-start(bf16[512,512]{1,0:T(8,128)(2,1)S(1)} %shard_map.70.refs_1_), channel_id=1, source_target_pairs={{0,1},{1,0},{2,3},{3,2},{4,5},{5,4},{6,7},{7,6},{8,9},{9,8},{10,11... | collective-permute-start | bytes 1572872 | tf_op jit(solution)/shard_map/ppermute | solution.py:544
  88.4 2.3 %collective-permute-done.5.refs_0_ = bf16[512,512]{1,0:T(8,128)(2,1)S(1)} collective-permute-done((bf16[512,512]{1,0:T(8,128)(2,1)S(1)}, bf16[512,512]{1,0:T(8,128)(2,1)S(1)}, u32[]{:S(2)}, u32[]{:S(2)}) %collective-permute-start.5) | collective-permute-done | bytes 524320 | tf_op jit(solution)/shard_map/ppermute | solution.py:544
  90.7 0.8 collective-permute-start.10
  91.5 4.8 %collective-permute-done.13.refs_2_ = bf16[512,512]{1,0:T(8,128)(2,1)S(1)} collective-permute-done((bf16[512,512]{1,0:T(8,128)(2,1)S(1)}, bf16[512,512]{1,0:T(8,128)(2,1)S(1)}, u32[]{:S(2)}, u32[]{:S(2)}) %collective-permute-start.13) | collective-permute-done | bytes 524320 | tf_op jit(solution)/shard_map/ppermute | solution.py:544
  96.3 0.8 collective-permute-start.14
  97.1 0.0 collective-permute-done.11.refs_3_
  97.1 0.0 collective-permute-done.10.refs_2_
  97.1 0.0 collective-permute-done.12.refs_5_
  97.1 1.0 shard_map.71
  98.0 0.6 collective-permute-done.14.refs_3_
  98.6 1.8 %shard_map.72 = (f32[1,3,512,512]{3,2,1,0:T(8,128)}, f32[1,3,512,512]{3,2,1,0:T(8,128)}) custom-call(bf16[1,512,512]{2,1,0:T(8,128)(2,1)S(1)} %get-tuple-element.48.refs_0_, bf16[1,512,512]{2,1,0:T(8,128)(2,1)S(1)} %get-tuple-element.49.refs_1_, bf16[512,512]{1,0:T(8,128)(2,1)S(1)} %collective-permute-done.13.refs_2_, ...), custom_call_target="tpu_custom_call", output_to_operand_aliasing={{0}: (6, {}), {1}: (7, {})} | custom-call | flops 536870912 | bytes 5767168 | tf_op jit(solution)/shard_map/pallas_call | solution.py:528
  (4 shorter events, 0.0 us)
Async XLA Ops:
  0.6 20.0 %collective-permute-start.1 = (bf16[3072,512]{1,0:T(8,128)(2,1)}, bf16[3072,512]{1,0:T(8,128)(2,1)}, u32[]{:S(2)}, u32[]{:S(2)}) collective-permute-start(bf16[3072,512]{1,0:T(8,128)(2,1)} %block_ref.3), channel_id=1, source_target_pairs={{0,1},{1,0},{2,3},{3,2},{4,5},{5,4},{6,7},{7,6},{8,9},{9,8},{10,11... | collective-permute-start | bytes 9437192 | tf_op jit(solution)/shard_map/ppermute | solution.py:544
  3.7 9.6 %copy-start.2 = (s32[16,3]{0,1:T(4,128)S(1)}, s32[16,3]{0,1:T(4,128)}, u32[]{:S(2)}) copy-start(s32[16,3]{0,1:T(4,128)} %param.4) | copy-start | bytes 580
  3.7 9.6 %copy-start.1 = (s32[16]{0:T(128)S(1)}, s32[16]{0:T(128)}, u32[]{:S(2)}) copy-start(s32[16]{0:T(128)} %live_ref.13) | copy-start | bytes 196
  3.7 36.4 %collective-permute-start.2 = (bf16[1536,512]{1,0:T(8,128)(2,1)}, bf16[1536,512]{1,0:T(8,128)(2,1)}, u32[]{:S(2)}, u32[]{:S(2)}) collective-permute-start(bf16[1536,512]{1,0:T(8,128)(2,1)} %shard_map.59.refs_0_), channel_id=1, source_target_pairs={{0,2},{1,3},{2,0},{3,1},{4,6},{5,7},{6,4},{7,5},{8,10},{9,11},{10,... | collective-permute-start | bytes 4718600 | tf_op jit(solution)/shard_map/ppermute | solution.py:544
  6.2 37.8 %collective-permute-start.4 = (bf16[1536,512]{1,0:T(8,128)(2,1)}, bf16[1536,512]{1,0:T(8,128)(2,1)S(1)}, u32[]{:S(2)}, u32[]{:S(2)}) collective-permute-start(bf16[1536,512]{1,0:T(8,128)(2,1)} %shard_map.60), channel_id=1, source_target_pairs={{1,4},{3,6},{5,8},{4,1},{7,10},{6,3},{9,12},{8,5},{11,14},{10,7},{... | collective-permute-start | bytes 4718600 | tf_op jit(solution)/shard_map/ppermute | solution.py:544
  9.8 35.8 %collective-permute-start.3 = (bf16[1536,512]{1,0:T(8,128)(2,1)}, bf16[1536,512]{1,0:T(8,128)(2,1)}, u32[]{:S(2)}, u32[]{:S(2)}) collective-permute-start(bf16[1536,512]{1,0:T(8,128)(2,1)} %shard_map.59.refs_0_), channel_id=1, source_target_pairs={{1,4},{3,6},{5,8},{4,1},{7,10},{6,3},{9,12},{8,5},{11,14},{10,7},{... | collective-permute-start | bytes 4718600 | tf_op jit(solution)/shard_map/ppermute | solution.py:544
  11.8 62.0 %collective-permute-start = (bf16[1536,512]{1,0:T(8,128)(2,1)}, bf16[1536,512]{1,0:T(8,128)(2,1)S(1)}, u32[]{:S(2)}, u32[]{:S(2)}) collective-permute-start(bf16[1536,512]{1,0:T(8,128)(2,1)} %shard_map.60), channel_id=1, source_target_pairs={{0,2},{1,3},{2,0},{3,1},{4,6},{5,7},{6,4},{7,5},{8,10},{9,11},{10,... | collective-permute-start | bytes 4718600 | tf_op jit(solution)/shard_map/ppermute | solution.py:544
  13.4 1.9 %copy-start = (bf16[3072,512]{1,0:T(8,128)(2,1)S(1)}, bf16[3072,512]{1,0:T(8,128)(2,1)}, u32[]{:S(2)}) copy-start(bf16[3072,512]{1,0:T(8,128)(2,1)} %block_ref.3) | copy-start | bytes 9437188
  40.1 37.5 %collective-permute-start.8 = (bf16[1536,512]{1,0:T(8,128)(2,1)}, bf16[1536,512]{1,0:T(8,128)(2,1)S(1)}, u32[]{:S(2)}, u32[]{:S(2)}) collective-permute-start(bf16[1536,512]{1,0:T(8,128)(2,1)} %shard_map.62.refs_0_), channel_id=1, source_target_pairs={{0,4},{1,5},{4,8},{5,9},{6,2},{7,3},{8,12},{9,13},{10,6},{11,7},{1... | collective-permute-start | bytes 4718600 | tf_op jit(solution)/shard_map/ppermute | solution.py:544
  73.7 9.8 %collective-permute-start.6 = (bf16[1536,512]{1,0:T(8,128)(2,1)S(1)}, bf16[1536,512]{1,0:T(8,128)(2,1)S(1)}, u32[]{:S(2)}, u32[]{:S(2)}) collective-permute-start(bf16[1536,512]{1,0:T(8,128)(2,1)S(1)} %shard_map.65.edge_ref.refs_0_), channel_id=1, source_target_pairs={{0,1},{1,0},{2,3},{3,2},{4,5},{5,4},{6,7},{7,6},{8,9},{9,8},{10,11... | collective-permute-start | bytes 4718600 | tf_op jit(solution)/shard_map/ppermute | solution.py:544
  74.5 7.7 %collective-permute-start.7 = (f32[512,512]{1,0:T(8,128)S(1)}, f32[512,512]{1,0:T(8,128)S(1)}, u32[]{:S(2)}, u32[]{:S(2)}) collective-permute-start(f32[512,512]{1,0:T(8,128)S(1)} %get-tuple-element.40), channel_id=1, source_target_pairs={{0,1},{1,0},{2,3},{3,2},{4,5},{5,4},{6,7},{7,6},{8,9},{9,8},{10,11... | collective-permute-start | bytes 3145736 | tf_op jit(solution)/shard_map/ppermute | solution.py:544
  74.8 10.9 %collective-permute-start.9 = (bf16[512,512]{1,0:T(8,128)(2,1)S(1)}, bf16[512,512]{1,0:T(8,128)(2,1)S(1)}, u32[]{:S(2)}, u32[]{:S(2)}) collective-permute-start(bf16[512,512]{1,0:T(8,128)(2,1)S(1)} %get-tuple-element.45), channel_id=1, source_target_pairs={{0,4},{1,2},{2,1},{4,8},{7,3},{5,6},{6,5},{8,12},{11,7},{9,10},{10... | collective-permute-start | bytes 1572872 | tf_op jit(solution)/shard_map/ppermute | solution.py:544
  76.1 14.5 %collective-permute-start.5 = (bf16[512,512]{1,0:T(8,128)(2,1)S(1)}, bf16[512,512]{1,0:T(8,128)(2,1)S(1)}, u32[]{:S(2)}, u32[]{:S(2)}) collective-permute-start(bf16[512,512]{1,0:T(8,128)(2,1)S(1)} %get-tuple-element.38), channel_id=1, source_target_pairs={{0,4},{1,2},{2,1},{4,8},{7,3},{5,6},{6,5},{8,12},{11,7},{9,10},{10... | collective-permute-start | bytes 1572872 | tf_op jit(solution)/shard_map/ppermute | solution.py:544
  80.3 16.8 %collective-permute-start.12 = (f32[512,512]{1,0:T(8,128)S(1)}, f32[512,512]{1,0:T(8,128)S(1)}, u32[]{:S(2)}, u32[]{:S(2)}) collective-permute-start(f32[512,512]{1,0:T(8,128)S(1)} %get-tuple-element.47), channel_id=1, source_target_pairs={{0,1},{1,0},{2,3},{3,2},{4,5},{5,4},{6,7},{7,6},{8,9},{9,8},{10,11... | collective-permute-start | bytes 3145736 | tf_op jit(solution)/shard_map/ppermute | solution.py:544
  82.2 14.1 %collective-permute-start.13 = (bf16[512,512]{1,0:T(8,128)(2,1)S(1)}, bf16[512,512]{1,0:T(8,128)(2,1)S(1)}, u32[]{:S(2)}, u32[]{:S(2)}) collective-permute-start(bf16[512,512]{1,0:T(8,128)(2,1)S(1)} %get-tuple-element.50), channel_id=1, source_target_pairs={{0,4},{1,2},{2,1},{4,8},{7,3},{5,6},{6,5},{8,12},{11,7},{9,10},{10... | collective-permute-start | bytes 1572872 | tf_op jit(solution)/shard_map/ppermute | solution.py:544
  85.8 11.3 %collective-permute-start.11 = (bf16[512,512]{1,0:T(8,128)(2,1)S(1)}, bf16[512,512]{1,0:T(8,128)(2,1)S(1)}, u32[]{:S(2)}, u32[]{:S(2)}) collective-permute-start(bf16[512,512]{1,0:T(8,128)(2,1)S(1)} %shard_map.70.refs_1_), channel_id=1, source_target_pairs={{0,1},{1,0},{2,3},{3,2},{4,5},{5,4},{6,7},{7,6},{8,9},{9,8},{10,11... | collective-permute-start | bytes 1572872 | tf_op jit(solution)/shard_map/ppermute | solution.py:544
  90.7 6.4 %collective-permute-start.10 = (bf16[512,512]{1,0:T(8,128)(2,1)S(1)}, bf16[512,512]{1,0:T(8,128)(2,1)S(1)}, u32[]{:S(2)}, u32[]{:S(2)}) collective-permute-start(bf16[512,512]{1,0:T(8,128)(2,1)S(1)} %shard_map.69.refs_0_), channel_id=1, source_target_pairs={{0,1},{1,0},{2,3},{3,2},{4,5},{5,4},{6,7},{7,6},{8,9},{9,8},{10,11... | collective-permute-start | bytes 1572872 | tf_op jit(solution)/shard_map/ppermute | solution.py:544
  96.3 2.3 %collective-permute-start.14 = (bf16[512,512]{1,0:T(8,128)(2,1)S(1)}, bf16[512,512]{1,0:T(8,128)(2,1)S(1)}, u32[]{:S(2)}, u32[]{:S(2)}) collective-permute-start(bf16[512,512]{1,0:T(8,128)(2,1)S(1)} %collective-permute-done.13.refs_2_), channel_id=1, source_target_pairs={{0,1},{1,0},{2,3},{3,2},{4,5},{5,4},{6,7},{7,6},{8,9},{9,8},{10,11... | collective-permute-start | bytes 1572872 | tf_op jit(solution)/shard_map/ppermute | solution.py:544

commit v5 on v4

--- a/solution.py
+++ b/solution.py
@@ -417,31 +417,40 @@
         wait_tile(tiles.at[i], out_sem.at[i])
 
 
-def add_kernel(
-    position_ref, live_ref, sig_ref, own_t_ref, pieces, before, outs, *, names, low, left, block_total,
-):
+def mask_kernel(position_ref, live_ref, sig_ref, own_t_ref, *masked, names, low, block_total):
     geo = Geometry(position_ref, live_ref, sig_ref, block_total)
-    tiles, masked = outs[: len(names)], outs[len(names) :]
-    for i, name in enumerate(names):
+    for out_ref, name in zip(masked, names):
         count = geo.count(geo.me, getattr(geo, name)) - low
-        tiles[i][...] = before[i][...]
-        for at, rows in enumerate(pieces[i]):
-            @pl.when(at < count)
-            def _():
-                dot_into(tiles[i], own_t_ref[low + at], rows[...])
-
-        for k in range(left):
-            at = len(pieces[i]) + k
-            kept = own_t_ref[low + at]
-            masked[i][k] = jnp.where(at < count, kept, jnp.zeros_like(kept))
-
-
-def last_kernel(masked, pieces, before, up_ref, low_ref, tiles, out_sem, *, names, block_total):
+        for k in range(out_ref.shape[0]):
+            kept = own_t_ref[low + k]
+            out_ref[k] = jnp.where(k < count, kept, jnp.zeros_like(kept))
+
+
+def mask_rows(scalars, own_t, names, low, block_total):
+    masked = jax.ShapeDtypeStruct((own_t.shape[0] - low, *own_t.shape[1:]), own_t.dtype)
+    return pl.pallas_call(
+        functools.partial(mask_kernel, names=names, low=low, block_total=block_total),
+        out_shape=(masked,) * len(names),
+        in_specs=[SMEM] * 3 + [VMEM],
+        out_specs=(VMEM,) * len(names),
+        compiler_params=pltpu.CompilerParams(vmem_limit_bytes=VMEM_LIMIT),
+    )(*scalars, own_t)
+
+
+def add_kernel(masked, pieces, before, outs):
+    for i, out_ref in enumerate(outs):
+        total = before[i][...]
+        for k, rows in enumerate(pieces[i]):
+            total += jnp.dot(masked[i][k], rows[...], preferred_element_type=jnp.float32)
+        out_ref[...] = total
+
+
+def last_kernel(masked, pieces, before, up_ref, low_ref, tiles, out_sem, *, names, first, block_total):
     geo = Geometry(lax.axis_index("ao"), None, None, block_total)
     for i, name in enumerate(names):
         total = before[i][...]
         for k, rows in enumerate(pieces[i]):
-            total += jnp.dot(masked[i][k], rows[...], preferred_element_type=jnp.float32)
+            total += jnp.dot(masked[i][first + k], rows[...], preferred_element_type=jnp.float32)
         tiles[i] = total
         geo.place_tile(tiles.at[i], getattr(geo, name), up_ref, low_ref, out_sem.at[i])
     for i in range(len(names)):
@@ -491,30 +500,25 @@
     )(*scalars, own_t, *pieces, *before, *outputs)
 
 
-def add_rows(scalars, own_t, jobs, low, left, block_total):
-    cols, n = own_t.shape[1], len(jobs)
-    names, pieces, before, span, rows_of = split_jobs(jobs)
+def add_rows(masked, jobs):
+    cols, n = masked[0].shape[1], len(jobs)
+    _, pieces, before, span, rows_of = split_jobs(jobs)
     n_in = len(pieces)
 
-    def body(position_ref, live_ref, sig_ref, own_t_ref, *refs):
-        add_kernel(
-            position_ref, live_ref, sig_ref, own_t_ref, rows_of(refs), refs[n_in : n_in + n], refs[n_in + n :],
-            names=names, low=low, left=left, block_total=block_total,
-        )
-
-    masked = jax.ShapeDtypeStruct((left, *own_t.shape[1:]), own_t.dtype)
-    outs = pl.pallas_call(
+    def body(*refs):
+        add_kernel(refs[:n], rows_of(refs[n:]), refs[n + n_in : 2 * n + n_in], refs[2 * n + n_in :])
+
+    return pl.pallas_call(
         body,
-        out_shape=tuple(jax.ShapeDtypeStruct(tile.shape, tile.dtype) for tile in before) + (masked,) * n,
-        in_specs=[SMEM] * 3 + [VMEM] * (1 + n_in + n),
-        out_specs=(VMEM,) * (2 * n),
+        out_shape=tuple(jax.ShapeDtypeStruct(tile.shape, tile.dtype) for tile in before),
+        in_specs=[VMEM] * (2 * n + n_in),
+        out_specs=(VMEM,) * n,
         compiler_params=pltpu.CompilerParams(vmem_limit_bytes=VMEM_LIMIT),
         cost_estimate=end_cost(n, span, cols),
-    )(*scalars, own_t, *pieces, *before)
-    return outs[:n], outs[n:]
-
-
-def last_tiles(masked, jobs, outputs, block_total):
+    )(*masked, *pieces, *before)
+
+
+def last_tiles(masked, jobs, first, outputs, block_total):
     cols, n = masked[0].shape[1], len(jobs)
     names, pieces, before, span, rows_of = split_jobs(jobs)
     n_in = len(pieces)
@@ -522,7 +526,7 @@
     def body(*refs):
         last_kernel(
             refs[:n], rows_of(refs[n:]), refs[n + n_in : 2 * n + n_in], *refs[2 * n + n_in + 2 :],
-            names=names, block_total=block_total,
+            names=names, first=first, block_total=block_total,
         )
 
     return pl.pallas_call(
@@ -567,7 +571,8 @@
         scalars, turned, "far", [far_head, far_tail], 0, total, None, (upper, lower), block_total
     )
 
-    y_tail = after(y_tail, made_y, made_far)
+    masked = mask_rows(scalars, own_t, ("relay", "last"), head, block_total)
+    y_tail = after(y_tail, made_y, made_far, masked[0])
     relay_tail = [send(piece, turn) for piece in pick(position, y_tail, far_tail, turns)]
     both_tail = send(y_tail, cores)
     relay_part, last_part, made_relay = pair_tiles(
@@ -580,9 +585,9 @@
     relay_tail[:2] = [after(piece, made_across, made_relay) for piece in relay_tail[:2]]
     last_tail = [send(piece, cores) for piece in relay_tail]
     jobs = [("relay", relay_tail[:-1], relay_part), ("last", last_tail[:-1], last_part)]
-    (relay_part, last_part), masked = add_rows(scalars, own_t, jobs, head, turns[-1], block_total)
+    relay_part, last_part = add_rows(masked, jobs)
     jobs = [("relay", relay_tail[-1:], relay_part), ("last", last_tail[-1:], last_part)]
-    upper, lower = last_tiles(masked, jobs, (upper, lower), block_total)
+    upper, lower = last_tiles(masked, jobs, sum(turns[:-1]), (upper, lower), block_total)
     return diagonal, upper, lower
 
 

time: 102 us -> 102 us (level)
  Pallas kernels: 27.5 us -> 35.3 us
  waiting for transfers between devices: 50.2 us -> 43.6 us
  starting transfers between devices: 19.9 us -> 18.6 us
    ppermute x15, waiting for transfers between devices: 50.2 us -> 43.6 us  [send(): return lax.ppermute(block, 'ao', level_route(block_total, moves))]
    pallas_call x3, Pallas kernels: 8.65 us -> 12.3 us  [pair_tiles(): pl.pallas_call(body, out_shape=tuple((jax.ShapeDtypeStruct(c.shape, c.dty...]
    pallas_call x1, Pallas kernels: 3.54 us -> 6.44 us  [core_tile(): pl.pallas_call(functools.partial(core_kernel, block_total=block_total), o...]
    ppermute x15, starting transfers between devices: 19.9 us -> 18.6 us  [send(): return lax.ppermute(block, 'ao', level_route(block_total, moves))]
    pallas_call x0 -> x1, Pallas kernels: none -> 1.12 us  [mask_rows(): pl.pallas_call(functools.partial(mask_kernel, names=names, low=low, block...]
  transfers between devices with their start and end apart: 15 -> 15, of which waited for: 7 -> 6; matrix products, arithmetic and copies ran while one was open for 0% -> 0% of each run, Pallas kernels for 26% -> 33%
where the time goes in v5:
time: 102 us; the launch traced here: 100 us
  waiting for transfers between devices  43.6 us (43%)
  Pallas kernels  35.3 us (35%)
  starting transfers between devices  18.6 us (18%)
  local copies, waits for them, and re-layouts  1.99 us (2%)
    ppermute x15, waiting for transfers between devices, send(): return lax.ppermute(block, 'ao', level_route(block_total, moves))  43.6 us
    ppermute x15, starting transfers between devices, send(): return lax.ppermute(block, 'ao', level_route(block_total, moves))  18.6 us
    pallas_call x3, Pallas kernels, pair_tiles(): pl.pallas_call(body, out_shape=tuple((jax.ShapeDtypeStruct(c.shape, c.dty...  12.3 us
    pallas_call x1, Pallas kernels, core_tile(): pl.pallas_call(functools.partial(core_kernel, block_total=block_total), o...  6.44 us
    pallas_call x1, Pallas kernels, own_tile(): pl.pallas_call(functools.partial(own_kernel, block_total=block_total), ou...  5.34 us
    pallas_call x2, Pallas kernels, rows_after(): pl.pallas_call(functools.partial(rows_kernel, low=low), out_shape=jax.Sha...  4.69 us
    pallas_call x1, Pallas kernels, end_tiles(): pl.pallas_call(body, out_shape=(*(jax.ShapeDtypeStruct(o.shape, o.dtype)...  2.08 us
  transfers between devices with their start and end apart: 15, of which 6 were waited for; matrix products, arithmetic and copies ran while one was open for 0% of the time, Pallas kernels for 33%

profile of v5, /device:TPU:5, one launch (start us, length us, event | category | flops | bytes accessed | tf_op | source)
XLA Modules:
  0.0 100.4 jit_solution(13095755738730184657)
XLA Ops:
  0.6 0.7 collective-permute-start.1
  1.4 2.3 %shard_map.60.refs_0_ = bf16[1536,512]{1,0:T(8,128)(2,1)} custom-call(bf16[3072,512]{1,0:T(8,128)(2,1)} %block_ref.3), custom_call_target="tpu_custom_call" | custom-call | tf_op jit(solution)/shard_map/pallas_call | solution.py:126
  3.7 0.0 copy-start.2
  3.7 0.0 copy-start.1
  3.7 0.1 collective-permute-start.2
  3.8 2.4 %shard_map.61 = bf16[1536,512]{1,0:T(8,128)(2,1)} custom-call(bf16[3072,512]{1,0:T(8,128)(2,1)} %block_ref.3, bf16[1536,512]{1,0:T(8,128)(2,1)} %shard_map.60.refs_0_), custom_call_target="tpu_custom_call" | custom-call | tf_op jit(solution)/shard_map/pallas_call | solution.py:126
  6.2 3.6 %collective-permute-start.4 = (bf16[1536,512]{1,0:T(8,128)(2,1)}, bf16[1536,512]{1,0:T(8,128)(2,1)S(1)}, u32[]{:S(2)}, u32[]{:S(2)}) collective-permute-start(bf16[1536,512]{1,0:T(8,128)(2,1)} %shard_map.61), channel_id=1, source_target_pairs={{1,4},{3,6},{5,8},{4,1},{7,10},{6,3},{9,12},{8,5},{11,14},{10,7},{... | collective-permute-start | bytes 4718600 | tf_op jit(solution)/shard_map/ppermute | solution.py:548
  9.8 2.0 %collective-permute-start.3 = (bf16[1536,512]{1,0:T(8,128)(2,1)}, bf16[1536,512]{1,0:T(8,128)(2,1)}, u32[]{:S(2)}, u32[]{:S(2)}) collective-permute-start(bf16[1536,512]{1,0:T(8,128)(2,1)} %shard_map.60.refs_0_), channel_id=1, source_target_pairs={{1,4},{3,6},{5,8},{4,1},{7,10},{6,3},{9,12},{8,5},{11,14},{10,7},{... | collective-permute-start | bytes 4718600 | tf_op jit(solution)/shard_map/ppermute | solution.py:548
  11.8 1.5 %collective-permute-start = (bf16[1536,512]{1,0:T(8,128)(2,1)}, bf16[1536,512]{1,0:T(8,128)(2,1)S(1)}, u32[]{:S(2)}, u32[]{:S(2)}) collective-permute-start(bf16[1536,512]{1,0:T(8,128)(2,1)} %shard_map.61), channel_id=1, source_target_pairs={{0,2},{1,3},{2,0},{3,1},{4,6},{5,7},{6,4},{7,5},{8,10},{9,11},{10,... | collective-permute-start | bytes 4718600 | tf_op jit(solution)/shard_map/ppermute | solution.py:548
  13.3 0.0 copy-done.2
  13.3 0.1 copy.16.sig_ref
  13.4 0.0 copy-done.1
  13.4 0.0 copy-start
  13.4 1.9 %copy-done = bf16[3072,512]{1,0:T(8,128)(2,1)S(1)} copy-done((bf16[3072,512]{1,0:T(8,128)(2,1)S(1)}, bf16[3072,512]{1,0:T(8,128)(2,1)}, u32[]{:S(2)}) %copy-start) | copy-done | bytes 3145752
  15.2 5.3 %shard_map.58 = (f32[1,512,512]{2,1,0:T(8,128)}, bf16[6,512,512]{2,1,0:T(8,128)(2,1)S(1)}) custom-call(s32[1]{0:T(128)} %bitcast.position_ref, s32[16]{0:T(128)S(1)} %copy-done.1, s32[16,3]{1,0:T(8,128)S(1)} %copy.16.sig_ref, bf16[3072,512]{1,0:T(8,128)(2,1)S(1)} %copy-done), custom_call_target="tpu_custom_call" | custom-call | flops 1610612736 | bytes 7340032 | tf_op jit(solution)/shard_map/pallas_call | solution.py:208
  20.6 0.0 collective-permute-done.1.core_ref
  20.6 6.4 %shard_map.62 = (f32[1,3,512,512]{3,2,1,0:T(8,128)}, f32[1,3,512,512]{3,2,1,0:T(8,128)}, bf16[6,512,512]{2,1,0:T(8,128)(2,1)S(1)}, f32[8,128]{1,0:T(8,128)S(1)}) custom-call(s32[1]{0:T(128)} %bitcast.position_ref, s32[16]{0:T(128)S(1)} %copy-done.1, s32[16,3]{1,0:T(8,128)S(1)} %copy.16.sig_ref, bf16[3072,512]{1,0:T(8,128)(2,1)} %collective-permute-done.1.core_ref, ...), custom_call_target="tpu_custom_call" | custom-call | flops 1610612736 | bytes 10485760 | tf_op jit(solution)/shard_map/pallas_call | solution.py:278
  27.1 13.1 %collective-permute-done.2.refs_0_ = bf16[1536,512]{1,0:T(8,128)(2,1)} collective-permute-done((bf16[1536,512]{1,0:T(8,128)(2,1)}, bf16[1536,512]{1,0:T(8,128)(2,1)}, u32[]{:S(2)}, u32[]{:S(2)}) %collective-permute-start.2) | collective-permute-done | bytes 1572896 | tf_op jit(solution)/shard_map/ppermute | solution.py:548
  40.1 1.3 %collective-permute-start.10 = (bf16[1536,512]{1,0:T(8,128)(2,1)}, bf16[1536,512]{1,0:T(8,128)(2,1)S(1)}, u32[]{:S(2)}, u32[]{:S(2)}) collective-permute-start(bf16[1536,512]{1,0:T(8,128)(2,1)} %shard_map.63.refs_0_), channel_id=1, source_target_pairs={{0,4},{1,5},{4,8},{5,9},{6,2},{7,3},{8,12},{9,13},{10,6},{11,7},{1... | collective-permute-start | bytes 4718600 | tf_op jit(solution)/shard_map/ppermute | solution.py:548
  41.4 1.1 %shard_map.59 = (bf16[3,512,512]{2,1,0:T(8,128)(2,1)S(1)}, bf16[3,512,512]{2,1,0:T(8,128)(2,1)S(1)}) custom-call(s32[1]{0:T(128)} %bitcast.position_ref, s32[16]{0:T(128)S(1)} %copy-done.1, s32[16,3]{1,0:T(8,128)S(1)} %copy.16.sig_ref, bf16[6,512,512]{2,1,0:T(8,128)(2,1)S(1)} %get-tuple-element.31.own_t_ref), custom_call_target="tpu_custom_call" | custom-call | tf_op jit(solution)/shard_map/pallas_call | solution.py:431
  42.5 3.9 %shard_map.64 = (f32[512,512]{1,0:T(8,128)S(1)}, f32[512,512]{1,0:T(8,128)S(1)}, f32[8,128]{1,0:T(8,128)S(1)}) custom-call(s32[1]{0:T(128)} %bitcast.position_ref, s32[16]{0:T(128)S(1)} %copy-done.1, s32[16,3]{1,0:T(8,128)S(1)} %copy.16.sig_ref, bf16[6,512,512]{2,1,0:T(8,128)(2,1)S(1)} %get-tuple-element.31.own_t_ref, ...), custom_call_target="tpu_custom_call" | custom-call | flops 1610612736 | bytes 8912896 | tf_op jit(solution)/shard_map/pallas_call | solution.py:378
  46.4 0.0 collective-permute-done.4.refs_1_.inner_ref
  46.4 0.0 collective-permute-done.3.refs_0_
  46.5 4.3 %shard_map.65 = (f32[1,3,512,512]{3,2,1,0:T(8,128)}, f32[1,3,512,512]{3,2,1,0:T(8,128)}, f32[8,128]{1,0:T(8,128)S(1)}) custom-call(s32[1]{0:T(128)} %bitcast.position_ref, s32[16]{0:T(128)S(1)} %copy-done.1, s32[16,3]{1,0:T(8,128)S(1)} %copy.16.sig_ref, ...), custom_call_target="tpu_custom_call", output_to_operand_aliasing={{0}: (7, {}), {1}: (8, {})} | custom-call | flops 3221225472 | bytes 13631488 | tf_op jit(solution)/shard_map/pallas_call | solution.py:378
  50.8 23.0 %collective-permute-done.refs_0_ = bf16[1536,512]{1,0:T(8,128)(2,1)S(1)} collective-permute-done((bf16[1536,512]{1,0:T(8,128)(2,1)}, bf16[1536,512]{1,0:T(8,128)(2,1)S(1)}, u32[]{:S(2)}, u32[]{:S(2)}) %collective-permute-start) | collective-permute-done | bytes 1572896 | tf_op jit(solution)/shard_map/ppermute | solution.py:548
  73.7 0.8 collective-permute-start.8
  74.5 0.0 collective-permute-start.9
  74.5 0.3 shard_map.67
  74.8 1.3 %collective-permute-start.11 = (bf16[512,512]{1,0:T(8,128)(2,1)S(1)}, bf16[512,512]{1,0:T(8,128)(2,1)S(1)}, u32[]{:S(2)}, u32[]{:S(2)}) collective-permute-start(bf16[512,512]{1,0:T(8,128)(2,1)S(1)} %get-tuple-element.48), channel_id=1, source_target_pairs={{0,4},{1,2},{2,1},{4,8},{7,3},{5,6},{6,5},{8,12},{11,7},{9,10},{10... | collective-permute-start | bytes 1572872 | tf_op jit(solution)/shard_map/ppermute | solution.py:548
  76.1 1.3 %collective-permute-start.7 = (bf16[512,512]{1,0:T(8,128)(2,1)S(1)}, bf16[512,512]{1,0:T(8,128)(2,1)S(1)}, u32[]{:S(2)}, u32[]{:S(2)}) collective-permute-start(bf16[512,512]{1,0:T(8,128)(2,1)S(1)} %get-tuple-element.41), channel_id=1, source_target_pairs={{0,4},{1,2},{2,1},{4,8},{7,3},{5,6},{6,5},{8,12},{11,7},{9,10},{10... | collective-permute-start | bytes 1572872 | tf_op jit(solution)/shard_map/ppermute | solution.py:548
  77.4 0.2 collective-permute-done.10.refs_0_
  77.6 4.1 %shard_map.69 = (f32[512,512]{1,0:T(8,128)S(1)}, f32[512,512]{1,0:T(8,128)S(1)}, f32[8,128]{1,0:T(8,128)S(1)}) custom-call(s32[1]{0:T(128)} %bitcast.position_ref, s32[16]{0:T(128)S(1)} %copy-done.1, s32[16,3]{1,0:T(8,128)S(1)} %copy.16.sig_ref, bf16[6,512,512]{2,1,0:T(8,128)(2,1)S(1)} %get-tuple-element.31.own_t_ref, ...), custom_call_target="tpu_custom_call" | custom-call | flops 1610612736 | bytes 8912896 | tf_op jit(solution)/shard_map/pallas_call | solution.py:378
  81.7 1.0 collective-permute-start.14
  82.7 0.0 collective-permute-done.9.refs_3_
  82.7 1.3 %collective-permute-start.5 = (bf16[512,512]{1,0:T(8,128)(2,1)S(1)}, bf16[512,512]{1,0:T(8,128)(2,1)S(1)}, u32[]{:S(2)}, u32[]{:S(2)}) collective-permute-start(bf16[512,512]{1,0:T(8,128)(2,1)S(1)} %get-tuple-element.40), channel_id=1, source_target_pairs={{0,4},{1,2},{2,1},{4,8},{7,3},{5,6},{6,5},{8,12},{11,7},{9,10},{10... | collective-permute-start | bytes 1572872 | tf_op jit(solution)/shard_map/ppermute | solution.py:548
  84.0 0.0 collective-permute-done.8.refs_1_
  84.0 2.1 %shard_map.68 = (f32[1,3,512,512]{3,2,1,0:T(8,128)}, f32[1,3,512,512]{3,2,1,0:T(8,128)}, f32[8,128]{1,0:T(8,128)S(1)}) custom-call(s32[1]{0:T(128)} %bitcast.position_ref, s32[16]{0:T(128)S(1)} %copy-done.1, s32[16,3]{1,0:T(8,128)S(1)} %copy.16.sig_ref, ...), custom_call_target="tpu_custom_call", output_to_operand_aliasing={{0}: (8, {}), {1}: (9, {})} | custom-call | flops 1610612736 | bytes 8912896 | tf_op jit(solution)/shard_map/pallas_call | solution.py:491
  86.1 0.0 collective-permute-done.11.refs_0_
  86.1 2.2 %collective-permute-start.13 = (bf16[512,512]{1,0:T(8,128)(2,1)S(1)}, bf16[512,512]{1,0:T(8,128)(2,1)S(1)}, u32[]{:S(2)}, u32[]{:S(2)}) collective-permute-start(bf16[512,512]{1,0:T(8,128)(2,1)S(1)} %shard_map.71.refs_3_), channel_id=1, source_target_pairs={{0,1},{1,0},{2,3},{3,2},{4,5},{5,4},{6,7},{7,6},{8,9},{9,8},{10,11... | collective-permute-start | bytes 1572872 | tf_op jit(solution)/shard_map/ppermute | solution.py:548
  88.3 2.3 %collective-permute-done.7.refs_0_ = bf16[512,512]{1,0:T(8,128)(2,1)S(1)} collective-permute-done((bf16[512,512]{1,0:T(8,128)(2,1)S(1)}, bf16[512,512]{1,0:T(8,128)(2,1)S(1)}, u32[]{:S(2)}, u32[]{:S(2)}) %collective-permute-start.7) | collective-permute-done | bytes 524320 | tf_op jit(solution)/shard_map/ppermute | solution.py:548
  90.7 0.8 collective-permute-start.12
  91.4 4.8 %collective-permute-done.5.refs_2_ = bf16[512,512]{1,0:T(8,128)(2,1)S(1)} collective-permute-done((bf16[512,512]{1,0:T(8,128)(2,1)S(1)}, bf16[512,512]{1,0:T(8,128)(2,1)S(1)}, u32[]{:S(2)}, u32[]{:S(2)}) %collective-permute-start.5) | collective-permute-done | bytes 524320 | tf_op jit(solution)/shard_map/ppermute | solution.py:548
  96.3 0.8 collective-permute-start.6
  97.1 0.0 collective-permute-done.13.refs_5_
  97.1 0.0 collective-permute-done.12.refs_4_
  97.1 0.0 collective-permute-done.14.refs_7_
  97.1 1.3 %shard_map.72 = (f32[512,512]{1,0:T(8,128)S(1)}, f32[512,512]{1,0:T(8,128)S(1)}) custom-call(bf16[3,512,512]{2,1,0:T(8,128)(2,1)S(1)} %get-tuple-element.32.refs_3_.refs_0_, bf16[3,512,512]{2,1,0:T(8,128)(2,1)S(1)} %get-tuple-element.33.refs_1_, bf16[512,512]{1,0:T(8,128)(2,1)S(1)} %shard_map.70.refs_2_, bf16[512,512]{1,0:T(8,128)(2,1)S(1)} %shard_map.71.refs_3_, ...), custom_call_target="tpu_custom_call" | custom-call | flops 1073741824 | bytes 7340032 | tf_op jit(solution)/shard_map/pallas_call | solution.py:511
  98.3 0.3 collective-permute-done.6.refs_3_
  98.6 1.8 %shard_map.73 = (f32[1,3,512,512]{3,2,1,0:T(8,128)}, f32[1,3,512,512]{3,2,1,0:T(8,128)}) custom-call(bf16[3,512,512]{2,1,0:T(8,128)(2,1)S(1)} %get-tuple-element.32.refs_3_.refs_0_, bf16[3,512,512]{2,1,0:T(8,128)(2,1)S(1)} %get-tuple-element.33.refs_1_, ...), custom_call_target="tpu_custom_call", output_to_operand_aliasing={{0}: (6, {}), {1}: (7, {})} | custom-call | flops 536870912 | bytes 5767168 | tf_op jit(solution)/shard_map/pallas_call | solution.py:532
  (4 shorter events, 0.0 us)
Async XLA Ops:
  0.6 20.0 %collective-permute-start.1 = (bf16[3072,512]{1,0:T(8,128)(2,1)}, bf16[3072,512]{1,0:T(8,128)(2,1)}, u32[]{:S(2)}, u32[]{:S(2)}) collective-permute-start(bf16[3072,512]{1,0:T(8,128)(2,1)} %block_ref.3), channel_id=1, source_target_pairs={{0,1},{1,0},{2,3},{3,2},{4,5},{5,4},{6,7},{7,6},{8,9},{9,8},{10,11... | collective-permute-start | bytes 9437192 | tf_op jit(solution)/shard_map/ppermute | solution.py:548
  3.7 9.6 %copy-start.2 = (s32[16,3]{0,1:T(4,128)S(1)}, s32[16,3]{0,1:T(4,128)}, u32[]{:S(2)}) copy-start(s32[16,3]{0,1:T(4,128)} %param.4) | copy-start | bytes 580
  3.7 9.6 %copy-start.1 = (s32[16]{0:T(128)S(1)}, s32[16]{0:T(128)}, u32[]{:S(2)}) copy-start(s32[16]{0:T(128)} %live_ref.13) | copy-start | bytes 196
  3.7 36.4 %collective-permute-start.2 = (bf16[1536,512]{1,0:T(8,128)(2,1)}, bf16[1536,512]{1,0:T(8,128)(2,1)}, u32[]{:S(2)}, u32[]{:S(2)}) collective-permute-start(bf16[1536,512]{1,0:T(8,128)(2,1)} %shard_map.60.refs_0_), channel_id=1, source_target_pairs={{0,2},{1,3},{2,0},{3,1},{4,6},{5,7},{6,4},{7,5},{8,10},{9,11},{10,... | collective-permute-start | bytes 4718600 | tf_op jit(solution)/shard_map/ppermute | solution.py:548
  6.2 40.3 %collective-permute-start.4 = (bf16[1536,512]{1,0:T(8,128)(2,1)}, bf16[1536,512]{1,0:T(8,128)(2,1)S(1)}, u32[]{:S(2)}, u32[]{:S(2)}) collective-permute-start(bf16[1536,512]{1,0:T(8,128)(2,1)} %shard_map.61), channel_id=1, source_target_pairs={{1,4},{3,6},{5,8},{4,1},{7,10},{6,3},{9,12},{8,5},{11,14},{10,7},{... | collective-permute-start | bytes 4718600 | tf_op jit(solution)/shard_map/ppermute | solution.py:548
  9.8 36.7 %collective-permute-start.3 = (bf16[1536,512]{1,0:T(8,128)(2,1)}, bf16[1536,512]{1,0:T(8,128)(2,1)}, u32[]{:S(2)}, u32[]{:S(2)}) collective-permute-start(bf16[1536,512]{1,0:T(8,128)(2,1)} %shard_map.60.refs_0_), channel_id=1, source_target_pairs={{1,4},{3,6},{5,8},{4,1},{7,10},{6,3},{9,12},{8,5},{11,14},{10,7},{... | collective-permute-start | bytes 4718600 | tf_op jit(solution)/shard_map/ppermute | solution.py:548
  11.8 62.0 %collective-permute-start = (bf16[1536,512]{1,0:T(8,128)(2,1)}, bf16[1536,512]{1,0:T(8,128)(2,1)S(1)}, u32[]{:S(2)}, u32[]{:S(2)}) collective-permute-start(bf16[1536,512]{1,0:T(8,128)(2,1)} %shard_map.61), channel_id=1, source_target_pairs={{0,2},{1,3},{2,0},{3,1},{4,6},{5,7},{6,4},{7,5},{8,10},{9,11},{10,... | collective-permute-start | bytes 4718600 | tf_op jit(solution)/shard_map/ppermute | solution.py:548
  13.4 1.9 %copy-start = (bf16[3072,512]{1,0:T(8,128)(2,1)S(1)}, bf16[3072,512]{1,0:T(8,128)(2,1)}, u32[]{:S(2)}) copy-start(bf16[3072,512]{1,0:T(8,128)(2,1)} %block_ref.3) | copy-start | bytes 9437188
  40.1 37.5 %collective-permute-start.10 = (bf16[1536,512]{1,0:T(8,128)(2,1)}, bf16[1536,512]{1,0:T(8,128)(2,1)S(1)}, u32[]{:S(2)}, u32[]{:S(2)}) collective-permute-start(bf16[1536,512]{1,0:T(8,128)(2,1)} %shard_map.63.refs_0_), channel_id=1, source_target_pairs={{0,4},{1,5},{4,8},{5,9},{6,2},{7,3},{8,12},{9,13},{10,6},{11,7},{1... | collective-permute-start | bytes 4718600 | tf_op jit(solution)/shard_map/ppermute | solution.py:548
  73.7 10.3 %collective-permute-start.8 = (bf16[1536,512]{1,0:T(8,128)(2,1)S(1)}, bf16[1536,512]{1,0:T(8,128)(2,1)S(1)}, u32[]{:S(2)}, u32[]{:S(2)}) collective-permute-start(bf16[1536,512]{1,0:T(8,128)(2,1)S(1)} %shard_map.66.edge_ref.refs_0_), channel_id=1, source_target_pairs={{0,1},{1,0},{2,3},{3,2},{4,5},{5,4},{6,7},{7,6},{8,9},{9,8},{10,11... | collective-permute-start | bytes 4718600 | tf_op jit(solution)/shard_map/ppermute | solution.py:548
  74.5 8.2 %collective-permute-start.9 = (f32[512,512]{1,0:T(8,128)S(1)}, f32[512,512]{1,0:T(8,128)S(1)}, u32[]{:S(2)}, u32[]{:S(2)}) collective-permute-start(f32[512,512]{1,0:T(8,128)S(1)} %get-tuple-element.43), channel_id=1, source_target_pairs={{0,1},{1,0},{2,3},{3,2},{4,5},{5,4},{6,7},{7,6},{8,9},{9,8},{10,11... | collective-permute-start | bytes 3145736 | tf_op jit(solution)/shard_map/ppermute | solution.py:548
  74.8 11.3 %collective-permute-start.11 = (bf16[512,512]{1,0:T(8,128)(2,1)S(1)}, bf16[512,512]{1,0:T(8,128)(2,1)S(1)}, u32[]{:S(2)}, u32[]{:S(2)}) collective-permute-start(bf16[512,512]{1,0:T(8,128)(2,1)S(1)} %get-tuple-element.48), channel_id=1, source_target_pairs={{0,4},{1,2},{2,1},{4,8},{7,3},{5,6},{6,5},{8,12},{11,7},{9,10},{10... | collective-permute-start | bytes 1572872 | tf_op jit(solution)/shard_map/ppermute | solution.py:548
  76.1 14.5 %collective-permute-start.7 = (bf16[512,512]{1,0:T(8,128)(2,1)S(1)}, bf16[512,512]{1,0:T(8,128)(2,1)S(1)}, u32[]{:S(2)}, u32[]{:S(2)}) collective-permute-start(bf16[512,512]{1,0:T(8,128)(2,1)S(1)} %get-tuple-element.41), channel_id=1, source_target_pairs={{0,4},{1,2},{2,1},{4,8},{7,3},{5,6},{6,5},{8,12},{11,7},{9,10},{10... | collective-permute-start | bytes 1572872 | tf_op jit(solution)/shard_map/ppermute | solution.py:548
  81.7 15.4 %collective-permute-start.14 = (f32[512,512]{1,0:T(8,128)S(1)}, f32[512,512]{1,0:T(8,128)S(1)}, u32[]{:S(2)}, u32[]{:S(2)}) collective-permute-start(f32[512,512]{1,0:T(8,128)S(1)} %get-tuple-element.50), channel_id=1, source_target_pairs={{0,1},{1,0},{2,3},{3,2},{4,5},{5,4},{6,7},{7,6},{8,9},{9,8},{10,11... | collective-permute-start | bytes 3145736 | tf_op jit(solution)/shard_map/ppermute | solution.py:548
  82.7 13.6 %collective-permute-start.5 = (bf16[512,512]{1,0:T(8,128)(2,1)S(1)}, bf16[512,512]{1,0:T(8,128)(2,1)S(1)}, u32[]{:S(2)}, u32[]{:S(2)}) collective-permute-start(bf16[512,512]{1,0:T(8,128)(2,1)S(1)} %get-tuple-element.40), channel_id=1, source_target_pairs={{0,4},{1,2},{2,1},{4,8},{7,3},{5,6},{6,5},{8,12},{11,7},{9,10},{10... | collective-permute-start | bytes 1572872 | tf_op jit(solution)/shard_map/ppermute | solution.py:548
  86.1 11.0 %collective-permute-start.13 = (bf16[512,512]{1,0:T(8,128)(2,1)S(1)}, bf16[512,512]{1,0:T(8,128)(2,1)S(1)}, u32[]{:S(2)}, u32[]{:S(2)}) collective-permute-start(bf16[512,512]{1,0:T(8,128)(2,1)S(1)} %shard_map.71.refs_3_), channel_id=1, source_target_pairs={{0,1},{1,0},{2,3},{3,2},{4,5},{5,4},{6,7},{7,6},{8,9},{9,8},{10,11... | collective-permute-start | bytes 1572872 | tf_op jit(solution)/shard_map/ppermute | solution.py:548
  90.7 6.4 %collective-permute-start.12 = (bf16[512,512]{1,0:T(8,128)(2,1)S(1)}, bf16[512,512]{1,0:T(8,128)(2,1)S(1)}, u32[]{:S(2)}, u32[]{:S(2)}) collective-permute-start(bf16[512,512]{1,0:T(8,128)(2,1)S(1)} %shard_map.70.refs_2_), channel_id=1, source_target_pairs={{0,1},{1,0},{2,3},{3,2},{4,5},{5,4},{6,7},{7,6},{8,9},{9,8},{10,11... | collective-permute-start | bytes 1572872 | tf_op jit(solution)/shard_map/ppermute | solution.py:548
  96.3 2.3 %collective-permute-start.6 = (bf16[512,512]{1,0:T(8,128)(2,1)S(1)}, bf16[512,512]{1,0:T(8,128)(2,1)S(1)}, u32[]{:S(2)}, u32[]{:S(2)}) collective-permute-start(bf16[512,512]{1,0:T(8,128)(2,1)S(1)} %collective-permute-done.5.refs_2_), channel_id=1, source_target_pairs={{0,1},{1,0},{2,3},{3,2},{4,5},{5,4},{6,7},{7,6},{8,9},{9,8},{10,11... | collective-permute-start | bytes 1572872 | tf_op jit(solution)/shard_map/ppermute | solution.py:548

commit v6 on v5

--- a/solution.py
+++ b/solution.py
@@ -555,10 +555,10 @@
 
     first = rows_after(b_half, 0, head)
     y_head = send(first, across)
-    later = rows_after(b_half, head, total - head, first)
+    core = send(b_half, cores)
+    later = rows_after(b_half, head, total - head, first, core)
     y_tail = send(later, across)
     far_head, far_tail = send(first, far), send(later, far)
-    core = send(b_half, cores)
 
     diagonal, own_t = own_tile(scalars, b_half, block_total)
     upper, lower, core_t, made_core = core_tile(scalars, core, own_t, block_total)

time: 102 us -> 102 us (level)
  Pallas kernels: 35.3 us -> 24.8 us
  waiting for transfers between devices: 43.6 us -> 51.5 us
  starting transfers between devices: 18.6 us -> 21.2 us
    ppermute x15, waiting for transfers between devices: 43.6 us -> 51.5 us  [send(): return lax.ppermute(block, 'ao', level_route(block_total, moves))]
    pallas_call x3, Pallas kernels: 12.3 us -> 6.35 us  [pair_tiles(): pl.pallas_call(body, out_shape=tuple((jax.ShapeDtypeStruct(c.shape, c.dty...]
    pallas_call x1, Pallas kernels: 5.34 us -> 2.55 us  [own_tile(): pl.pallas_call(functools.partial(own_kernel, block_total=block_total), ou...]
    ppermute x15, starting transfers between devices: 18.6 us -> 21.2 us  [send(): return lax.ppermute(block, 'ao', level_route(block_total, moves))]
    pallas_call x1, Pallas kernels: 6.44 us -> 4.71 us  [core_tile(): pl.pallas_call(functools.partial(core_kernel, block_total=block_total), o...]
  transfers between devices with their start and end apart: 15 -> 15, of which waited for: 6 -> 5; matrix products, arithmetic and copies ran while one was open for 0% -> 0% of each run, Pallas kernels for 33% -> 23%
where the time goes in v6:
time: 102 us; the launch traced here: 100 us
  waiting for transfers between devices  51.5 us (50%)
  Pallas kernels  24.8 us (24%)
  starting transfers between devices  21.2 us (21%)
  local copies, waits for them, and re-layouts  1.99 us (2%)
    ppermute x15, waiting for transfers between devices, send(): return lax.ppermute(block, 'ao', level_route(block_total, moves))  51.5 us
    ppermute x15, starting transfers between devices, send(): return lax.ppermute(block, 'ao', level_route(block_total, moves))  21.2 us
    pallas_call x3, Pallas kernels, pair_tiles(): pl.pallas_call(body, out_shape=tuple((jax.ShapeDtypeStruct(c.shape, c.dty...  6.35 us
    pallas_call x1, Pallas kernels, core_tile(): pl.pallas_call(functools.partial(core_kernel, block_total=block_total), o...  4.71 us
    pallas_call x2, Pallas kernels, rows_after(): pl.pallas_call(functools.partial(rows_kernel, low=low), out_shape=jax.Sha...  4.69 us
    pallas_call x1, Pallas kernels, own_tile(): pl.pallas_call(functools.partial(own_kernel, block_total=block_total), ou...  2.55 us
    pallas_call x1, Pallas kernels, end_tiles(): pl.pallas_call(body, out_shape=(*(jax.ShapeDtypeStruct(o.shape, o.dtype)...  2.08 us
  transfers between devices with their start and end apart: 15, of which 5 were waited for; matrix products, arithmetic and copies ran while one was open for 0% of the time, Pallas kernels for 23%

profile of v6, /device:TPU:5, one launch (start us, length us, event | category | flops | bytes accessed | tf_op | source)
XLA Modules:
  0.0 100.4 jit_solution(8707139628952282058)
XLA Ops:
  0.6 0.7 collective-permute-start
  1.4 2.3 %shard_map.60.refs_0_ = bf16[1536,512]{1,0:T(8,128)(2,1)} custom-call(bf16[3072,512]{1,0:T(8,128)(2,1)} %block_ref.3), custom_call_target="tpu_custom_call" | custom-call | tf_op jit(solution)/shard_map/pallas_call | solution.py:126
  3.7 0.0 copy-start.2
  3.7 0.0 copy-start.1
  3.7 0.1 collective-permute-start.2
  3.8 3.6 %collective-permute-start.3 = (bf16[1536,512]{1,0:T(8,128)(2,1)}, bf16[1536,512]{1,0:T(8,128)(2,1)}, u32[]{:S(2)}, u32[]{:S(2)}) collective-permute-start(bf16[1536,512]{1,0:T(8,128)(2,1)} %shard_map.60.refs_0_), channel_id=1, source_target_pairs={{1,4},{3,6},{5,8},{4,1},{7,10},{6,3},{9,12},{8,5},{11,14},{10,7},{... | collective-permute-start | bytes 4718600 | tf_op jit(solution)/shard_map/ppermute | solution.py:548
  7.4 0.0 collective-permute-done.refs_1_.core_ref
  7.4 2.4 %shard_map.61 = bf16[1536,512]{1,0:T(8,128)(2,1)} custom-call(bf16[3072,512]{1,0:T(8,128)(2,1)} %block_ref.3, bf16[1536,512]{1,0:T(8,128)(2,1)} %shard_map.60.refs_0_, bf16[3072,512]{1,0:T(8,128)(2,1)} %collective-permute-done.refs_1_.core_ref), custom_call_target="tpu_custom_call" | custom-call | tf_op jit(solution)/shard_map/pallas_call | solution.py:126
  9.8 3.0 %collective-permute-start.4 = (bf16[1536,512]{1,0:T(8,128)(2,1)}, bf16[1536,512]{1,0:T(8,128)(2,1)S(1)}, u32[]{:S(2)}, u32[]{:S(2)}) collective-permute-start(bf16[1536,512]{1,0:T(8,128)(2,1)} %shard_map.61), channel_id=1, source_target_pairs={{1,4},{3,6},{5,8},{4,1},{7,10},{6,3},{9,12},{8,5},{11,14},{10,7},{... | collective-permute-start | bytes 4718600 | tf_op jit(solution)/shard_map/ppermute | solution.py:548
  12.8 0.4 collective-permute-start.1
  13.3 0.0 copy-done.2
  13.3 0.1 copy.16.sig_ref
  13.4 0.0 copy-done.1
  13.4 0.0 copy-start
  13.4 1.9 %copy-done = bf16[3072,512]{1,0:T(8,128)(2,1)S(1)} copy-done((bf16[3072,512]{1,0:T(8,128)(2,1)S(1)}, bf16[3072,512]{1,0:T(8,128)(2,1)}, u32[]{:S(2)}) %copy-start) | copy-done | bytes 3145752
  15.3 2.6 %shard_map.58 = (f32[1,512,512]{2,1,0:T(8,128)}, bf16[6,512,512]{2,1,0:T(8,128)(2,1)S(1)}) custom-call(s32[1]{0:T(128)} %bitcast.position_ref, s32[16]{0:T(128)S(1)} %copy-done.1, s32[16,3]{1,0:T(8,128)S(1)} %copy.16.sig_ref, bf16[3072,512]{1,0:T(8,128)(2,1)S(1)} %copy-done), custom_call_target="tpu_custom_call" | custom-call | flops 1610612736 | bytes 7340032 | tf_op jit(solution)/shard_map/pallas_call | solution.py:208
  17.8 4.7 %shard_map.62 = (f32[1,3,512,512]{3,2,1,0:T(8,128)}, f32[1,3,512,512]{3,2,1,0:T(8,128)}, bf16[6,512,512]{2,1,0:T(8,128)(2,1)S(1)}, f32[8,128]{1,0:T(8,128)S(1)}) custom-call(s32[1]{0:T(128)} %bitcast.position_ref, s32[16]{0:T(128)S(1)} %copy-done.1, s32[16,3]{1,0:T(8,128)S(1)} %copy.16.sig_ref, bf16[3072,512]{1,0:T(8,128)(2,1)} %collective-permute-done.refs_1_.core_ref, ...), custom_call_target="tpu_custom_call" | custom-call | flops 1610612736 | bytes 10485760 | tf_op jit(solution)/shard_map/pallas_call | solution.py:278
  22.5 17.6 %collective-permute-done.2.refs_0_ = bf16[1536,512]{1,0:T(8,128)(2,1)} collective-permute-done((bf16[1536,512]{1,0:T(8,128)(2,1)}, bf16[1536,512]{1,0:T(8,128)(2,1)}, u32[]{:S(2)}, u32[]{:S(2)}) %collective-permute-start.2) | collective-permute-done | bytes 1572896 | tf_op jit(solution)/shard_map/ppermute | solution.py:548
  40.1 1.3 %collective-permute-start.10 = (bf16[1536,512]{1,0:T(8,128)(2,1)}, bf16[1536,512]{1,0:T(8,128)(2,1)S(1)}, u32[]{:S(2)}, u32[]{:S(2)}) collective-permute-start(bf16[1536,512]{1,0:T(8,128)(2,1)} %shard_map.63.refs_0_), channel_id=1, source_target_pairs={{0,4},{1,5},{4,8},{5,9},{6,2},{7,3},{8,12},{9,13},{10,6},{11,7},{1... | collective-permute-start | bytes 4718600 | tf_op jit(solution)/shard_map/ppermute | solution.py:548
  41.4 1.1 %shard_map.59 = (bf16[3,512,512]{2,1,0:T(8,128)(2,1)S(1)}, bf16[3,512,512]{2,1,0:T(8,128)(2,1)S(1)}) custom-call(s32[1]{0:T(128)} %bitcast.position_ref, s32[16]{0:T(128)S(1)} %copy-done.1, s32[16,3]{1,0:T(8,128)S(1)} %copy.16.sig_ref, bf16[6,512,512]{2,1,0:T(8,128)(2,1)S(1)} %get-tuple-element.31.own_t_ref), custom_call_target="tpu_custom_call" | custom-call | tf_op jit(solution)/shard_map/pallas_call | solution.py:431
  42.5 1.2 %shard_map.64 = (f32[512,512]{1,0:T(8,128)S(1)}, f32[512,512]{1,0:T(8,128)S(1)}, f32[8,128]{1,0:T(8,128)S(1)}) custom-call(s32[1]{0:T(128)} %bitcast.position_ref, s32[16]{0:T(128)S(1)} %copy-done.1, s32[16,3]{1,0:T(8,128)S(1)} %copy.16.sig_ref, bf16[6,512,512]{2,1,0:T(8,128)(2,1)S(1)} %get-tuple-element.31.own_t_ref, ...), custom_call_target="tpu_custom_call" | custom-call | flops 1610612736 | bytes 8912896 | tf_op jit(solution)/shard_map/pallas_call | solution.py:378
  43.7 0.0 collective-permute-done.3.refs_0_
  43.8 0.0 collective-permute-done.4.refs_1_.inner_ref
  43.8 3.4 %shard_map.65 = (f32[1,3,512,512]{3,2,1,0:T(8,128)}, f32[1,3,512,512]{3,2,1,0:T(8,128)}, f32[8,128]{1,0:T(8,128)S(1)}) custom-call(s32[1]{0:T(128)} %bitcast.position_ref, s32[16]{0:T(128)S(1)} %copy-done.1, s32[16,3]{1,0:T(8,128)S(1)} %copy.16.sig_ref, ...), custom_call_target="tpu_custom_call", output_to_operand_aliasing={{0}: (7, {}), {1}: (8, {})} | custom-call | flops 3221225472 | bytes 13631488 | tf_op jit(solution)/shard_map/pallas_call | solution.py:378
  47.2 26.5 %collective-permute-done.1.refs_0_ = bf16[1536,512]{1,0:T(8,128)(2,1)S(1)} collective-permute-done((bf16[1536,512]{1,0:T(8,128)(2,1)}, bf16[1536,512]{1,0:T(8,128)(2,1)S(1)}, u32[]{:S(2)}, u32[]{:S(2)}) %collective-permute-start.1) | collective-permute-done | bytes 1572896 | tf_op jit(solution)/shard_map/ppermute | solution.py:548
  73.7 0.8 collective-permute-start.8
  74.5 0.0 collective-permute-start.9
  74.5 0.3 shard_map.67
  74.8 1.3 %collective-permute-start.11 = (bf16[512,512]{1,0:T(8,128)(2,1)S(1)}, bf16[512,512]{1,0:T(8,128)(2,1)S(1)}, u32[]{:S(2)}, u32[]{:S(2)}) collective-permute-start(bf16[512,512]{1,0:T(8,128)(2,1)S(1)} %get-tuple-element.48), channel_id=1, source_target_pairs={{0,4},{1,2},{2,1},{4,8},{7,3},{5,6},{6,5},{8,12},{11,7},{9,10},{10... | collective-permute-start | bytes 1572872 | tf_op jit(solution)/shard_map/ppermute | solution.py:548
  76.1 1.3 %collective-permute-start.7 = (bf16[512,512]{1,0:T(8,128)(2,1)S(1)}, bf16[512,512]{1,0:T(8,128)(2,1)S(1)}, u32[]{:S(2)}, u32[]{:S(2)}) collective-permute-start(bf16[512,512]{1,0:T(8,128)(2,1)S(1)} %get-tuple-element.41), channel_id=1, source_target_pairs={{0,4},{1,2},{2,1},{4,8},{7,3},{5,6},{6,5},{8,12},{11,7},{9,10},{10... | collective-permute-start | bytes 1572872 | tf_op jit(solution)/shard_map/ppermute | solution.py:548
  77.4 0.0 collective-permute-done.10.refs_0_
  77.4 1.7 %shard_map.69 = (f32[512,512]{1,0:T(8,128)S(1)}, f32[512,512]{1,0:T(8,128)S(1)}, f32[8,128]{1,0:T(8,128)S(1)}) custom-call(s32[1]{0:T(128)} %bitcast.position_ref, s32[16]{0:T(128)S(1)} %copy-done.1, s32[16,3]{1,0:T(8,128)S(1)} %copy.16.sig_ref, bf16[6,512,512]{2,1,0:T(8,128)(2,1)S(1)} %get-tuple-element.31.own_t_ref, ...), custom_call_target="tpu_custom_call" | custom-call | flops 1610612736 | bytes 8912896 | tf_op jit(solution)/shard_map/pallas_call | solution.py:378
  79.1 5.0 %collective-permute-start.14 = (f32[512,512]{1,0:T(8,128)S(1)}, f32[512,512]{1,0:T(8,128)S(1)}, u32[]{:S(2)}, u32[]{:S(2)}) collective-permute-start(f32[512,512]{1,0:T(8,128)S(1)} %get-tuple-element.50), channel_id=1, source_target_pairs={{0,1},{1,0},{2,3},{3,2},{4,5},{5,4},{6,7},{7,6},{8,9},{9,8},{10,11... | collective-permute-start | bytes 3145736 | tf_op jit(solution)/shard_map/ppermute | solution.py:548
  84.2 0.0 collective-permute-done.9.refs_3_
  84.2 1.3 %collective-permute-start.5 = (bf16[512,512]{1,0:T(8,128)(2,1)S(1)}, bf16[512,512]{1,0:T(8,128)(2,1)S(1)}, u32[]{:S(2)}, u32[]{:S(2)}) collective-permute-start(bf16[512,512]{1,0:T(8,128)(2,1)S(1)} %get-tuple-element.40), channel_id=1, source_target_pairs={{0,4},{1,2},{2,1},{4,8},{7,3},{5,6},{6,5},{8,12},{11,7},{9,10},{10... | collective-permute-start | bytes 1572872 | tf_op jit(solution)/shard_map/ppermute | solution.py:548
  85.5 0.0 collective-permute-done.8.refs_1_
  85.5 2.1 %shard_map.68 = (f32[1,3,512,512]{3,2,1,0:T(8,128)}, f32[1,3,512,512]{3,2,1,0:T(8,128)}, f32[8,128]{1,0:T(8,128)S(1)}) custom-call(s32[1]{0:T(128)} %bitcast.position_ref, s32[16]{0:T(128)S(1)} %copy-done.1, s32[16,3]{1,0:T(8,128)S(1)} %copy.16.sig_ref, ...), custom_call_target="tpu_custom_call", output_to_operand_aliasing={{0}: (8, {}), {1}: (9, {})} | custom-call | flops 1610612736 | bytes 8912896 | tf_op jit(solution)/shard_map/pallas_call | solution.py:491
  87.6 0.0 collective-permute-done.11.refs_0_
  87.6 0.8 collective-permute-start.13
  88.3 2.3 %collective-permute-done.7.refs_0_ = bf16[512,512]{1,0:T(8,128)(2,1)S(1)} collective-permute-done((bf16[512,512]{1,0:T(8,128)(2,1)S(1)}, bf16[512,512]{1,0:T(8,128)(2,1)S(1)}, u32[]{:S(2)}, u32[]{:S(2)}) %collective-permute-start.7) | collective-permute-done | bytes 524320 | tf_op jit(solution)/shard_map/ppermute | solution.py:548
  90.7 0.8 collective-permute-start.12
  91.4 4.8 %collective-permute-done.5.refs_2_ = bf16[512,512]{1,0:T(8,128)(2,1)S(1)} collective-permute-done((bf16[512,512]{1,0:T(8,128)(2,1)S(1)}, bf16[512,512]{1,0:T(8,128)(2,1)S(1)}, u32[]{:S(2)}, u32[]{:S(2)}) %collective-permute-start.5) | collective-permute-done | bytes 524320 | tf_op jit(solution)/shard_map/ppermute | solution.py:548
  96.3 0.8 collective-permute-start.6
  97.1 0.0 collective-permute-done.14.refs_7_
  97.1 0.0 collective-permute-done.13.refs_5_
  97.1 0.0 collective-permute-done.12.refs_4_
  97.1 1.3 %shard_map.72 = (f32[512,512]{1,0:T(8,128)S(1)}, f32[512,512]{1,0:T(8,128)S(1)}) custom-call(bf16[3,512,512]{2,1,0:T(8,128)(2,1)S(1)} %get-tuple-element.32.refs_3_.refs_0_, bf16[3,512,512]{2,1,0:T(8,128)(2,1)S(1)} %get-tuple-element.33.refs_1_, bf16[512,512]{1,0:T(8,128)(2,1)S(1)} %shard_map.70.refs_2_, bf16[512,512]{1,0:T(8,128)(2,1)S(1)} %shard_map.71.refs_3_, ...), custom_call_target="tpu_custom_call" | custom-call | flops 1073741824 | bytes 7340032 | tf_op jit(solution)/shard_map/pallas_call | solution.py:511
  98.3 0.3 collective-permute-done.6.refs_3_
  98.6 1.8 %shard_map.73 = (f32[1,3,512,512]{3,2,1,0:T(8,128)}, f32[1,3,512,512]{3,2,1,0:T(8,128)}) custom-call(bf16[3,512,512]{2,1,0:T(8,128)(2,1)S(1)} %get-tuple-element.32.refs_3_.refs_0_, bf16[3,512,512]{2,1,0:T(8,128)(2,1)S(1)} %get-tuple-element.33.refs_1_, ...), custom_call_target="tpu_custom_call", output_to_operand_aliasing={{0}: (6, {}), {1}: (7, {})} | custom-call | flops 536870912 | bytes 5767168 | tf_op jit(solution)/shard_map/pallas_call | solution.py:532
  (4 shorter events, 0.0 us)
Async XLA Ops:
  0.6 6.8 %collective-permute-start = (bf16[3072,512]{1,0:T(8,128)(2,1)}, bf16[3072,512]{1,0:T(8,128)(2,1)}, u32[]{:S(2)}, u32[]{:S(2)}) collective-permute-start(bf16[3072,512]{1,0:T(8,128)(2,1)} %block_ref.3), channel_id=1, source_target_pairs={{0,1},{1,0},{2,3},{3,2},{4,5},{5,4},{6,7},{7,6},{8,9},{9,8},{10,11... | collective-permute-start | bytes 9437192 | tf_op jit(solution)/shard_map/ppermute | solution.py:548
  3.7 9.6 %copy-start.2 = (s32[16,3]{0,1:T(4,128)S(1)}, s32[16,3]{0,1:T(4,128)}, u32[]{:S(2)}) copy-start(s32[16,3]{0,1:T(4,128)} %param.4) | copy-start | bytes 580
  3.7 9.6 %copy-start.1 = (s32[16]{0:T(128)S(1)}, s32[16]{0:T(128)}, u32[]{:S(2)}) copy-start(s32[16]{0:T(128)} %live_ref.13) | copy-start | bytes 196
  3.7 36.4 %collective-permute-start.2 = (bf16[1536,512]{1,0:T(8,128)(2,1)}, bf16[1536,512]{1,0:T(8,128)(2,1)}, u32[]{:S(2)}, u32[]{:S(2)}) collective-permute-start(bf16[1536,512]{1,0:T(8,128)(2,1)} %shard_map.60.refs_0_), channel_id=1, source_target_pairs={{0,2},{1,3},{2,0},{3,1},{4,6},{5,7},{6,4},{7,5},{8,10},{9,11},{10,... | collective-permute-start | bytes 4718600 | tf_op jit(solution)/shard_map/ppermute | solution.py:548
  3.8 39.9 %collective-permute-start.3 = (bf16[1536,512]{1,0:T(8,128)(2,1)}, bf16[1536,512]{1,0:T(8,128)(2,1)}, u32[]{:S(2)}, u32[]{:S(2)}) collective-permute-start(bf16[1536,512]{1,0:T(8,128)(2,1)} %shard_map.60.refs_0_), channel_id=1, source_target_pairs={{1,4},{3,6},{5,8},{4,1},{7,10},{6,3},{9,12},{8,5},{11,14},{10,7},{... | collective-permute-start | bytes 4718600 | tf_op jit(solution)/shard_map/ppermute | solution.py:548
  9.8 34.0 %collective-permute-start.4 = (bf16[1536,512]{1,0:T(8,128)(2,1)}, bf16[1536,512]{1,0:T(8,128)(2,1)S(1)}, u32[]{:S(2)}, u32[]{:S(2)}) collective-permute-start(bf16[1536,512]{1,0:T(8,128)(2,1)} %shard_map.61), channel_id=1, source_target_pairs={{1,4},{3,6},{5,8},{4,1},{7,10},{6,3},{9,12},{8,5},{11,14},{10,7},{... | collective-permute-start | bytes 4718600 | tf_op jit(solution)/shard_map/ppermute | solution.py:548
  12.8 60.9 %collective-permute-start.1 = (bf16[1536,512]{1,0:T(8,128)(2,1)}, bf16[1536,512]{1,0:T(8,128)(2,1)S(1)}, u32[]{:S(2)}, u32[]{:S(2)}) collective-permute-start(bf16[1536,512]{1,0:T(8,128)(2,1)} %shard_map.61), channel_id=1, source_target_pairs={{0,2},{1,3},{2,0},{3,1},{4,6},{5,7},{6,4},{7,5},{8,10},{9,11},{10,... | collective-permute-start | bytes 4718600 | tf_op jit(solution)/shard_map/ppermute | solution.py:548
  13.4 1.9 %copy-start = (bf16[3072,512]{1,0:T(8,128)(2,1)S(1)}, bf16[3072,512]{1,0:T(8,128)(2,1)}, u32[]{:S(2)}) copy-start(bf16[3072,512]{1,0:T(8,128)(2,1)} %block_ref.3) | copy-start | bytes 9437188
  40.1 37.3 %collective-permute-start.10 = (bf16[1536,512]{1,0:T(8,128)(2,1)}, bf16[1536,512]{1,0:T(8,128)(2,1)S(1)}, u32[]{:S(2)}, u32[]{:S(2)}) collective-permute-start(bf16[1536,512]{1,0:T(8,128)(2,1)} %shard_map.63.refs_0_), channel_id=1, source_target_pairs={{0,4},{1,5},{4,8},{5,9},{6,2},{7,3},{8,12},{9,13},{10,6},{11,7},{1... | collective-permute-start | bytes 4718600 | tf_op jit(solution)/shard_map/ppermute | solution.py:548
  73.7 11.7 %collective-permute-start.8 = (bf16[1536,512]{1,0:T(8,128)(2,1)S(1)}, bf16[1536,512]{1,0:T(8,128)(2,1)S(1)}, u32[]{:S(2)}, u32[]{:S(2)}) collective-permute-start(bf16[1536,512]{1,0:T(8,128)(2,1)S(1)} %shard_map.66.edge_ref.refs_0_), channel_id=1, source_target_pairs={{0,1},{1,0},{2,3},{3,2},{4,5},{5,4},{6,7},{7,6},{8,9},{9,8},{10,11... | collective-permute-start | bytes 4718600 | tf_op jit(solution)/shard_map/ppermute | solution.py:548
  74.5 9.6 %collective-permute-start.9 = (f32[512,512]{1,0:T(8,128)S(1)}, f32[512,512]{1,0:T(8,128)S(1)}, u32[]{:S(2)}, u32[]{:S(2)}) collective-permute-start(f32[512,512]{1,0:T(8,128)S(1)} %get-tuple-element.43), channel_id=1, source_target_pairs={{0,1},{1,0},{2,3},{3,2},{4,5},{5,4},{6,7},{7,6},{8,9},{9,8},{10,11... | collective-permute-start | bytes 3145736 | tf_op jit(solution)/shard_map/ppermute | solution.py:548
  74.8 12.7 %collective-permute-start.11 = (bf16[512,512]{1,0:T(8,128)(2,1)S(1)}, bf16[512,512]{1,0:T(8,128)(2,1)S(1)}, u32[]{:S(2)}, u32[]{:S(2)}) collective-permute-start(bf16[512,512]{1,0:T(8,128)(2,1)S(1)} %get-tuple-element.48), channel_id=1, source_target_pairs={{0,4},{1,2},{2,1},{4,8},{7,3},{5,6},{6,5},{8,12},{11,7},{9,10},{10... | collective-permute-start | bytes 1572872 | tf_op jit(solution)/shard_map/ppermute | solution.py:548
  76.1 14.5 %collective-permute-start.7 = (bf16[512,512]{1,0:T(8,128)(2,1)S(1)}, bf16[512,512]{1,0:T(8,128)(2,1)S(1)}, u32[]{:S(2)}, u32[]{:S(2)}) collective-permute-start(bf16[512,512]{1,0:T(8,128)(2,1)S(1)} %get-tuple-element.41), channel_id=1, source_target_pairs={{0,4},{1,2},{2,1},{4,8},{7,3},{5,6},{6,5},{8,12},{11,7},{9,10},{10... | collective-permute-start | bytes 1572872 | tf_op jit(solution)/shard_map/ppermute | solution.py:548
  79.1 17.9 %collective-permute-start.14 = (f32[512,512]{1,0:T(8,128)S(1)}, f32[512,512]{1,0:T(8,128)S(1)}, u32[]{:S(2)}, u32[]{:S(2)}) collective-permute-start(f32[512,512]{1,0:T(8,128)S(1)} %get-tuple-element.50), channel_id=1, source_target_pairs={{0,1},{1,0},{2,3},{3,2},{4,5},{5,4},{6,7},{7,6},{8,9},{9,8},{10,11... | collective-permute-start | bytes 3145736 | tf_op jit(solution)/shard_map/ppermute | solution.py:548
  84.2 12.1 %collective-permute-start.5 = (bf16[512,512]{1,0:T(8,128)(2,1)S(1)}, bf16[512,512]{1,0:T(8,128)(2,1)S(1)}, u32[]{:S(2)}, u32[]{:S(2)}) collective-permute-start(bf16[512,512]{1,0:T(8,128)(2,1)S(1)} %get-tuple-element.40), channel_id=1, source_target_pairs={{0,4},{1,2},{2,1},{4,8},{7,3},{5,6},{6,5},{8,12},{11,7},{9,10},{10... | collective-permute-start | bytes 1572872 | tf_op jit(solution)/shard_map/ppermute | solution.py:548
  87.6 9.5 %collective-permute-start.13 = (bf16[512,512]{1,0:T(8,128)(2,1)S(1)}, bf16[512,512]{1,0:T(8,128)(2,1)S(1)}, u32[]{:S(2)}, u32[]{:S(2)}) collective-permute-start(bf16[512,512]{1,0:T(8,128)(2,1)S(1)} %shard_map.71.refs_3_), channel_id=1, source_target_pairs={{0,1},{1,0},{2,3},{3,2},{4,5},{5,4},{6,7},{7,6},{8,9},{9,8},{10,11... | collective-permute-start | bytes 1572872 | tf_op jit(solution)/shard_map/ppermute | solution.py:548
  90.7 6.4 %collective-permute-start.12 = (bf16[512,512]{1,0:T(8,128)(2,1)S(1)}, bf16[512,512]{1,0:T(8,128)(2,1)S(1)}, u32[]{:S(2)}, u32[]{:S(2)}) collective-permute-start(bf16[512,512]{1,0:T(8,128)(2,1)S(1)} %shard_map.70.refs_2_), channel_id=1, source_target_pairs={{0,1},{1,0},{2,3},{3,2},{4,5},{5,4},{6,7},{7,6},{8,9},{9,8},{10,11... | collective-permute-start | bytes 1572872 | tf_op jit(solution)/shard_map/ppermute | solution.py:548
  96.3 2.3 %collective-permute-start.6 = (bf16[512,512]{1,0:T(8,128)(2,1)S(1)}, bf16[512,512]{1,0:T(8,128)(2,1)S(1)}, u32[]{:S(2)}, u32[]{:S(2)}) collective-permute-start(bf16[512,512]{1,0:T(8,128)(2,1)S(1)} %collective-permute-done.5.refs_2_), channel_id=1, source_target_pairs={{0,1},{1,0},{2,3},{3,2},{4,5},{5,4},{6,7},{7,6},{8,9},{9,8},{10,11... | collective-permute-start | bytes 1572872 | tf_op jit(solution)/shard_map/ppermute | solution.py:548

commit v7 on v6

--- a/solution.py
+++ b/solution.py
@@ -437,12 +437,18 @@
     )(*scalars, own_t)
 
 
-def add_kernel(masked, pieces, before, outs):
-    for i, out_ref in enumerate(outs):
+def add_kernel(masked, ready, others, before, up_ref, low_ref, part_ref, tile, out_sem, *, names, block_total):
+    geo = Geometry(lax.axis_index("ao"), None, None, block_total)
+    for i, blocks in enumerate((ready, others)):
         total = before[i][...]
-        for k, rows in enumerate(pieces[i]):
+        for k, rows in enumerate(blocks):
             total += jnp.dot(masked[i][k], rows[...], preferred_element_type=jnp.float32)
-        out_ref[...] = total
+        if i == 0:
+            tile[...] = total
+            geo.place_tile(tile, getattr(geo, names[0]), up_ref, low_ref, out_sem.at[0])
+        else:
+            part_ref[...] = total
+    wait_tile(tile, out_sem.at[0])
 
 
 def last_kernel(masked, pieces, before, up_ref, low_ref, tiles, out_sem, *, names, first, block_total):
@@ -500,22 +506,34 @@
     )(*scalars, own_t, *pieces, *before, *outputs)
 
 
-def add_rows(masked, jobs):
-    cols, n = masked[0].shape[1], len(jobs)
-    _, pieces, before, span, rows_of = split_jobs(jobs)
-    n_in = len(pieces)
+def add_rows(masked, jobs, outputs, block_total):
+    cols = masked[0].shape[1]
+    names = [job[0] for job in jobs]
+    pieces = [list(job[1]) for job in jobs]
+    before = [job[2] for job in jobs]
+    arrays = [*pieces[0], *pieces[1]]
+    n, n_first = len(arrays), len(pieces[0])
 
     def body(*refs):
-        add_kernel(refs[:n], rows_of(refs[n:]), refs[n + n_in : 2 * n + n_in], refs[2 * n + n_in :])
+        blocks = [[rows_at(ref, k) for ref in refs[low:high] for k in range(ref.shape[0] // ROWBLK)]
+                  for low, high in ((2, 2 + n_first), (2 + n_first, 2 + n))]
+        add_kernel(
+            refs[:2], *blocks, refs[2 + n : 4 + n], *refs[6 + n :], names=names, block_total=block_total,
+        )
 
     return pl.pallas_call(
         body,
-        out_shape=tuple(jax.ShapeDtypeStruct(tile.shape, tile.dtype) for tile in before),
-        in_specs=[VMEM] * (2 * n + n_in),
-        out_specs=(VMEM,) * n,
-        compiler_params=pltpu.CompilerParams(vmem_limit_bytes=VMEM_LIMIT),
-        cost_estimate=end_cost(n, span, cols),
-    )(*masked, *pieces, *before)
+        out_shape=(
+            *(jax.ShapeDtypeStruct(o.shape, o.dtype) for o in outputs),
+            jax.ShapeDtypeStruct(before[1].shape, jnp.float32),
+        ),
+        in_specs=[VMEM] * (4 + n) + [ANY] * 2,
+        out_specs=(ANY, ANY, VMEM),
+        scratch_shapes=[pltpu.VMEM((cols, cols), jnp.float32), pltpu.SemaphoreType.DMA((1,))],
+        input_output_aliases={4 + n: 0, 5 + n: 1},
+        compiler_params=pltpu.CompilerParams(vmem_limit_bytes=VMEM_LIMIT),
+        cost_estimate=end_cost(2, 2, cols),
+    )(*masked, *arrays, *before, *outputs)
 
 
 def last_tiles(masked, jobs, first, outputs, block_total):
@@ -584,10 +602,10 @@
 
     relay_tail[:2] = [after(piece, made_across, made_relay) for piece in relay_tail[:2]]
     last_tail = [send(piece, cores) for piece in relay_tail]
-    jobs = [("relay", relay_tail[:-1], relay_part), ("last", last_tail[:-1], last_part)]
-    relay_part, last_part = add_rows(masked, jobs)
-    jobs = [("relay", relay_tail[-1:], relay_part), ("last", last_tail[-1:], last_part)]
-    upper, lower = last_tiles(masked, jobs, sum(turns[:-1]), (upper, lower), block_total)
+    jobs = [("relay", relay_tail, relay_part), ("last", last_tail[:-1], last_part)]
+    upper, lower, last_part = add_rows(masked, jobs, (upper, lower), block_total)
+    jobs = [("last", last_tail[-1:], last_part)]
+    upper, lower = last_tiles(masked[1:], jobs, sum(turns[:-1]), (upper, lower), block_total)
     return diagonal, upper, lower
 
 

time: 102 us -> 104 us (1.020)
  the two profiles are of different devices: /device:TPU:5 before, /device:TPU:17 now
where the time goes in v7:
time: 104 us; the launch traced here: 103 us
  Pallas kernels  39.6 us (38%)
  waiting for transfers between devices  37.2 us (36%)
  starting transfers between devices  23.5 us (23%)
  local copies, waits for them, and re-layouts  1.99 us (2%)
    ppermute x15, waiting for transfers between devices, send(): return lax.ppermute(block, 'ao', level_route(block_total, moves))  37.2 us
    ppermute x15, starting transfers between devices, send(): return lax.ppermute(block, 'ao', level_route(block_total, moves))  23.5 us
    pallas_call x3, Pallas kernels, pair_tiles(): pl.pallas_call(body, out_shape=tuple((jax.ShapeDtypeStruct(c.shape, c.dty...  14.5 us
    pallas_call x1, Pallas kernels, core_tile(): pl.pallas_call(functools.partial(core_kernel, block_total=block_total), o...  6.2 us
    pallas_call x1, Pallas kernels, own_tile(): pl.pallas_call(functools.partial(own_kernel, block_total=block_total), ou...  6.04 us
    pallas_call x2, Pallas kernels, rows_after(): pl.pallas_call(functools.partial(rows_kernel, low=low), out_shape=jax.Sha...  4.69 us
    pallas_call x1, Pallas kernels, end_tiles(): pl.pallas_call(body, out_shape=(*(jax.ShapeDtypeStruct(o.shape, o.dtype)...  3.39 us
  transfers between devices with their start and end apart: 15, of which 4 were waited for; matrix products, arithmetic and copies ran while one was open for 0% of the time, Pallas kernels for 37%

profile of v7, /device:TPU:17, one launch (start us, length us, event | category | flops | bytes accessed | tf_op | source)
XLA Modules:
  0.0 103.2 jit_solution(10802460096809493875)
XLA Ops:
  0.6 0.7 collective-permute-start
  1.4 2.3 %shard_map.60.refs_0_ = bf16[1536,512]{1,0:T(8,128)(2,1)} custom-call(bf16[3072,512]{1,0:T(8,128)(2,1)} %block_ref.3), custom_call_target="tpu_custom_call" | custom-call | tf_op jit(solution)/shard_map/pallas_call | solution.py:126
  3.7 0.0 copy-start.2
  3.7 0.0 copy-start.1
  3.7 1.3 %collective-permute-start.2 = (bf16[1536,512]{1,0:T(8,128)(2,1)}, bf16[1536,512]{1,0:T(8,128)(2,1)}, u32[]{:S(2)}, u32[]{:S(2)}) collective-permute-start(bf16[1536,512]{1,0:T(8,128)(2,1)} %shard_map.60.refs_0_), channel_id=1, source_target_pairs={{0,2},{1,3},{2,0},{3,1},{4,6},{5,7},{6,4},{7,5},{8,10},{9,11},{10,... | collective-permute-start | bytes 4718600 | tf_op jit(solution)/shard_map/ppermute | solution.py:566
  5.0 3.4 %collective-permute-start.3 = (bf16[1536,512]{1,0:T(8,128)(2,1)}, bf16[1536,512]{1,0:T(8,128)(2,1)}, u32[]{:S(2)}, u32[]{:S(2)}) collective-permute-start(bf16[1536,512]{1,0:T(8,128)(2,1)} %shard_map.60.refs_0_), channel_id=1, source_target_pairs={{1,4},{3,6},{5,8},{4,1},{7,10},{6,3},{9,12},{8,5},{11,14},{10,7},{... | collective-permute-start | bytes 4718600 | tf_op jit(solution)/shard_map/ppermute | solution.py:566
  8.4 0.0 collective-permute-done.refs_1_.core_ref
  8.4 2.4 %shard_map.61 = bf16[1536,512]{1,0:T(8,128)(2,1)} custom-call(bf16[3072,512]{1,0:T(8,128)(2,1)} %block_ref.3, bf16[1536,512]{1,0:T(8,128)(2,1)} %shard_map.60.refs_0_, bf16[3072,512]{1,0:T(8,128)(2,1)} %collective-permute-done.refs_1_.core_ref), custom_call_target="tpu_custom_call" | custom-call | tf_op jit(solution)/shard_map/pallas_call | solution.py:126
  10.8 2.2 %collective-permute-start.4 = (bf16[1536,512]{1,0:T(8,128)(2,1)}, bf16[1536,512]{1,0:T(8,128)(2,1)S(1)}, u32[]{:S(2)}, u32[]{:S(2)}) collective-permute-start(bf16[1536,512]{1,0:T(8,128)(2,1)} %shard_map.61), channel_id=1, source_target_pairs={{1,4},{3,6},{5,8},{4,1},{7,10},{6,3},{9,12},{8,5},{11,14},{10,7},{... | collective-permute-start | bytes 4718600 | tf_op jit(solution)/shard_map/ppermute | solution.py:566
  13.0 1.1 %collective-permute-start.1 = (bf16[1536,512]{1,0:T(8,128)(2,1)}, bf16[1536,512]{1,0:T(8,128)(2,1)S(1)}, u32[]{:S(2)}, u32[]{:S(2)}) collective-permute-start(bf16[1536,512]{1,0:T(8,128)(2,1)} %shard_map.61), channel_id=1, source_target_pairs={{0,2},{1,3},{2,0},{3,1},{4,6},{5,7},{6,4},{7,5},{8,10},{9,11},{10,... | collective-permute-start | bytes 4718600 | tf_op jit(solution)/shard_map/ppermute | solution.py:566
  14.1 0.0 copy-done.2
  14.1 0.1 copy.18.sig_ref
  14.2 0.0 copy-done.1
  14.2 0.0 copy-start
  14.2 1.9 %copy-done = bf16[3072,512]{1,0:T(8,128)(2,1)S(1)} copy-done((bf16[3072,512]{1,0:T(8,128)(2,1)S(1)}, bf16[3072,512]{1,0:T(8,128)(2,1)}, u32[]{:S(2)}) %copy-start) | copy-done | bytes 3145752
  16.1 6.0 %shard_map.58 = (f32[1,512,512]{2,1,0:T(8,128)}, bf16[6,512,512]{2,1,0:T(8,128)(2,1)S(1)}) custom-call(s32[1]{0:T(128)} %bitcast.position_ref, s32[16]{0:T(128)S(1)} %copy-done.1, s32[16,3]{1,0:T(8,128)S(1)} %copy.18.sig_ref, bf16[3072,512]{1,0:T(8,128)(2,1)S(1)} %copy-done), custom_call_target="tpu_custom_call" | custom-call | flops 1610612736 | bytes 7340032 | tf_op jit(solution)/shard_map/pallas_call | solution.py:208
  22.2 6.2 %shard_map.62 = (f32[1,3,512,512]{3,2,1,0:T(8,128)}, f32[1,3,512,512]{3,2,1,0:T(8,128)}, bf16[6,512,512]{2,1,0:T(8,128)(2,1)S(1)}, f32[8,128]{1,0:T(8,128)S(1)}) custom-call(s32[1]{0:T(128)} %bitcast.position_ref, s32[16]{0:T(128)S(1)} %copy-done.1, s32[16,3]{1,0:T(8,128)S(1)} %copy.18.sig_ref, bf16[3072,512]{1,0:T(8,128)(2,1)} %collective-permute-done.refs_1_.core_ref, ...), custom_call_target="tpu_custom_call" | custom-call | flops 1610612736 | bytes 10485760 | tf_op jit(solution)/shard_map/pallas_call | solution.py:278
  28.4 11.8 %collective-permute-done.2.refs_0_ = bf16[1536,512]{1,0:T(8,128)(2,1)} collective-permute-done((bf16[1536,512]{1,0:T(8,128)(2,1)}, bf16[1536,512]{1,0:T(8,128)(2,1)}, u32[]{:S(2)}, u32[]{:S(2)}) %collective-permute-start.2) | collective-permute-done | bytes 1572896 | tf_op jit(solution)/shard_map/ppermute | solution.py:566
  40.1 3.2 %collective-permute-start.10 = (bf16[1536,512]{1,0:T(8,128)(2,1)}, bf16[1536,512]{1,0:T(8,128)(2,1)S(1)}, u32[]{:S(2)}, u32[]{:S(2)}) collective-permute-start(bf16[1536,512]{1,0:T(8,128)(2,1)} %shard_map.63.refs_0_), channel_id=1, source_target_pairs={{0,4},{1,5},{4,8},{5,9},{6,2},{7,3},{8,12},{9,13},{10,6},{11,7},{1... | collective-permute-start | bytes 4718600 | tf_op jit(solution)/shard_map/ppermute | solution.py:566
  43.3 1.1 %shard_map.59 = (bf16[3,512,512]{2,1,0:T(8,128)(2,1)S(1)}, bf16[3,512,512]{2,1,0:T(8,128)(2,1)S(1)}) custom-call(s32[1]{0:T(128)} %bitcast.position_ref, s32[16]{0:T(128)S(1)} %copy-done.1, s32[16,3]{1,0:T(8,128)S(1)} %copy.18.sig_ref, bf16[6,512,512]{2,1,0:T(8,128)(2,1)S(1)} %get-tuple-element.32.own_t_ref), custom_call_target="tpu_custom_call" | custom-call | tf_op jit(solution)/shard_map/pallas_call | solution.py:431
  44.5 4.7 %shard_map.64 = (f32[512,512]{1,0:T(8,128)S(1)}, f32[512,512]{1,0:T(8,128)S(1)}, f32[8,128]{1,0:T(8,128)S(1)}) custom-call(s32[1]{0:T(128)} %bitcast.position_ref, s32[16]{0:T(128)S(1)} %copy-done.1, s32[16,3]{1,0:T(8,128)S(1)} %copy.18.sig_ref, bf16[6,512,512]{2,1,0:T(8,128)(2,1)S(1)} %get-tuple-element.32.own_t_ref, ...), custom_call_target="tpu_custom_call" | custom-call | flops 1610612736 | bytes 8912896 | tf_op jit(solution)/shard_map/pallas_call | solution.py:378
  49.2 0.0 collective-permute-done.3.refs_0_
  49.2 0.0 collective-permute-done.4.refs_1_.inner_ref
  49.2 5.6 %shard_map.65 = (f32[1,3,512,512]{3,2,1,0:T(8,128)}, f32[1,3,512,512]{3,2,1,0:T(8,128)}, f32[8,128]{1,0:T(8,128)S(1)}) custom-call(s32[1]{0:T(128)} %bitcast.position_ref, s32[16]{0:T(128)S(1)} %copy-done.1, s32[16,3]{1,0:T(8,128)S(1)} %copy.18.sig_ref, ...), custom_call_target="tpu_custom_call", output_to_operand_aliasing={{0}: (7, {}), {1}: (8, {})} | custom-call | flops 3221225472 | bytes 13631488 | tf_op jit(solution)/shard_map/pallas_call | solution.py:378
  54.8 18.9 %collective-permute-done.1.refs_0_ = bf16[1536,512]{1,0:T(8,128)(2,1)S(1)} collective-permute-done((bf16[1536,512]{1,0:T(8,128)(2,1)}, bf16[1536,512]{1,0:T(8,128)(2,1)S(1)}, u32[]{:S(2)}, u32[]{:S(2)}) %collective-permute-start.1) | collective-permute-done | bytes 1572896 | tf_op jit(solution)/shard_map/ppermute | solution.py:566
  73.7 0.8 collective-permute-start.8
  74.5 0.0 collective-permute-start.9
  74.5 0.3 shard_map.67
  74.8 3.5 %collective-permute-start.11 = (bf16[512,512]{1,0:T(8,128)(2,1)S(1)}, bf16[512,512]{1,0:T(8,128)(2,1)S(1)}, u32[]{:S(2)}, u32[]{:S(2)}) collective-permute-start(bf16[512,512]{1,0:T(8,128)(2,1)S(1)} %get-tuple-element.49), channel_id=1, source_target_pairs={{0,4},{1,2},{2,1},{4,8},{7,3},{5,6},{6,5},{8,12},{11,7},{9,10},{10... | collective-permute-start | bytes 1572872 | tf_op jit(solution)/shard_map/ppermute | solution.py:566
  78.4 0.0 collective-permute-done.10.refs_0_
  78.4 4.1 %shard_map.69 = (f32[512,512]{1,0:T(8,128)S(1)}, f32[512,512]{1,0:T(8,128)S(1)}, f32[8,128]{1,0:T(8,128)S(1)}) custom-call(s32[1]{0:T(128)} %bitcast.position_ref, s32[16]{0:T(128)S(1)} %copy-done.1, s32[16,3]{1,0:T(8,128)S(1)} %copy.18.sig_ref, bf16[6,512,512]{2,1,0:T(8,128)(2,1)S(1)} %get-tuple-element.32.own_t_ref, ...), custom_call_target="tpu_custom_call" | custom-call | flops 1610612736 | bytes 8912896 | tf_op jit(solution)/shard_map/pallas_call | solution.py:378
  82.5 0.1 collective-permute-start.14
  82.6 2.7 %collective-permute-start.7 = (bf16[512,512]{1,0:T(8,128)(2,1)S(1)}, bf16[512,512]{1,0:T(8,128)(2,1)S(1)}, u32[]{:S(2)}, u32[]{:S(2)}) collective-permute-start(bf16[512,512]{1,0:T(8,128)(2,1)S(1)} %get-tuple-element.42), channel_id=1, source_target_pairs={{0,4},{1,2},{2,1},{4,8},{7,3},{5,6},{6,5},{8,12},{11,7},{9,10},{10... | collective-permute-start | bytes 1572872 | tf_op jit(solution)/shard_map/ppermute | solution.py:566
  85.3 0.0 collective-permute-done.9.refs_3_
  85.3 2.8 %collective-permute-start.5 = (bf16[512,512]{1,0:T(8,128)(2,1)S(1)}, bf16[512,512]{1,0:T(8,128)(2,1)S(1)}, u32[]{:S(2)}, u32[]{:S(2)}) collective-permute-start(bf16[512,512]{1,0:T(8,128)(2,1)S(1)} %get-tuple-element.41), channel_id=1, source_target_pairs={{0,4},{1,2},{2,1},{4,8},{7,3},{5,6},{6,5},{8,12},{11,7},{9,10},{10... | collective-permute-start | bytes 1572872 | tf_op jit(solution)/shard_map/ppermute | solution.py:566
  88.2 0.0 collective-permute-done.8.refs_1_
  88.2 3.4 %shard_map.68 = (f32[1,3,512,512]{3,2,1,0:T(8,128)}, f32[1,3,512,512]{3,2,1,0:T(8,128)}, f32[8,128]{1,0:T(8,128)S(1)}) custom-call(s32[1]{0:T(128)} %bitcast.position_ref, s32[16]{0:T(128)S(1)} %copy-done.1, s32[16,3]{1,0:T(8,128)S(1)} %copy.18.sig_ref, ...), custom_call_target="tpu_custom_call", output_to_operand_aliasing={{0}: (8, {}), {1}: (9, {})} | custom-call | flops 1610612736 | bytes 8912896 | tf_op jit(solution)/shard_map/pallas_call | solution.py:497
  91.6 0.0 collective-permute-done.11.refs_0_
  91.6 0.1 collective-permute-start.13
  91.7 1.7 %collective-permute-done.7.refs_0_ = bf16[512,512]{1,0:T(8,128)(2,1)S(1)} collective-permute-done((bf16[512,512]{1,0:T(8,128)(2,1)S(1)}, bf16[512,512]{1,0:T(8,128)(2,1)S(1)}, u32[]{:S(2)}, u32[]{:S(2)}) %collective-permute-start.7) | collective-permute-done | bytes 524320 | tf_op jit(solution)/shard_map/ppermute | solution.py:566
  93.4 0.8 collective-permute-start.12
  94.1 4.9 %collective-permute-done.5.refs_4_ = bf16[512,512]{1,0:T(8,128)(2,1)S(1)} collective-permute-done((bf16[512,512]{1,0:T(8,128)(2,1)S(1)}, bf16[512,512]{1,0:T(8,128)(2,1)S(1)}, u32[]{:S(2)}, u32[]{:S(2)}) %collective-permute-start.5) | collective-permute-done | bytes 524320 | tf_op jit(solution)/shard_map/ppermute | solution.py:566
  99.0 0.8 collective-permute-start.6
  99.8 0.0 collective-permute-done.14.refs_8_
  99.8 0.0 collective-permute-done.13.refs_6_
  99.8 0.0 collective-permute-done.12.refs_5_
  99.8 2.0 %shard_map.72 = (f32[1,3,512,512]{3,2,1,0:T(8,128)}, f32[1,3,512,512]{3,2,1,0:T(8,128)}, f32[512,512]{1,0:T(8,128)S(1)}) custom-call(bf16[3,512,512]{2,1,0:T(8,128)(2,1)S(1)} %get-tuple-element.40.refs_3_.refs_0_, bf16[3,512,512]{2,1,0:T(8,128)(2,1)S(1)} %get-tuple-element.33.refs_1_.refs_0_, ...), custom_call_target="tpu_custom_call", output_to_operand_aliasing={{0}: (9, {}), {1}: (10, {})} | custom-call | flops 1073741824 | bytes 7340032 | tf_op jit(solution)/shard_map/pallas_call | solution.py:524
  101.7 0.0 collective-permute-done.6.refs_1_
  101.8 1.4 %shard_map.73 = (f32[1,3,512,512]{3,2,1,0:T(8,128)}, f32[1,3,512,512]{3,2,1,0:T(8,128)}) custom-call(bf16[3,512,512]{2,1,0:T(8,128)(2,1)S(1)} %get-tuple-element.33.refs_1_.refs_0_, bf16[512,512]{1,0:T(8,128)(2,1)S(1)} %collective-permute-done.6.refs_1_, f32[512,512]{1,0:T(8,128)S(1)} %get-tuple-element.54.refs_2_, ...), custom_call_target="tpu_custom_call", output_to_operand_aliasing={{0}: (3, {}), {1}: (4, {})} | custom-call | flops 268435456 | bytes 3145728 | tf_op jit(solution)/shard_map/pallas_call | solution.py:550
  (4 shorter events, 0.0 us)
Async XLA Ops:
  0.6 7.8 %collective-permute-start = (bf16[3072,512]{1,0:T(8,128)(2,1)}, bf16[3072,512]{1,0:T(8,128)(2,1)}, u32[]{:S(2)}, u32[]{:S(2)}) collective-permute-start(bf16[3072,512]{1,0:T(8,128)(2,1)} %block_ref.3), channel_id=1, source_target_pairs={{0,1},{1,0},{2,3},{3,2},{4,5},{5,4},{6,7},{7,6},{8,9},{9,8},{10,11... | collective-permute-start | bytes 9437192 | tf_op jit(solution)/shard_map/ppermute | solution.py:566
  3.7 10.4 %copy-start.2 = (s32[16,3]{0,1:T(4,128)S(1)}, s32[16,3]{0,1:T(4,128)}, u32[]{:S(2)}) copy-start(s32[16,3]{0,1:T(4,128)} %param.4) | copy-start | bytes 580
  3.7 10.5 %copy-start.1 = (s32[16]{0:T(128)S(1)}, s32[16]{0:T(128)}, u32[]{:S(2)}) copy-start(s32[16]{0:T(128)} %live_ref.13) | copy-start | bytes 196
  3.7 36.4 %collective-permute-start.2 = (bf16[1536,512]{1,0:T(8,128)(2,1)}, bf16[1536,512]{1,0:T(8,128)(2,1)}, u32[]{:S(2)}, u32[]{:S(2)}) collective-permute-start(bf16[1536,512]{1,0:T(8,128)(2,1)} %shard_map.60.refs_0_), channel_id=1, source_target_pairs={{0,2},{1,3},{2,0},{3,1},{4,6},{5,7},{6,4},{7,5},{8,10},{9,11},{10,... | collective-permute-start | bytes 4718600 | tf_op jit(solution)/shard_map/ppermute | solution.py:566
  5.0 44.2 %collective-permute-start.3 = (bf16[1536,512]{1,0:T(8,128)(2,1)}, bf16[1536,512]{1,0:T(8,128)(2,1)}, u32[]{:S(2)}, u32[]{:S(2)}) collective-permute-start(bf16[1536,512]{1,0:T(8,128)(2,1)} %shard_map.60.refs_0_), channel_id=1, source_target_pairs={{1,4},{3,6},{5,8},{4,1},{7,10},{6,3},{9,12},{8,5},{11,14},{10,7},{... | collective-permute-start | bytes 4718600 | tf_op jit(solution)/shard_map/ppermute | solution.py:566
  10.8 38.4 %collective-permute-start.4 = (bf16[1536,512]{1,0:T(8,128)(2,1)}, bf16[1536,512]{1,0:T(8,128)(2,1)S(1)}, u32[]{:S(2)}, u32[]{:S(2)}) collective-permute-start(bf16[1536,512]{1,0:T(8,128)(2,1)} %shard_map.61), channel_id=1, source_target_pairs={{1,4},{3,6},{5,8},{4,1},{7,10},{6,3},{9,12},{8,5},{11,14},{10,7},{... | collective-permute-start | bytes 4718600 | tf_op jit(solution)/shard_map/ppermute | solution.py:566
  13.0 60.7 %collective-permute-start.1 = (bf16[1536,512]{1,0:T(8,128)(2,1)}, bf16[1536,512]{1,0:T(8,128)(2,1)S(1)}, u32[]{:S(2)}, u32[]{:S(2)}) collective-permute-start(bf16[1536,512]{1,0:T(8,128)(2,1)} %shard_map.61), channel_id=1, source_target_pairs={{0,2},{1,3},{2,0},{3,1},{4,6},{5,7},{6,4},{7,5},{8,10},{9,11},{10,... | collective-permute-start | bytes 4718600 | tf_op jit(solution)/shard_map/ppermute | solution.py:566
  14.2 1.9 %copy-start = (bf16[3072,512]{1,0:T(8,128)(2,1)S(1)}, bf16[3072,512]{1,0:T(8,128)(2,1)}, u32[]{:S(2)}) copy-start(bf16[3072,512]{1,0:T(8,128)(2,1)} %block_ref.3) | copy-start | bytes 9437188
  40.1 38.2 %collective-permute-start.10 = (bf16[1536,512]{1,0:T(8,128)(2,1)}, bf16[1536,512]{1,0:T(8,128)(2,1)S(1)}, u32[]{:S(2)}, u32[]{:S(2)}) collective-permute-start(bf16[1536,512]{1,0:T(8,128)(2,1)} %shard_map.63.refs_0_), channel_id=1, source_target_pairs={{0,4},{1,5},{4,8},{5,9},{6,2},{7,3},{8,12},{9,13},{10,6},{11,7},{1... | collective-permute-start | bytes 4718600 | tf_op jit(solution)/shard_map/ppermute | solution.py:566
  73.7 14.4 %collective-permute-start.8 = (bf16[1536,512]{1,0:T(8,128)(2,1)S(1)}, bf16[1536,512]{1,0:T(8,128)(2,1)S(1)}, u32[]{:S(2)}, u32[]{:S(2)}) collective-permute-start(bf16[1536,512]{1,0:T(8,128)(2,1)S(1)} %shard_map.66.edge_ref.refs_0_), channel_id=1, source_target_pairs={{0,1},{1,0},{2,3},{3,2},{4,5},{5,4},{6,7},{7,6},{8,9},{9,8},{10,11... | collective-permute-start | bytes 4718600 | tf_op jit(solution)/shard_map/ppermute | solution.py:566
  74.5 10.8 %collective-permute-start.9 = (f32[512,512]{1,0:T(8,128)S(1)}, f32[512,512]{1,0:T(8,128)S(1)}, u32[]{:S(2)}, u32[]{:S(2)}) collective-permute-start(f32[512,512]{1,0:T(8,128)S(1)} %get-tuple-element.44), channel_id=1, source_target_pairs={{0,1},{1,0},{2,3},{3,2},{4,5},{5,4},{6,7},{7,6},{8,9},{9,8},{10,11... | collective-permute-start | bytes 3145736 | tf_op jit(solution)/shard_map/ppermute | solution.py:566
  74.8 16.8 %collective-permute-start.11 = (bf16[512,512]{1,0:T(8,128)(2,1)S(1)}, bf16[512,512]{1,0:T(8,128)(2,1)S(1)}, u32[]{:S(2)}, u32[]{:S(2)}) collective-permute-start(bf16[512,512]{1,0:T(8,128)(2,1)S(1)} %get-tuple-element.49), channel_id=1, source_target_pairs={{0,4},{1,2},{2,1},{4,8},{7,3},{5,6},{6,5},{8,12},{11,7},{9,10},{10... | collective-permute-start | bytes 1572872 | tf_op jit(solution)/shard_map/ppermute | solution.py:566
  82.5 17.3 %collective-permute-start.14 = (f32[512,512]{1,0:T(8,128)S(1)}, f32[512,512]{1,0:T(8,128)S(1)}, u32[]{:S(2)}, u32[]{:S(2)}) collective-permute-start(f32[512,512]{1,0:T(8,128)S(1)} %get-tuple-element.51), channel_id=1, source_target_pairs={{0,1},{1,0},{2,3},{3,2},{4,5},{5,4},{6,7},{7,6},{8,9},{9,8},{10,11... | collective-permute-start | bytes 3145736 | tf_op jit(solution)/shard_map/ppermute | solution.py:566
  82.6 10.8 %collective-permute-start.7 = (bf16[512,512]{1,0:T(8,128)(2,1)S(1)}, bf16[512,512]{1,0:T(8,128)(2,1)S(1)}, u32[]{:S(2)}, u32[]{:S(2)}) collective-permute-start(bf16[512,512]{1,0:T(8,128)(2,1)S(1)} %get-tuple-element.42), channel_id=1, source_target_pairs={{0,4},{1,2},{2,1},{4,8},{7,3},{5,6},{6,5},{8,12},{11,7},{9,10},{10... | collective-permute-start | bytes 1572872 | tf_op jit(solution)/shard_map/ppermute | solution.py:566
  85.3 13.6 %collective-permute-start.5 = (bf16[512,512]{1,0:T(8,128)(2,1)S(1)}, bf16[512,512]{1,0:T(8,128)(2,1)S(1)}, u32[]{:S(2)}, u32[]{:S(2)}) collective-permute-start(bf16[512,512]{1,0:T(8,128)(2,1)S(1)} %get-tuple-element.41), channel_id=1, source_target_pairs={{0,4},{1,2},{2,1},{4,8},{7,3},{5,6},{6,5},{8,12},{11,7},{9,10},{10... | collective-permute-start | bytes 1572872 | tf_op jit(solution)/shard_map/ppermute | solution.py:566
  91.6 8.2 %collective-permute-start.13 = (bf16[512,512]{1,0:T(8,128)(2,1)S(1)}, bf16[512,512]{1,0:T(8,128)(2,1)S(1)}, u32[]{:S(2)}, u32[]{:S(2)}) collective-permute-start(bf16[512,512]{1,0:T(8,128)(2,1)S(1)} %shard_map.71.refs_3_), channel_id=1, source_target_pairs={{0,1},{1,0},{2,3},{3,2},{4,5},{5,4},{6,7},{7,6},{8,9},{9,8},{10,11... | collective-permute-start | bytes 1572872 | tf_op jit(solution)/shard_map/ppermute | solution.py:566
  93.4 6.4 %collective-permute-start.12 = (bf16[512,512]{1,0:T(8,128)(2,1)S(1)}, bf16[512,512]{1,0:T(8,128)(2,1)S(1)}, u32[]{:S(2)}, u32[]{:S(2)}) collective-permute-start(bf16[512,512]{1,0:T(8,128)(2,1)S(1)} %shard_map.70.refs_2_), channel_id=1, source_target_pairs={{0,1},{1,0},{2,3},{3,2},{4,5},{5,4},{6,7},{7,6},{8,9},{9,8},{10,11... | collective-permute-start | bytes 1572872 | tf_op jit(solution)/shard_map/ppermute | solution.py:566
  99.0 2.8 %collective-permute-start.6 = (bf16[512,512]{1,0:T(8,128)(2,1)S(1)}, bf16[512,512]{1,0:T(8,128)(2,1)S(1)}, u32[]{:S(2)}, u32[]{:S(2)}) collective-permute-start(bf16[512,512]{1,0:T(8,128)(2,1)S(1)} %collective-permute-done.5.refs_4_), channel_id=1, source_target_pairs={{0,1},{1,0},{2,3},{3,2},{4,5},{5,4},{6,7},{7,6},{8,9},{9,8},{10,11... | collective-permute-start | bytes 1572872 | tf_op jit(solution)/shard_map/ppermute | solution.py:566
